TPU v7x, 32 devices: a whole 2x2x4 slice. The times are simulated.
32 devices in a mesh: frames: 16 (over z, x, core), pos: 2 (over y).
Axes of the slice: x: 2, y: 2, z: 4, core: 2. Of those that a mesh axis runs over, the one named last changes fastest.
Arguments:
- frames_in: bfloat16 [3584, 2, 1024], P('frames', 'pos'), may hold values from -6 to 6
- code_table: bfloat16 [2, 2048, 1024], P('pos', 'frames'), may hold values from -6 to 6
- code_ids: int32 [3584, 2], P('frames', 'pos'), may hold values from 0 to 2047
- delays: int32 [3, 2], P(None, 'pos'), may hold values from 1 to 2, as said below
- item_lengths: int32 [3], replicated, may hold values from 1 to 3360, as said below
- w_qkv: bfloat16 [2, 2, 1024, 3072], P(None, 'pos', 'frames'), may hold values from -0.1875 to 0.1875
- w_out: bfloat16 [2, 2, 1024, 1024], P(None, 'pos', 'frames'), may hold values from -0.25 to 0.25
- w_gate: bfloat16 [2, 2, 1024, 4096], P(None, 'pos', 'frames'), may hold values from -0.1875 to 0.1875
- w_up: bfloat16 [2, 2, 1024, 4096], P(None, 'pos', 'frames'), may hold values from -0.1875 to 0.1875
- w_down: bfloat16 [2, 2, 4096, 1024], P(None, 'pos', 'frames'), may hold values from -0.1875 to 0.1875
- gain_attn: bfloat16 [2, 2, 1024], P(None, 'pos', 'frames'), may hold values from 0.099609375 to 1.8984375
- gain_ffn: bfloat16 [2, 2, 1024], P(None, 'pos', 'frames'), may hold values from 0.099609375 to 1.8984375
- cotangent: bfloat16 [3584, 2, 1024], P('frames', 'pos'), may hold values from -6 to 6
Outputs:
- activations: bfloat16 [3584, 2, 1024], P('frames', 'pos')
- input_grad: float32 [3584, 2, 1024], P('frames', 'pos')
- table_grad: float32 [2, 2048, 1024], P('pos', 'frames')
- qkv_grad: float32 [2, 2, 1024, 3072], P(None, 'pos', 'frames')
- out_grad: float32 [2, 2, 1024, 1024], P(None, 'pos', 'frames')
- gate_grad: float32 [2, 2, 1024, 4096], P(None, 'pos', 'frames')
- up_grad: float32 [2, 2, 1024, 4096], P(None, 'pos', 'frames')
- down_grad: float32 [2, 2, 4096, 1024], P(None, 'pos', 'frames')
- attn_gain_grad: float32 [2, 2, 1024], P(None, 'pos', 'frames')
- ffn_gain_grad: float32 [2, 2, 1024], P(None, 'pos', 'frames')
Inputs may be any that keep to these rules, and one draw needn't show every extreme that they name: delays in frames; both values occur in every draw. `item_lengths`: 3 item lengths, each at least 1, summing to 3584; the longest has exactly 3360 frames.
All inputs are finite; a program needn't handle non-finite values.
Results may differ from a plain program's by a relative error of at most 0.017.
Values may be sent and summed in bfloat16 or wider, within the bound.
A program may use at most 320 MiB of HBM per device.

v0:
```python
import math

import jax
import jax.numpy as jnp
from jax import lax
from jax.sharding import PartitionSpec as P

HEADS = 16
HD = 64
LAYERS = 2


EPSILON = 1e-06
HIGHEST = lax.Precision.HIGHEST


def passed_along(x, axis, by):
    size = lax.axis_size(axis)
    pairs = [(i, i + by) for i in range(size) if 0 <= i + by < size]
    return lax.ppermute(x, axis, pairs)


def inverse_rms(stream):
    return lax.rsqrt(jnp.mean(stream * stream, axis=-1, keepdims=True) + EPSILON)


def plain(left, right):
    return jnp.dot(left, right, preferred_element_type=jnp.float32)


def left_trans(left, right):
    return lax.dot_general(
        left, right, (((0,), (0,)), ((), ())), preferred_element_type=jnp.float32
    )


def right_trans(left, right):
    return lax.dot_general(
        left, right, (((1,), (1,)), ((), ())), preferred_element_type=jnp.float32
    )


def norm_back(gradient, stream, inverse, gain_row):
    scaled = gradient * gain_row
    gain_grad = jnp.sum(gradient * stream * inverse, axis=0)
    inner_sum = jnp.mean(scaled * stream, axis=-1, keepdims=True)
    return (inverse * scaled - stream * inverse * inverse * inverse * inner_sum, gain_grad)


def split_heads(frame_qkv):
    rows_here, positions = (frame_qkv.shape[0], frame_qkv.shape[1])
    values = frame_qkv.astype(jnp.float32).reshape(rows_here, positions, 3, HEADS, HD)
    return (values[:, :, 0], values[:, :, 1], values[:, :, 2])


def layer_forward(stream, weights):
    qkv_all, out_all, gate_all, up_all, down_all, attn_gain, ffn_gain = weights
    inv_attn = inverse_rms(stream)
    normed_attn = (stream * inv_attn * attn_gain).astype(jnp.bfloat16)
    qkv_rows = plain(normed_attn, qkv_all).astype(jnp.bfloat16)
    frame_qkv = lax.all_to_all(qkv_rows[:, None, :], "pos", split_axis=0, concat_axis=1, tiled=True)
    rows_here, positions = (frame_qkv.shape[0], frame_qkv.shape[1])
    queries, key_rows, value_rows = split_heads(frame_qkv)
    scores = jnp.einsum("mihe,mjhe->mhij", queries, key_rows, precision=HIGHEST) / math.sqrt(HD)
    causal = jnp.arange(positions)[:, None] >= jnp.arange(positions)[None, :]
    scores = jnp.where(causal, scores, -1e30)
    largest = jnp.max(scores, axis=-1, keepdims=True)
    expon = jnp.exp(scores - largest)
    attention_probs = expon / jnp.sum(expon, axis=-1, keepdims=True)
    attended = jnp.einsum("mhij,mjhe->mihe", attention_probs, value_rows, precision=HIGHEST)
    attended = attended.reshape(rows_here, positions, HEADS * HD).astype(jnp.bfloat16)
    attended_rows = lax.all_to_all(attended, "pos", split_axis=1, concat_axis=0, tiled=True)[:, 0]
    middle = stream + plain(attended_rows, out_all)
    inv_ffn = inverse_rms(middle)
    normed_ffn = (middle * inv_ffn * ffn_gain).astype(jnp.bfloat16)
    gate_pre = plain(normed_ffn, gate_all)
    up_pre = plain(normed_ffn, up_all)
    gated_rows = (jax.nn.silu(gate_pre) * up_pre).astype(jnp.bfloat16)
    result = middle + plain(gated_rows, down_all)
    cache = (
        inv_attn,
        normed_attn,
        frame_qkv,
        attention_probs,
        attended_rows,
        middle,
        inv_ffn,
        normed_ffn,
        gate_pre,
        up_pre,
        gated_rows,
    )
    return (result, cache)


def layer_backward(gradient, stream, weights, cache):
    qkv_all, out_all, gate_all, up_all, down_all, attn_gain, ffn_gain = weights
    (
        inv_attn,
        normed_attn,
        frame_qkv,
        attention_probs,
        attended_rows,
        middle,
        inv_ffn,
        normed_ffn,
        gate_pre,
        up_pre,
        gated_rows,
    ) = cache
    grad_ffn = gradient.astype(jnp.bfloat16)
    down_part = left_trans(gated_rows, grad_ffn)
    grad_gated = right_trans(grad_ffn, down_all)
    sigmoid_gate = jax.nn.sigmoid(gate_pre)
    grad_gate = (
        grad_gated * up_pre * sigmoid_gate * (1.0 + gate_pre * (1.0 - sigmoid_gate))
    ).astype(jnp.bfloat16)
    grad_up = (grad_gated * gate_pre * sigmoid_gate).astype(jnp.bfloat16)
    gate_part = left_trans(normed_ffn, grad_gate)
    up_part = left_trans(normed_ffn, grad_up)
    grad_normed = right_trans(grad_gate, gate_all) + right_trans(grad_up, up_all)
    grad_middle, ffn_gain_part = norm_back(grad_normed, middle, inv_ffn, ffn_gain)
    grad_middle = gradient + grad_middle
    grad_attn = grad_middle.astype(jnp.bfloat16)
    out_part = left_trans(attended_rows, grad_attn)
    grad_attended = right_trans(grad_attn, out_all).astype(jnp.bfloat16)
    frame_grad = lax.all_to_all(
        grad_attended[:, None, :], "pos", split_axis=0, concat_axis=1, tiled=True
    )
    rows_here, positions = (frame_grad.shape[0], frame_grad.shape[1])
    queries, key_rows, value_rows = split_heads(frame_qkv)
    grad_heads = frame_grad.astype(jnp.float32).reshape(rows_here, positions, HEADS, HD)
    grad_probs = jnp.einsum("mihe,mjhe->mhij", grad_heads, value_rows, precision=HIGHEST)
    grad_values = jnp.einsum("mhij,mihe->mjhe", attention_probs, grad_heads, precision=HIGHEST)
    grad_scores = (
        attention_probs
        * (grad_probs - jnp.sum(attention_probs * grad_probs, axis=-1, keepdims=True))
        / math.sqrt(HD)
    )
    grad_queries = jnp.einsum("mhij,mjhe->mihe", grad_scores, key_rows, precision=HIGHEST)
    grad_keys = jnp.einsum("mhij,mihe->mjhe", grad_scores, queries, precision=HIGHEST)
    grad_frame_qkv = jnp.stack([grad_queries, grad_keys, grad_values], axis=2)
    grad_frame_qkv = grad_frame_qkv.reshape(rows_here, positions, 3 * HEADS * HD).astype(
        jnp.bfloat16
    )
    grad_qkv = lax.all_to_all(grad_frame_qkv, "pos", split_axis=1, concat_axis=0, tiled=True)[:, 0]
    qkv_part = left_trans(normed_attn, grad_qkv)
    grad_normed_attn = right_trans(grad_qkv, qkv_all)
    grad_stream, attn_gain_part = norm_back(grad_normed_attn, stream, inv_attn, attn_gain)
    pieces = (qkv_part, out_part, gate_part, up_part, down_part, attn_gain_part, ffn_gain_part)
    return (grad_middle + grad_stream, pieces)


def body(
    frames_in,
    code_table,
    code_ids,
    delays,
    item_lengths,
    w_qkv,
    w_out,
    w_gate,
    w_up,
    w_down,
    gain_attn,
    gain_ffn,
    cotangent,
):
    local_frames = frames_in.shape[0]
    item_count = item_lengths.shape[0]
    earlier = passed_along(code_ids[local_frames - 2 :], "frames", 1)
    extended = jnp.concatenate([earlier, code_ids], axis=0)[:, 0]
    global_frame = lax.axis_index("frames") * local_frames + jnp.arange(
        local_frames, dtype=jnp.int32
    )
    item_ends = jnp.cumsum(item_lengths)
    starts = item_ends - item_lengths
    item_index = jnp.sum((starts[None, :] <= global_frame[:, None]).astype(jnp.int32), axis=1) - 1
    chosen = item_index[:, None] == jnp.arange(item_count, dtype=jnp.int32)[None, :]
    item_begin = jnp.sum(jnp.where(chosen, starts[None, :], 0), axis=1)
    delay_rows = jnp.sum(jnp.where(chosen, delays[:, 0][None, :], 0), axis=1)
    source_local = jnp.arange(local_frames, dtype=jnp.int32) + 2 - delay_rows
    code_rows = jnp.take(extended, source_local, axis=0)
    is_valid = global_frame - delay_rows >= item_begin
    vocab_size = code_table.shape[1] * lax.axis_size("frames")
    matches = code_rows[:, None] == jnp.arange(vocab_size, dtype=jnp.int32)[None, :]
    onehot = (matches & is_valid[:, None]).astype(jnp.bfloat16)
    full_table = lax.all_gather(code_table, "frames", axis=1, tiled=True)[0]
    stream = frames_in[:, 0].astype(jnp.float32) + plain(onehot, full_table)
    inputs = []
    kept_weights = []
    for layer_index in range(LAYERS):
        fetched = (
            lax.all_gather(w_qkv[layer_index], "frames", axis=1, tiled=True),
            lax.all_gather(w_out[layer_index], "frames", axis=1, tiled=True),
            lax.all_gather(w_gate[layer_index], "frames", axis=1, tiled=True),
            lax.all_gather(w_up[layer_index], "frames", axis=1, tiled=True),
            lax.all_gather(w_down[layer_index], "frames", axis=1, tiled=True),
            lax.all_gather(gain_attn[layer_index], "frames", axis=1, tiled=True),
            lax.all_gather(gain_ffn[layer_index], "frames", axis=1, tiled=True),
        )
        weights = tuple((piece[0] for piece in fetched))
        inputs.append(stream)
        kept_weights.append(weights)
        stream, unused = layer_forward(stream, weights)
    output = stream.astype(jnp.bfloat16)[:, None, :]
    gradient = cotangent[:, 0].astype(jnp.float32)
    collected = [None] * LAYERS
    for layer_index in reversed(range(LAYERS)):
        fetched = (
            lax.all_gather(w_qkv[layer_index], "frames", axis=1, tiled=True),
            lax.all_gather(w_out[layer_index], "frames", axis=1, tiled=True),
            lax.all_gather(w_gate[layer_index], "frames", axis=1, tiled=True),
            lax.all_gather(w_up[layer_index], "frames", axis=1, tiled=True),
            lax.all_gather(w_down[layer_index], "frames", axis=1, tiled=True),
            lax.all_gather(gain_attn[layer_index], "frames", axis=1, tiled=True),
            lax.all_gather(gain_ffn[layer_index], "frames", axis=1, tiled=True),
        )
        weights = tuple((piece[0] for piece in fetched))
        unused, cache = layer_forward(inputs[layer_index], weights)
        gradient, pieces = layer_backward(gradient, inputs[layer_index], weights, cache)
        collected[layer_index] = (
            lax.psum_scatter(pieces[0][None], "frames", scatter_dimension=1, tiled=True),
            lax.psum_scatter(pieces[1][None], "frames", scatter_dimension=1, tiled=True),
            lax.psum_scatter(pieces[2][None], "frames", scatter_dimension=1, tiled=True),
            lax.psum_scatter(pieces[3][None], "frames", scatter_dimension=1, tiled=True),
            lax.psum_scatter(pieces[4][None], "frames", scatter_dimension=1, tiled=True),
            lax.psum_scatter(pieces[5][None], "frames", scatter_dimension=1, tiled=True),
            lax.psum_scatter(pieces[6][None], "frames", scatter_dimension=1, tiled=True),
        )
    grad_embed = gradient.astype(jnp.bfloat16)
    table_part = left_trans(onehot, grad_embed)
    table_share = lax.psum_scatter(table_part[None], "frames", scatter_dimension=1, tiled=True)
    stacked = [
        jnp.stack([collected[layer_index][slot] for layer_index in range(LAYERS)], axis=0)
        for slot in range(7)
    ]
    return (
        output,
        gradient[:, None, :],
        table_share,
        stacked[0],
        stacked[1],
        stacked[2],
        stacked[3],
        stacked[4],
        stacked[5],
        stacked[6],
    )


def solution(mesh):
    return jax.shard_map(
        body,
        mesh=mesh,
        in_specs=(
            P("frames", "pos", None),
            P("pos", "frames", None),
            P("frames", "pos"),
            P(None, "pos"),
            P(),
            P(None, "pos", "frames", None),
            P(None, "pos", "frames", None),
            P(None, "pos", "frames", None),
            P(None, "pos", "frames", None),
            P(None, "pos", "frames", None),
            P(None, "pos", "frames"),
            P(None, "pos", "frames"),
            P("frames", "pos", None),
        ),
        out_specs=(
            P("frames", "pos", None),
            P("frames", "pos", None),
            P("pos", "frames", None),
            P(None, "pos", "frames", None),
            P(None, "pos", "frames", None),
            P(None, "pos", "frames", None),
            P(None, "pos", "frames", None),
            P(None, "pos", "frames", None),
            P(None, "pos", "frames"),
            P(None, "pos", "frames"),
        ),
        check_vma=False,
    )
```

profile of v0, /device:TPU:0, one launch (start us, length us, event | category | flops | bytes accessed | tf_op | source)
XLA Modules:
  0.0 2792.1 jit_solution(15542160336543024948)
XLA Ops:
  22.1 35.1 %all-reduce.4 = (bf16[1024]{0:T(1024)(128)(2,1)S(1)}, bf16[1024]{0:T(1024)(128)(2,1)S(1)}, bf16[1024]{0:T(1024)(128)(2,1)S(1)}, bf16[1024]{0:T(1024)(128)(2,1)S(1)}) all-reduce(bf16[1024]{0:T(1024)(128)(2,1)S(1)} %dynamic-update-slice, bf16[1024]{0:T(1024)(128)(2,1)S(1)} %dynamic-update-slice.1, ...), channel_id=2, replica_groups=mesh['frames'=16,'pos'=2] {'frames'}, use_global_device_ids=true, to_apply=%add | all-reduce | flops 4096 | bytes 16384
  67.0 60.6 %all-gather.28.cloned.1.call-done = bf16[1,1,1024,3072]{3,2,1,0:T(8,128)(2,1)} async-done(((bf16[1,1,64,3072]{3,2,1,0:T(8,128)(2,1)}), bf16[1,1,1024,3072]{3,2,1,0:T(8,128)(2,1)}) %all-gather.28.cloned.1.call-update) | async-done | bytes 6291472 | tf_op jit(solution)/shard_map/all_gather | solution.py:194
  140.9 17.9 all-to-all-done
  202.0 44.1 %all-gather.32.cloned.1.call-done = bf16[1,1,1024,4096]{3,2,1,0:T(8,128)(2,1)} async-done(((bf16[1,1,64,4096]{3,2,1,0:T(8,128)(2,1)}), bf16[1,1,1024,4096]{3,2,1,0:T(8,128)(2,1)}) %all-gather.32.cloned.1.call-update) | async-done | bytes 8388624 | tf_op jit(solution)/shard_map/all_gather | solution.py:196
  253.4 68.5 %all-gather.34.cloned.1.call-done = bf16[1,1,1024,4096]{3,2,1,0:T(8,128)(2,1)} async-done(((bf16[1,1,64,4096]{3,2,1,0:T(8,128)(2,1)}), bf16[1,1,1024,4096]{3,2,1,0:T(8,128)(2,1)}) %all-gather.34.cloned.1.call-update) | async-done | bytes 8388624 | tf_op jit(solution)/shard_map/all_gather | solution.py:197
  331.2 66.4 %all-gather.36.cloned.1.call-done = bf16[1,1,4096,1024]{3,2,1,0:T(8,128)(2,1)} async-done(((bf16[1,1,256,1024]{3,2,1,0:T(8,128)(2,1)}), bf16[1,1,4096,1024]{3,2,1,0:T(8,128)(2,1)}) %all-gather.36.cloned.1.call-update) | async-done | bytes 8388624 | tf_op jit(solution)/shard_map/all_gather | solution.py:198
  403.8 56.3 %all-gather.38.cloned.1.call-done = bf16[1,1,1024,3072]{3,2,1,0:T(8,128)(2,1)} async-done(((bf16[1,1,64,3072]{3,2,1,0:T(8,128)(2,1)}), bf16[1,1,1024,3072]{3,2,1,0:T(8,128)(2,1)}) %all-gather.38.cloned.1.call-update) | async-done | bytes 6291472 | tf_op jit(solution)/shard_map/all_gather | solution.py:194
  475.5 17.9 all-to-all-done.2
  543.6 34.0 %all-gather.40.cloned.1.call-done = bf16[1,1,1024,1024]{3,2,1,0:T(8,128)(2,1)} async-done(((bf16[1,1,64,1024]{3,2,1,0:T(8,128)(2,1)}), bf16[1,1,1024,1024]{3,2,1,0:T(8,128)(2,1)}) %all-gather.40.cloned.1.call-update) | async-done | bytes 2097168 | tf_op jit(solution)/shard_map/all_gather | solution.py:195
  580.3 73.6 %all-gather.44.cloned.1.call-done = bf16[1,1,1024,4096]{3,2,1,0:T(8,128)(2,1)} async-done(((bf16[1,1,64,4096]{3,2,1,0:T(8,128)(2,1)}), bf16[1,1,1024,4096]{3,2,1,0:T(8,128)(2,1)}) %all-gather.44.cloned.1.call-update) | async-done | bytes 8388624 | tf_op jit(solution)/shard_map/all_gather | solution.py:197
  661.2 68.6 %all-gather.42.cloned.1.call-done = bf16[1,1,1024,4096]{3,2,1,0:T(8,128)(2,1)} async-done(((bf16[1,1,64,4096]{3,2,1,0:T(8,128)(2,1)}), bf16[1,1,1024,4096]{3,2,1,0:T(8,128)(2,1)}) %all-gather.42.cloned.1.call-update) | async-done | bytes 8388624 | tf_op jit(solution)/shard_map/all_gather | solution.py:196
  729.8 10.4 multiply_convert_fusion.3
  751.6 11.5 all_to_all.140
  810.7 20.8 all_to_all.141
  837.4 12.0 multiply_convert_fusion.1
  863.1 9.8 all_to_all.142
  928.6 11.4 all-to-all-done.7
  1004.5 9.8 convolution_bitcast_fusion.5
  1024.0 9.8 convolution_bitcast_fusion.3
  1050.3 51.0 %reduce-scatter.48.cloned.1.call-done = f32[64,1]{1,0:T(8,128)} async-done(((f32[1024,1]{1,0:T(8,128)}), f32[64,1]{1,0:T(8,128)}) %reduce-scatter.48.cloned.1.call-update) | async-done | bytes 272
  1104.0 56.5 %reduce-scatter.46.cloned.1.call-done = f32[64,1]{1,0:T(8,128)} async-done(((f32[1024,1]{1,0:T(8,128)}), f32[64,1]{1,0:T(8,128)}) %reduce-scatter.46.cloned.1.call-update) | async-done | bytes 272
  1162.0 74.0 %reduce-scatter.32.cloned.1.call-done = f32[1,64,1024]{2,1,0:T(8,128)} async-done(((f32[1,1024,1024]{2,1,0:T(8,128)}), f32[1,64,1024]{2,1,0:T(8,128)}) %reduce-scatter.32.cloned.1.call-update) | async-done | bytes 262160 | tf_op jit(solution)/shard_map/reduce_scatter | solution.py:224
  1235.9 75.7 %reduce-scatter.30.cloned.1.call-done = f32[1,64,1024]{2,1,0:T(8,128)} async-done(((f32[1,1024,1024]{2,1,0:T(8,128)}), f32[1,64,1024]{2,1,0:T(8,128)}) %reduce-scatter.30.cloned.1.call-update) | async-done | bytes 262160 | tf_op jit(solution)/shard_map/reduce_scatter | solution.py:224
  1313.5 135.9 %reduce-scatter.28.cloned.1.call-done = f32[1,64,3072]{2,1,0:T(8,128)} async-done(((f32[1,1024,3072]{2,1,0:T(8,128)}), f32[1,64,3072]{2,1,0:T(8,128)}) %reduce-scatter.28.cloned.1.call-update) | async-done | bytes 786448 | tf_op jit(solution)/shard_map/reduce_scatter | solution.py:223
  1449.4 138.0 %reduce-scatter.26.cloned.1.call-done = f32[1,64,3072]{2,1,0:T(8,128)} async-done(((f32[1,1024,3072]{2,1,0:T(8,128)}), f32[1,64,3072]{2,1,0:T(8,128)}) %reduce-scatter.26.cloned.1.call-update) | async-done | bytes 786448 | tf_op jit(solution)/shard_map/reduce_scatter | solution.py:223
  1590.0 179.0 %reduce-scatter.44.cloned.1.call-done = f32[1,256,1024]{2,1,0:T(8,128)} async-done(((f32[1,4096,1024]{2,1,0:T(8,128)}), f32[1,256,1024]{2,1,0:T(8,128)}) %reduce-scatter.44.cloned.1.call-update) | async-done | bytes 1048592 | tf_op jit(solution)/shard_map/reduce_scatter | solution.py:227
  1769.0 181.7 %reduce-scatter.42.cloned.1.call-done = f32[1,256,1024]{2,1,0:T(8,128)} async-done(((f32[1,4096,1024]{2,1,0:T(8,128)}), f32[1,256,1024]{2,1,0:T(8,128)}) %reduce-scatter.42.cloned.1.call-update) | async-done | bytes 1048592 | tf_op jit(solution)/shard_map/reduce_scatter | solution.py:227
  1953.8 178.6 %reduce-scatter.36.cloned.1.call-done = f32[1,64,4096]{2,1,0:T(8,128)} async-done(((f32[1,1024,4096]{2,1,0:T(8,128)}), f32[1,64,4096]{2,1,0:T(8,128)}) %reduce-scatter.36.cloned.1.call-update) | async-done | bytes 1048592 | tf_op jit(solution)/shard_map/reduce_scatter | solution.py:225
  2132.3 181.7 %reduce-scatter.34.cloned.1.call-done = f32[1,64,4096]{2,1,0:T(8,128)} async-done(((f32[1,1024,4096]{2,1,0:T(8,128)}), f32[1,64,4096]{2,1,0:T(8,128)}) %reduce-scatter.34.cloned.1.call-update) | async-done | bytes 1048592 | tf_op jit(solution)/shard_map/reduce_scatter | solution.py:225
  2317.1 178.5 %reduce-scatter.40.cloned.1.call-done = f32[1,64,4096]{2,1,0:T(8,128)} async-done(((f32[1,1024,4096]{2,1,0:T(8,128)}), f32[1,64,4096]{2,1,0:T(8,128)}) %reduce-scatter.40.cloned.1.call-update) | async-done | bytes 1048592 | tf_op jit(solution)/shard_map/reduce_scatter | solution.py:226
  2495.6 181.7 %reduce-scatter.38.cloned.1.call-done = f32[1,64,4096]{2,1,0:T(8,128)} async-done(((f32[1,1024,4096]{2,1,0:T(8,128)}), f32[1,64,4096]{2,1,0:T(8,128)}) %reduce-scatter.38.cloned.1.call-update) | async-done | bytes 1048592 | tf_op jit(solution)/shard_map/reduce_scatter | solution.py:226
  2680.3 105.1 %reduce-scatter.24.cloned.1.call-done = f32[1,128,1024]{2,1,0:T(8,128)} async-done(((f32[1,2048,1024]{2,1,0:T(8,128)}), f32[1,128,1024]{2,1,0:T(8,128)}) %reduce-scatter.24.cloned.1.call-update) | async-done | bytes 524304 | tf_op jit(solution)/shard_map/reduce_scatter | solution.py:233
  (343 shorter events, 420.2 us)
Async XLA Ops:
  7.2 56.3 %all-gather.26.cloned.1.call-start = ((), (), s32[]{:S(2)}) async-start(), calls=%async_computation.23 | async-start | bytes 4456448 | tf_op jit(solution)/shard_map/all_gather | solution.py:188
  7.9 119.7 %all-gather.28.cloned.1.call-start = ((), (), s32[]{:S(2)}) async-start(), calls=%async_computation.35 | async-start | bytes 6684672 | tf_op jit(solution)/shard_map/all_gather | solution.py:194
  10.0 182.2 %all-gather.30.cloned.1.call-start = ((), (), s32[]{:S(2)}) async-start(), calls=%async_computation.36 | async-start | bytes 2228224 | tf_op jit(solution)/shard_map/all_gather | solution.py:195
  10.9 235.3 %all-gather.32.cloned.1.call-start = ((), (), s32[]{:S(2)}) async-start(), calls=%async_computation.37 | async-start | bytes 8912896 | tf_op jit(solution)/shard_map/all_gather | solution.py:196
  12.0 309.9 %all-gather.34.cloned.1.call-start = ((), (), s32[]{:S(2)}) async-start(), calls=%async_computation.38 | async-start | bytes 8912896 | tf_op jit(solution)/shard_map/all_gather | solution.py:197
  13.1 384.6 %all-gather.36.cloned.1.call-start = ((), (), s32[]{:S(2)}) async-start(), calls=%async_computation.39 | async-start | bytes 8912896 | tf_op jit(solution)/shard_map/all_gather | solution.py:198
  14.6 445.5 %all-gather.38.cloned.1.call-start = ((), (), s32[]{:S(2)}) async-start(), calls=%async_computation.40 | async-start | bytes 6684672 | tf_op jit(solution)/shard_map/all_gather | solution.py:194
  15.4 520.4 %all-gather.46.cloned.1.call-start = ((), (), s32[]{:S(2)}) async-start(), calls=%async_computation.44 | async-start | bytes 8912896 | tf_op jit(solution)/shard_map/all_gather | solution.py:198
  16.1 561.5 %all-gather.40.cloned.1.call-start = ((), (), s32[]{:S(2)}) async-start(), calls=%async_computation.41 | async-start | bytes 2228224 | tf_op jit(solution)/shard_map/all_gather | solution.py:195
  16.9 637.1 %all-gather.44.cloned.1.call-start = ((), (), s32[]{:S(2)}) async-start(), calls=%async_computation.43 | async-start | bytes 8912896 | tf_op jit(solution)/shard_map/all_gather | solution.py:197
  17.4 712.4 %all-gather.42.cloned.1.call-start = ((), (), s32[]{:S(2)}) async-start(), calls=%async_computation.42 | async-start | bytes 8912896 | tf_op jit(solution)/shard_map/all_gather | solution.py:196
  17.6 40.1 %collective-permute-start = (s32[2,1]{0,1:T(1,128)S(1)}, s32[2,1]{0,1:T(1,128)S(1)}, u32[]{:S(2)}, u32[]{:S(2)}) collective-permute-start(s32[2,1]{0,1:T(1,128)S(1)} %slice.42), channel_id=1, source_target_pairs={{0,2},{2,4},{4,6},{6,8},{8,10},{10,12},{12,14},{14,16},{16,18},{18... | collective-permute-start | bytes 32 | tf_op jit(solution)/shard_map/ppermute | solution.py:20
  136.2 22.6 all-to-all-start
  188.7 10.6 all-to-all-start.1
  470.5 22.9 all-to-all-start.2
  523.2 54.5 %all-to-all-start.3 = ((bf16[112,2,1024]{2,0,1:T(8,128)(2,1)}), bf16[112,2,1024]{2,0,1:T(8,128)(2,1)S(1)}, u32[]{:S(2)}, u32[]{:S(2)}) async-start(bf16[112,2,1024]{2,0,1:T(8,128)(2,1)} %copy.128), calls=%async_computation.3 | async-start | bytes 917504 | tf_op jit(solution)/shard_map/all_to_all | solution.py:72
  920.5 19.5 all-to-all-start.7
  925.0 123.6 %reduce-scatter.52.cloned.1.call-start = ((), (), s32[]{:S(2)}) async-start(), calls=%async_computation.48 | async-start | bytes 557056
  926.1 123.3 %reduce-scatter.50.cloned.1.call-start = ((), (), s32[]{:S(2)}) async-start(), calls=%async_computation.47 | async-start | bytes 557056
  927.3 174.1 %reduce-scatter.48.cloned.1.call-start = ((), (), s32[]{:S(2)}) async-start(), calls=%async_computation.46 | async-start | bytes 557056
  928.4 232.2 %reduce-scatter.46.cloned.1.call-start = ((), (), s32[]{:S(2)}) async-start(), calls=%async_computation.45 | async-start | bytes 557056
  947.4 288.5 %reduce-scatter.32.cloned.1.call-start = ((), (), s32[]{:S(2)}) async-start(), calls=%async_computation.28 | async-start | bytes 4456448 | tf_op jit(solution)/shard_map/reduce_scatter | solution.py:224
  951.3 360.3 %reduce-scatter.30.cloned.1.call-start = ((), (), s32[]{:S(2)}) async-start(), calls=%async_computation.27 | async-start | bytes 4456448 | tf_op jit(solution)/shard_map/reduce_scatter | solution.py:224
  955.0 494.3 %reduce-scatter.28.cloned.1.call-start = ((), (), s32[]{:S(2)}) async-start(), calls=%async_computation.26 | async-start | bytes 13369344 | tf_op jit(solution)/shard_map/reduce_scatter | solution.py:223
  964.0 623.4 %reduce-scatter.26.cloned.1.call-start = ((), (), s32[]{:S(2)}) async-start(), calls=%async_computation.25 | async-start | bytes 13369344 | tf_op jit(solution)/shard_map/reduce_scatter | solution.py:223
  971.9 797.1 %reduce-scatter.44.cloned.1.call-start = ((), (), s32[]{:S(2)}) async-start(), calls=%async_computation.34 | async-start | bytes 17825792 | tf_op jit(solution)/shard_map/reduce_scatter | solution.py:227
  982.6 968.1 %reduce-scatter.42.cloned.1.call-start = ((), (), s32[]{:S(2)}) async-start(), calls=%async_computation.33 | async-start | bytes 17825792 | tf_op jit(solution)/shard_map/reduce_scatter | solution.py:227
  993.5 1138.8 %reduce-scatter.36.cloned.1.call-start = ((), (), s32[]{:S(2)}) async-start(), calls=%async_computation.30 | async-start | bytes 17825792 | tf_op jit(solution)/shard_map/reduce_scatter | solution.py:225
  1003.5 1310.5 %reduce-scatter.34.cloned.1.call-start = ((), (), s32[]{:S(2)}) async-start(), calls=%async_computation.29 | async-start | bytes 17825792 | tf_op jit(solution)/shard_map/reduce_scatter | solution.py:225
  1014.3 1481.3 %reduce-scatter.40.cloned.1.call-start = ((), (), s32[]{:S(2)}) async-start(), calls=%async_computation.32 | async-start | bytes 17825792 | tf_op jit(solution)/shard_map/reduce_scatter | solution.py:226
  1024.0 1653.2 %reduce-scatter.38.cloned.1.call-start = ((), (), s32[]{:S(2)}) async-start(), calls=%async_computation.31 | async-start | bytes 17825792 | tf_op jit(solution)/shard_map/reduce_scatter | solution.py:226
  1033.8 1751.6 %reduce-scatter.24.cloned.1.call-start = ((), (), s32[]{:S(2)}) async-start(), calls=%async_computation.24 | async-start | bytes 8912896 | tf_op jit(solution)/shard_map/reduce_scatter | solution.py:233
  (64 other events, 1116.5 us)
Sparse Core Ops, SparseCore 0:
  10.2 53.2 all-gather.25
  66.4 61.2 all-gather.27
  129.8 39.9 all-gather.29
  172.4 73.6 all-gather.31
  248.7 73.1 all-gather.33
  324.5 73.1 all-gather.35
  400.0 60.0 all-gather.37
  462.3 73.4 all-gather.45
  538.0 39.6 all-gather.39
  580.2 73.6 all-gather.43
  656.7 73.1 all-gather.41
  929.1 54.5 reduce-scatter.51
  987.7 54.8 reduce-scatter.49
  1046.5 54.7 reduce-scatter.47
  1105.7 54.8 reduce-scatter.45
  1164.3 71.6 reduce-scatter.31
  1240.1 71.4 reduce-scatter.29
  1315.5 133.8 reduce-scatter.27
  1453.4 133.8 reduce-scatter.25
  1591.3 177.6 reduce-scatter.43
  1773.1 177.5 reduce-scatter.41
  1954.8 177.5 reduce-scatter.35
  2136.5 177.5 reduce-scatter.33
  2318.0 177.5 reduce-scatter.39
  2499.7 177.5 reduce-scatter.37
  2681.7 103.6 reduce-scatter.23
where the time goes:
time: 2800 us; the launch traced here: 2790 us
  waiting for transfers between devices  2260 us (81%)
  matrix products  275 us (10%)
  local copies, waits for them, and re-layouts  90.8 us (3%)
  blocking collectives  77.2 us (3%)
  other arithmetic  47.7 us (2%)
    reduce_scatter x2, waiting for transfers between devices, body(): lax.psum_scatter(pieces[4][None], 'frames', scatter_dimension=1, tiled=True)  361 us
    reduce_scatter x2, waiting for transfers between devices, body(): lax.psum_scatter(pieces[2][None], 'frames', scatter_dimension=1, tiled=True)  360 us
    reduce_scatter x2, waiting for transfers between devices, body(): lax.psum_scatter(pieces[3][None], 'frames', scatter_dimension=1, tiled=True)  360 us
    reduce_scatter x2, waiting for transfers between devices, body(): lax.psum_scatter(pieces[0][None], 'frames', scatter_dimension=1, tiled=True)  274 us
    reduce_scatter x2, waiting for transfers between devices, body(): lax.psum_scatter(pieces[1][None], 'frames', scatter_dimension=1, tiled=True)  150 us
    all_gather x2, waiting for transfers between devices, body(): lax.all_gather(w_up[layer_index], 'frames', axis=1, tiled=True)  142 us
    all_gather x2, waiting for transfers between devices, body(): lax.all_gather(w_qkv[layer_index], 'frames', axis=1, tiled=True)  117 us
    all_gather x2, waiting for transfers between devices, body(): lax.all_gather(w_gate[layer_index], 'frames', axis=1, tiled=True)  113 us
  transfers between devices with their start and end apart: 32, of which 27 were waited for; matrix products, arithmetic and copies ran while one was open for 9% of the time, Pallas kernels for 0%

commit v1 on v0

v1 whole, which is shorter than its diff:
```python
import math

import jax
import jax.numpy as jnp
from jax import lax
from jax.sharding import PartitionSpec as P

HEADS = 16
HD = 64
LAYERS = 2
EPSILON = 1e-06
HIGHEST = lax.Precision.HIGHEST
BF = jnp.bfloat16
F32 = jnp.float32


def plain(left, right):
    return jnp.dot(left, right, preferred_element_type=F32)


def left_trans(left, right):
    return lax.dot_general(left, right, (((0,), (0,)), ((), ())), preferred_element_type=F32)


def right_trans(left, right):
    return lax.dot_general(left, right, (((1,), (1,)), ((), ())), preferred_element_type=F32)


def inverse_rms(stream):
    return lax.rsqrt(jnp.mean(stream * stream, axis=-1, keepdims=True) + EPSILON)


def norm_back(gradient, stream, inverse, gain_row):
    scaled = gradient * gain_row
    gain_grad = jnp.sum(gradient * stream * inverse, axis=0)
    inner_sum = jnp.mean(scaled * stream, axis=-1, keepdims=True)
    return (inverse * scaled - stream * inverse * inverse * inverse * inner_sum, gain_grad)


def head_matrix():
    rows = lax.broadcasted_iota(jnp.int32, (HEADS * HD, HEADS), 0) // HD
    cols = lax.broadcasted_iota(jnp.int32, (HEADS * HD, HEADS), 1)
    return (rows == cols).astype(F32)


def head_sum(values):
    return jnp.dot(values, head_matrix(), precision=HIGHEST)


def head_spread(values):
    return jnp.dot(values, head_matrix().T, precision=HIGHEST)


class Plan:
    def __init__(self, count):
        self.count = count
        self.team = 8 if count % 8 == 0 else count
        self.teams = count // self.team
        self.inside = [[g * self.team + t for t in range(self.team)] for g in range(self.teams)]
        self.across = [[g * self.team + t for g in range(self.teams)] for t in range(self.team)]

    def gather_inside(self, rows):
        return lax.all_gather(rows, "frames", axis=0, tiled=True, axis_index_groups=self.inside)

    def scatter_inside(self, rows):
        return lax.psum_scatter(
            rows, "frames", scatter_dimension=0, tiled=True, axis_index_groups=self.inside
        )

    def gather_across(self, rows):
        return lax.all_gather(rows, "frames", axis=0, tiled=True, axis_index_groups=self.across)

    def scatter_across(self, rows):
        return lax.psum_scatter(
            rows, "frames", scatter_dimension=0, tiled=True, axis_index_groups=self.across
        )

    def swap_inside(self, parts):
        return lax.all_to_all(
            parts, "frames", split_axis=0, concat_axis=0, tiled=True, axis_index_groups=self.inside
        )

    def ffn_weights(self, gate, up, down):
        rows = gate.shape[0]
        both = jnp.stack([gate, up], axis=1).reshape(rows, 2, self.teams, self.team, -1)
        parts = both.transpose(3, 0, 1, 2, 4).reshape(self.team * rows, -1)
        mine = self.swap_inside(parts)
        return self.gather_across(mine), self.gather_across(down)

    def ffn_grads(self, both_part, down_part):
        down = self.scatter_across(down_part.astype(BF)).astype(F32)
        both = self.scatter_across(both_part.astype(BF))
        parts = self.swap_inside(both)
        rows = parts.shape[0] // self.team
        parts = parts.astype(F32).reshape(self.team, rows, 2, self.teams, -1)
        both = parts.transpose(1, 2, 3, 0, 4).reshape(rows, 2, -1)
        return both[:, 0], both[:, 1], down


def attend(qkv, other):
    width = HEADS * HD
    position = lax.axis_index("pos")
    q, k, v = (qkv[:, i * width : (i + 1) * width].astype(F32) for i in range(3))
    k0, v0 = (other[:, i * width : (i + 1) * width].astype(F32) for i in range(2))
    own = head_sum(q * k) / math.sqrt(HD)
    past = jnp.where(position > 0, head_sum(q * k0) / math.sqrt(HD), -1e30)
    largest = jnp.maximum(own, past)
    own, past = jnp.exp(own - largest), jnp.exp(past - largest)
    total = own + past
    own, past = own / total, past / total
    attended = head_spread(own) * v + head_spread(past) * v0
    return attended.astype(BF), own, past


def attend_back(grad, qkv, other, own, past):
    width = HEADS * HD
    q, k, v = (qkv[:, i * width : (i + 1) * width].astype(F32) for i in range(3))
    k0, v0 = (other[:, i * width : (i + 1) * width].astype(F32) for i in range(2))
    grad = grad.astype(F32)
    d_own, d_past = head_sum(grad * v), head_sum(grad * v0)
    inner = own * d_own + past * d_past
    s_own = head_spread(own * (d_own - inner) / math.sqrt(HD))
    s_past = head_spread(past * (d_past - inner) / math.sqrt(HD))
    own, past = head_spread(own), head_spread(past)
    d_q = s_own * k + s_past * k0
    d_k = s_own * q
    d_v = own * grad
    d_other = jnp.concatenate([s_past * q, past * grad], axis=1)
    return d_q, d_k, d_v, d_other


def body(
    frames_in,
    code_table,
    code_ids,
    delays,
    item_lengths,
    w_qkv,
    w_out,
    w_gate,
    w_up,
    w_down,
    gain_attn,
    gain_ffn,
    cotangent,
):
    count = lax.axis_size("frames")
    plan = Plan(count)
    positions = lax.axis_size("pos")
    onward = [(i, i + 1) for i in range(positions - 1)]
    backward = [(i + 1, i) for i in range(positions - 1)]
    local_frames = frames_in.shape[0]
    item_count = item_lengths.shape[0]
    width = frames_in.shape[-1]

    neighbours = [(i, i + 1) for i in range(count - 1)]
    earlier = lax.ppermute(code_ids[local_frames - 2 :], "frames", neighbours)
    extended = jnp.concatenate([earlier, code_ids], axis=0)[:, 0]
    global_frame = lax.axis_index("frames") * local_frames + jnp.arange(
        local_frames, dtype=jnp.int32
    )
    item_ends = jnp.cumsum(item_lengths)
    starts = item_ends - item_lengths
    item_index = jnp.sum((starts[None, :] <= global_frame[:, None]).astype(jnp.int32), axis=1) - 1
    chosen = item_index[:, None] == jnp.arange(item_count, dtype=jnp.int32)[None, :]
    item_begin = jnp.sum(jnp.where(chosen, starts[None, :], 0), axis=1)
    delay_rows = jnp.sum(jnp.where(chosen, delays[:, 0][None, :], 0), axis=1)
    one_back = extended[1 : local_frames + 1]
    two_back = extended[:local_frames]
    code_rows = jnp.where(delay_rows == 1, one_back, two_back)
    is_valid = global_frame - delay_rows >= item_begin
    vocab_size = code_table.shape[1] * count
    matches = code_rows[:, None] == jnp.arange(vocab_size, dtype=jnp.int32)[None, :]
    onehot = (matches & is_valid[:, None]).astype(BF)

    gains = jnp.stack([gain_attn[0, 0], gain_attn[1, 0], gain_ffn[0, 0], gain_ffn[1, 0]], axis=1)
    gains = jnp.pad(gains, ((0, 0), (0, 124)))
    full_table = lax.all_gather(code_table[0], "frames", axis=0, tiled=True)
    first_qkv = lax.all_gather(
        jnp.concatenate([w_qkv[0, 0], gains], axis=1), "frames", axis=0, tiled=True
    )
    gain_rows = first_qkv[:, 3 * width : 3 * width + 4].astype(F32).T
    qkv_all = [first_qkv[:, : 3 * width], None]
    out_all = [lax.all_gather(w_out[0, 0], "frames", axis=0, tiled=True), None]
    ffn_all = [plan.ffn_weights(w_gate[0, 0], w_up[0, 0], w_down[0, 0]), None]
    qkv_all[1] = lax.all_gather(w_qkv[1, 0], "frames", axis=0, tiled=True)
    out_all[1] = lax.all_gather(w_out[1, 0], "frames", axis=0, tiled=True)
    ffn_all[1] = plan.ffn_weights(w_gate[1, 0], w_up[1, 0], w_down[1, 0])

    stream = frames_in[:, 0].astype(F32) + plain(onehot, full_table)
    kept = []
    for layer in range(LAYERS):
        inv_attn = inverse_rms(stream)
        normed_attn = (stream * inv_attn * gain_rows[layer]).astype(BF)
        qkv = plain(normed_attn, qkv_all[layer]).astype(BF)
        other = lax.ppermute(qkv[:, width:], "pos", onward)
        attended, own, past = attend(qkv, other)
        middle = stream + plain(attended, out_all[layer])
        inv_ffn = inverse_rms(middle)
        normed_ffn = (middle * inv_ffn * gain_rows[2 + layer]).astype(BF)
        team_normed = plan.gather_inside(normed_ffn)
        both_all, down_all = ffn_all[layer]
        pre = plain(team_normed, both_all)
        half = pre.shape[1] // 2
        gate_pre, up_pre = pre[:, :half], pre[:, half:]
        gated = (jax.nn.silu(gate_pre) * up_pre).astype(BF)
        result = plain(gated, down_all).astype(BF)
        new_stream = middle + plan.scatter_inside(result).astype(F32)
        kept.append(
            (
                stream,
                inv_attn,
                normed_attn,
                qkv,
                other,
                own,
                past,
                attended,
                middle,
                inv_ffn,
                team_normed,
                gate_pre,
                up_pre,
                gated,
            )
        )
        stream = new_stream
    output = stream.astype(BF)[:, None, :]

    gradient = cotangent[:, 0].astype(F32)
    collected = [None] * LAYERS
    gain_parts = [None] * (2 * LAYERS)
    for layer in reversed(range(LAYERS)):
        (
            stream,
            inv_attn,
            normed_attn,
            qkv,
            other,
            own,
            past,
            attended,
            middle,
            inv_ffn,
            team_normed,
            gate_pre,
            up_pre,
            gated,
        ) = kept[layer]
        both_all, down_all = ffn_all[layer]
        grad_out = plan.gather_inside(gradient.astype(BF))
        grad_gated = right_trans(grad_out, down_all)
        sig = jax.nn.sigmoid(gate_pre)
        grad_gate = (grad_gated * up_pre * sig * (1.0 + gate_pre * (1.0 - sig))).astype(BF)
        grad_up = (grad_gated * gate_pre * sig).astype(BF)
        grad_both = jnp.concatenate([grad_gate, grad_up], axis=1)
        grad_normed = plan.scatter_inside(right_trans(grad_both, both_all).astype(BF)).astype(F32)
        down_part = left_trans(gated, grad_out)
        both_part = left_trans(team_normed, grad_both)
        ffn_shares = plan.ffn_grads(both_part, down_part)
        grad_middle, gain_parts[2 + layer] = norm_back(
            grad_normed, middle, inv_ffn, gain_rows[2 + layer]
        )
        grad_middle = gradient + grad_middle
        grad_attn = grad_middle.astype(BF)
        grad_attended = right_trans(grad_attn, out_all[layer]).astype(BF)
        d_q, d_k, d_v, d_other = attend_back(grad_attended, qkv, other, own, past)
        arrived = lax.ppermute(d_other.astype(BF), "pos", backward).astype(F32)
        grad_qkv = jnp.concatenate([d_q, d_k + arrived[:, :width], d_v + arrived[:, width:]], axis=1)
        grad_qkv = grad_qkv.astype(BF)
        out_part = left_trans(attended, grad_attn).astype(BF)
        out_share = lax.psum_scatter(out_part, "frames", scatter_dimension=0, tiled=True)
        grad_normed_attn = right_trans(grad_qkv, qkv_all[layer])
        grad_stream, gain_parts[layer] = norm_back(
            grad_normed_attn, stream, inv_attn, gain_rows[layer]
        )
        gradient = grad_middle + grad_stream
        qkv_part = left_trans(normed_attn, grad_qkv).astype(BF)
        if layer == 0:
            tail = jnp.stack(gain_parts, axis=1).astype(BF)
            qkv_part = jnp.concatenate([qkv_part, jnp.pad(tail, ((0, 0), (0, 124)))], axis=1)
        qkv_share = lax.psum_scatter(qkv_part, "frames", scatter_dimension=0, tiled=True)
        collected[layer] = (qkv_share.astype(F32), out_share.astype(F32)) + ffn_shares
    table_part = left_trans(onehot, gradient.astype(BF)).astype(BF)
    table_share = lax.psum_scatter(table_part, "frames", scatter_dimension=0, tiled=True)
    gain_shares = collected[0][0][:, 3 * width : 3 * width + 4].T
    collected[0] = (collected[0][0][:, : 3 * width],) + collected[0][1:]
    stacked = [
        jnp.stack([collected[layer][slot] for layer in range(LAYERS)], axis=0)[:, None]
        for slot in range(5)
    ]
    return (
        output,
        gradient[:, None, :],
        table_share.astype(F32)[None],
        stacked[0],
        stacked[1],
        stacked[2],
        stacked[3],
        stacked[4],
        gain_shares[:2][:, None],
        gain_shares[2:][:, None],
    )


def solution(mesh):
    return jax.shard_map(
        body,
        mesh=mesh,
        in_specs=(
            P("frames", "pos", None),
            P("pos", "frames", None),
            P("frames", "pos"),
            P(None, "pos"),
            P(),
            P(None, "pos", "frames", None),
            P(None, "pos", "frames", None),
            P(None, "pos", "frames", None),
            P(None, "pos", "frames", None),
            P(None, "pos", "frames", None),
            P(None, "pos", "frames"),
            P(None, "pos", "frames"),
            P("frames", "pos", None),
        ),
        out_specs=(
            P("frames", "pos", None),
            P("frames", "pos", None),
            P("pos", "frames", None),
            P(None, "pos", "frames", None),
            P(None, "pos", "frames", None),
            P(None, "pos", "frames", None),
            P(None, "pos", "frames", None),
            P(None, "pos", "frames", None),
            P(None, "pos", "frames"),
            P(None, "pos", "frames"),
        ),
        check_vma=False,
    )
```

time: 2800 us -> 1430 us (0.51)
  waiting for transfers between devices: 2260 us -> 1100 us
  matrix products: 275 us -> 164 us
  blocking collectives: 77.2 us -> 26.6 us
  local copies, waits for them, and re-layouts: 90.8 us -> 48.7 us
    reduce_scatter x11 -> x13, waiting for transfers between devices: 1610 us -> 578 us  [the longest x2 174 us: body(): lax.psum_scatter(qkv_part, 'frames', scatter_dimension=0, tiled=True)]
    unnamed x30 -> x26, waiting for transfers between devices: 111 us -> 3.62 us
    ppermute x1 -> x5, waiting for transfers between devices: 0.01 us -> 74.9 us  [the longest x2 43.9 us: body(): arrived = lax.ppermute(d_other.astype(BF), 'pos', backward).astype(F32)]
    dot_general x23 -> x25, matrix products: 141 us -> 81.2 us  [the longest x9 44.8 us: plain(): return jnp.dot(left, right, preferred_element_type=F32)]
    all_to_all x5 -> x3, waiting for transfers between devices: 54.2 us -> 0.01 us  [swap_inside(): lax.all_to_all(parts, 'frames', split_axis=0, concat_axis=0, tiled=True,...]
    all_gather x11 -> x13, waiting for transfers between devices: 485 us -> 438 us  [the longest x4 154 us: gather_across(): lax.all_gather(rows, 'frames', axis=0, tiled=True, axis_index_groups=self...]
    dot_general x11 -> x9, matrix products: 85.1 us -> 43.5 us  [left_trans(): lax.dot_general(left, right, (((0,), (0,)), ((), ())), preferred_element_...]
    unnamed x1 -> x0, blocking collectives: 35.1 us -> none
  transfers between devices with their start and end apart: 32 -> 34, of which waited for: 27 -> 30; matrix products, arithmetic and copies ran while one was open for 9% -> 13% of each run, Pallas kernels for 0% -> 0%
where the time goes in v1:
time: 1430 us; the launch traced here: 1420 us
  waiting for transfers between devices  1100 us (77%)
  matrix products  164 us (11%)
  local copies, waits for them, and re-layouts  48.7 us (3%)
  other arithmetic  36.9 us (3%)
  starting transfers between devices  30.8 us (2%)
  blocking collectives  26.6 us (2%)
  between operations  15.6 us (1%)
    reduce_scatter x2, waiting for transfers between devices, body(): lax.psum_scatter(qkv_part, 'frames', scatter_dimension=0, tiled=True)  174 us
    all_gather x4, waiting for transfers between devices, gather_across(): lax.all_gather(rows, 'frames', axis=0, tiled=True, axis_index_groups=self...  154 us
    reduce_scatter x4, waiting for transfers between devices, scatter_inside(): lax.psum_scatter(rows, 'frames', scatter_dimension=0, tiled=True, axis_in...  130 us
    reduce_scatter x2, waiting for transfers between devices, body(): lax.psum_scatter(out_part, 'frames', scatter_dimension=0, tiled=True)  114 us
    all_gather x4, waiting for transfers between devices, gather_inside(): lax.all_gather(rows, 'frames', axis=0, tiled=True, axis_index_groups=self...  111 us
    reduce_scatter x4, waiting for transfers between devices, scatter_across(): lax.psum_scatter(rows, 'frames', scatter_dimension=0, tiled=True, axis_in...  87.1 us
    reduce_scatter x1, waiting for transfers between devices, body(): lax.psum_scatter(table_part, 'frames', scatter_dimension=0, tiled=True)  74.1 us
    all_gather x1, waiting for transfers between devices, body(): qkv_all[1] = lax.all_gather(w_qkv[1, 0], 'frames', axis=0, tiled=True)  65.6 us
  transfers between devices with their start and end apart: 34, of which 30 were waited for; matrix products, arithmetic and copies ran while one was open for 13% of the time, Pallas kernels for 0%

profile of v1, /device:TPU:0, one launch (start us, length us, event | category | flops | bytes accessed | tf_op | source)
XLA Modules:
  0.0 1418.0 jit_solution(1253433506805756646)
XLA Ops:
  27.3 38.3 %all-gather.33.cloned.1.call-done = bf16[1,2048,1024]{2,1,0:T(8,128)(2,1)} async-done(((bf16[1,128,1024]{2,1,0:T(8,128)(2,1)}), bf16[1,2048,1024]{2,1,0:T(8,128)(2,1)}) %all-gather.33.cloned.1.call-update) | async-done | bytes 4194320 | tf_op jit(solution)/shard_map/all_gather | solution.py:178
  69.1 61.3 %all-gather.21.cloned.1.call-done = bf16[1024,3200]{1,0:T(8,128)(2,1)} async-done(((bf16[64,3200]{1,0:T(8,128)(2,1)}), bf16[1024,3200]{1,0:T(8,128)(2,1)}) %all-gather.21.cloned.1.call-update) | async-done | bytes 6553616 | tf_op jit(solution)/shard_map/all_gather | solution.py:179
  146.0 15.4 %collective-permute-done.1 = bf16[224,2048]{1,0:T(8,128)(2,1)} collective-permute-done((bf16[224,2048]{1,0:T(8,128)(2,1)S(1)}, bf16[224,2048]{1,0:T(8,128)(2,1)}, u32[]{:S(2)}, u32[]{:S(2)}) %collective-permute-start.1) | collective-permute-done | bytes 917536 | tf_op jit(solution)/shard_map/ppermute | solution.py:196
  177.9 52.4 %all-gather.25.cloned.1.call-done = bf16[1024,1024]{1,0:T(8,128)(2,1)} async-done(((bf16[512,1024]{1,0:T(8,128)(2,1)}), bf16[1024,1024]{1,0:T(8,128)(2,1)}) %all-gather.25.cloned.1.call-update) | async-done | bytes 2097168 | tf_op jit(solution)/shard_map/all_gather | solution.py:71
  230.3 28.0 %all-gather.23.cloned.1.call-done = bf16[1792,1024]{1,0:T(8,128)(2,1)} async-done(((bf16[224,1024]{1,0:T(8,128)(2,1)}), bf16[1792,1024]{1,0:T(8,128)(2,1)}) %all-gather.23.cloned.1.call-update) | async-done | bytes 3670032 | tf_op jit(solution)/shard_map/all_gather | solution.py:63
  269.4 24.4 %all-gather.37.cloned.1.call-done = bf16[1,1,512,1024]{3,2,1,0:T(8,128)(2,1)} async-done(((bf16[1,1,256,1024]{3,2,1,0:T(8,128)(2,1)}), bf16[1,1,512,1024]{3,2,1,0:T(8,128)(2,1)}) %all-gather.37.cloned.1.call-update) | async-done | bytes 1048592 | tf_op jit(solution)/shard_map/all_gather | solution.py:71
  308.1 43.4 %reduce-scatter.14.cloned.1.call-done = bf16[224,1024]{1,0:T(8,128)(2,1)} async-done(((bf16[1792,1024]{1,0:T(8,128)(2,1)}), bf16[224,1024]{1,0:T(8,128)(2,1)}) %reduce-scatter.14.cloned.1.call-update) | async-done | bytes 458768 | tf_op jit(solution)/shard_map/reduce_scatter | solution.py:66
  352.7 65.6 %all-gather.39.cloned.1.call-done = bf16[1,1,1024,3072]{3,2,1,0:T(8,128)(2,1)} async-done(((bf16[1,1,64,3072]{3,2,1,0:T(8,128)(2,1)}), bf16[1,1,1024,3072]{3,2,1,0:T(8,128)(2,1)}) %all-gather.39.cloned.1.call-update) | async-done | bytes 6291472 | tf_op jit(solution)/shard_map/all_gather | solution.py:186
  432.1 15.7 %collective-permute-done.2 = bf16[224,2048]{1,0:T(8,128)(2,1)} collective-permute-done((bf16[224,2048]{1,0:T(8,128)(2,1)}, bf16[224,2048]{1,0:T(8,128)(2,1)}, u32[]{:S(2)}, u32[]{:S(2)}) %collective-permute-start.2) | collective-permute-done | bytes 917536 | tf_op jit(solution)/shard_map/ppermute | solution.py:196
  465.3 52.3 %all-gather.29.cloned.1.call-done = bf16[1024,1024]{1,0:T(8,128)(2,1)} async-done(((bf16[512,1024]{1,0:T(8,128)(2,1)}), bf16[1024,1024]{1,0:T(8,128)(2,1)}) %all-gather.29.cloned.1.call-update) | async-done | bytes 2097168 | tf_op jit(solution)/shard_map/all_gather | solution.py:71
  517.6 28.2 %all-gather.27.cloned.1.call-done = bf16[1792,1024]{1,0:T(8,128)(2,1)} async-done(((bf16[224,1024]{1,0:T(8,128)(2,1)}), bf16[1792,1024]{1,0:T(8,128)(2,1)}) %all-gather.27.cloned.1.call-update) | async-done | bytes 3670032 | tf_op jit(solution)/shard_map/all_gather | solution.py:63
  545.8 9.7 fusion.226
  555.5 25.2 %all-gather.43.cloned.1.call-done = bf16[1,1,512,1024]{3,2,1,0:T(8,128)(2,1)} async-done(((bf16[1,1,256,1024]{3,2,1,0:T(8,128)(2,1)}), bf16[1,1,512,1024]{3,2,1,0:T(8,128)(2,1)}) %all-gather.43.cloned.1.call-update) | async-done | bytes 1048592 | tf_op jit(solution)/shard_map/all_gather | solution.py:71
  580.7 27.6 %all-gather.45.cloned.1.call-done = bf16[1792,1,1024]{2,0,1:T(8,128)(2,1)} async-done(((bf16[224,1,1024]{2,0,1:T(8,128)(2,1)}), bf16[1792,1,1024]{2,0,1:T(8,128)(2,1)}) %all-gather.45.cloned.1.call-update) | async-done | bytes 3670032 | tf_op jit(solution)/shard_map/all_gather | solution.py:63
  608.3 9.2 multiply_convert_fusion.3
  631.0 36.9 %reduce-scatter.18.cloned.1.call-done = bf16[224,1024]{1,0:T(8,128)(2,1)} async-done(((bf16[1792,1024]{1,0:T(8,128)(2,1)}), bf16[224,1024]{1,0:T(8,128)(2,1)}) %reduce-scatter.18.cloned.1.call-update) | async-done | bytes 458768 | tf_op jit(solution)/shard_map/reduce_scatter | solution.py:66
  669.2 45.2 %reduce-scatter.16.cloned.1.call-done = bf16[224,1024]{1,0:T(8,128)(2,1)} async-done(((bf16[1792,1024]{1,0:T(8,128)(2,1)}), bf16[224,1024]{1,0:T(8,128)(2,1)}) %reduce-scatter.16.cloned.1.call-update) | async-done | bytes 458768 | tf_op jit(solution)/shard_map/reduce_scatter | solution.py:66
  727.8 22.0 %collective-permute-done.3 = bf16[224,2048]{1,0:T(8,128)(2,1)S(1)} collective-permute-done((bf16[224,2048]{1,0:T(8,128)(2,1)S(1)}, bf16[224,2048]{1,0:T(8,128)(2,1)S(1)}, u32[]{:S(2)}, u32[]{:S(2)}) %collective-permute-start.3) | collective-permute-done | bytes 917536 | tf_op jit(solution)/shard_map/ppermute | solution.py:268
  754.8 27.1 %all-gather.31.cloned.1.call-done = bf16[1792,1024]{1,0:T(8,128)(2,1)} async-done(((bf16[224,1024]{1,0:T(8,128)(2,1)}), bf16[1792,1024]{1,0:T(8,128)(2,1)}) %all-gather.31.cloned.1.call-update) | async-done | bytes 3670032 | tf_op jit(solution)/shard_map/all_gather | solution.py:63
  781.9 7.7 multiply_convert_fusion.1
  797.0 8.5 fusion.32
  805.7 8.5 fusion.33
  858.2 21.9 %collective-permute-done.4 = bf16[224,2048]{1,0:T(8,128)(2,1)S(1)} collective-permute-done((bf16[224,2048]{1,0:T(8,128)(2,1)S(1)}, bf16[224,2048]{1,0:T(8,128)(2,1)S(1)}, u32[]{:S(2)}, u32[]{:S(2)}) %collective-permute-start.4) | collective-permute-done | bytes 917536 | tf_op jit(solution)/shard_map/ppermute | solution.py:268
  899.7 26.6 %all_to_all.42 = bf16[8,64,1024]{2,1,0:T(8,128)(2,1)} all-to-all(bf16[8,64,1024]{2,1,0:T(8,128)(2,1)} %bitcast.219), channel_id=1, replica_groups={{0,2,4,6,8,10,12,14},{16,18,20,22,24,26,28,30},{1,3,5,7,9,11,13,15},{17..., dimensions={0} | all-to-all | bytes 2097152 | tf_op jit(solution)/shard_map/all_to_all | solution.py:79
  933.8 23.1 %reduce-scatter.32.cloned.1.call-done = bf16[512,1024]{1,0:T(8,128)(2,1)} async-done(((bf16[1024,1024]{1,0:T(8,128)(2,1)}), bf16[512,1024]{1,0:T(8,128)(2,1)}) %reduce-scatter.32.cloned.1.call-update) | async-done | bytes 1048592 | tf_op jit(solution)/shard_map/reduce_scatter | solution.py:74
  962.6 27.9 %reduce-scatter.38.cloned.1.call-done = bf16[256,1024]{1,0:T(8,128)(2,1)} async-done(((bf16[512,1024]{1,0:T(8,128)(2,1)}), bf16[256,1024]{1,0:T(8,128)(2,1)}) %reduce-scatter.38.cloned.1.call-update) | async-done | bytes 524304 | tf_op jit(solution)/shard_map/reduce_scatter | solution.py:74
  990.5 33.8 %reduce-scatter.36.cloned.1.call-done = bf16[256,1024]{1,0:T(8,128)(2,1)} async-done(((bf16[512,1024]{1,0:T(8,128)(2,1)}), bf16[256,1024]{1,0:T(8,128)(2,1)}) %reduce-scatter.36.cloned.1.call-update) | async-done | bytes 524304 | tf_op jit(solution)/shard_map/reduce_scatter | solution.py:74
  1027.0 85.6 %reduce-scatter.26.cloned.1.call-done = bf16[64,3072]{1,0:T(8,128)(2,1)} async-done(((bf16[1024,3072]{1,0:T(8,128)(2,1)}), bf16[64,3072]{1,0:T(8,128)(2,1)}) %reduce-scatter.26.cloned.1.call-update) | async-done | bytes 393232 | tf_op jit(solution)/shard_map/reduce_scatter | solution.py:282
  1128.1 49.4 %reduce-scatter.30.cloned.1.call-done = bf16[64,1024]{1,0:T(8,128)(2,1)} async-done(((bf16[1024,1024]{1,0:T(8,128)(2,1)}), bf16[64,1024]{1,0:T(8,128)(2,1)}) %reduce-scatter.30.cloned.1.call-update) | async-done | bytes 131088 | tf_op jit(solution)/shard_map/reduce_scatter | solution.py:272
  1177.5 64.2 %reduce-scatter.28.cloned.1.call-done = bf16[64,1024]{1,0:T(8,128)(2,1)} async-done(((bf16[1024,1024]{1,0:T(8,128)(2,1)}), bf16[64,1024]{1,0:T(8,128)(2,1)}) %reduce-scatter.28.cloned.1.call-update) | async-done | bytes 131088 | tf_op jit(solution)/shard_map/reduce_scatter | solution.py:272
  1243.5 74.1 %reduce-scatter.22.cloned.1.call-done = bf16[128,1024]{1,0:T(8,128)(2,1)} async-done(((bf16[2048,1024]{1,0:T(8,128)(2,1)}), bf16[128,1024]{1,0:T(8,128)(2,1)}) %reduce-scatter.22.cloned.1.call-update) | async-done | bytes 262160 | tf_op jit(solution)/shard_map/reduce_scatter | solution.py:285
  1319.3 88.0 %reduce-scatter.24.cloned.1.call-done = bf16[64,3200]{1,0:T(8,128)(2,1)} async-done(((bf16[1024,3200]{1,0:T(8,128)(2,1)}), bf16[64,3200]{1,0:T(8,128)(2,1)}) %reduce-scatter.24.cloned.1.call-update) | async-done | bytes 409616 | tf_op jit(solution)/shard_map/reduce_scatter | solution.py:282
  (303 shorter events, 255.4 us)
Async XLA Ops:
  7.2 58.4 %all-gather.33.cloned.1.call-start = ((), (), s32[]{:S(2)}) async-start(), calls=%async_computation.36 | async-start | bytes 4456448 | tf_op jit(solution)/shard_map/all_gather | solution.py:178
  7.9 122.4 %all-gather.21.cloned.1.call-start = ((), (), s32[]{:S(2)}) async-start(), calls=%async_computation.17 | async-start | bytes 6963200 | tf_op jit(solution)/shard_map/all_gather | solution.py:179
  11.6 161.4 %all-gather.35.cloned.1.call-start = ((), (), s32[]{:S(2)}) async-start(), calls=%async_computation.37 | async-start | bytes 2228224 | tf_op jit(solution)/shard_map/all_gather | solution.py:184
  20.7 121.6 %all-to-all-start = ((bf16[8,64,1024]{2,1,0:T(8,128)(2,1)}), bf16[8,64,1024]{2,1,0:T(8,128)(2,1)S(1)}, u32[]{:S(2)}, u32[]{:S(2)}) async-start(bf16[8,64,1024]{2,1,0:T(8,128)(2,1)} %all_to_all.28), calls=%async_computation | async-start | bytes 2097152 | tf_op jit(solution)/shard_map/all_to_all | solution.py:79
  26.8 203.6 %all-gather.25.cloned.1.call-start = ((), (), s32[]{:S(2)}) async-start(), calls=%async_computation.19 | async-start | bytes 3145728 | tf_op jit(solution)/shard_map/all_gather | solution.py:71
  137.9 23.4 %collective-permute-start.1 = (bf16[224,2048]{1,0:T(8,128)(2,1)S(1)}, bf16[224,2048]{1,0:T(8,128)(2,1)}, u32[]{:S(2)}, u32[]{:S(2)}) collective-permute-start(bf16[224,2048]{1,0:T(8,128)(2,1)S(1)} %slice.227), channel_id=1, source_target_pairs={{0,1},{2,3},{4,5},{6,7},{8,9},{10,11},{12,13},{14,15},{16,17},{18,... | collective-permute-start | bytes 2752520 | tf_op jit(solution)/shard_map/ppermute | solution.py:196
  143.3 115.1 %all-gather.23.cloned.1.call-start = ((), (), s32[]{:S(2)}) async-start(), calls=%async_computation.18 | async-start | bytes 4128768 | tf_op jit(solution)/shard_map/all_gather | solution.py:63
  176.4 117.4 %all-gather.37.cloned.1.call-start = ((), (), s32[]{:S(2)}) async-start(), calls=%async_computation.38 | async-start | bytes 1572864 | tf_op jit(solution)/shard_map/all_gather | solution.py:71
  177.5 174.0 %reduce-scatter.14.cloned.1.call-start = ((), (), s32[]{:S(2)}) async-start(), calls=%async_computation.20 | async-start | bytes 4128768 | tf_op jit(solution)/shard_map/reduce_scatter | solution.py:66
  299.0 119.3 %all-gather.39.cloned.1.call-start = ((), (), s32[]{:S(2)}) async-start(), calls=%async_computation.39 | async-start | bytes 6684672 | tf_op jit(solution)/shard_map/all_gather | solution.py:186
  299.8 160.6 %all-gather.41.cloned.1.call-start = ((), (), s32[]{:S(2)}) async-start(), calls=%async_computation.40 | async-start | bytes 2228224 | tf_op jit(solution)/shard_map/all_gather | solution.py:187
  304.5 124.0 %all-to-all-start.1 = ((bf16[8,64,1024]{2,1,0:T(8,128)(2,1)}), bf16[8,64,1024]{2,1,0:T(8,128)(2,1)S(1)}, u32[]{:S(2)}, u32[]{:S(2)}) async-start(bf16[8,64,1024]{2,1,0:T(8,128)(2,1)} %all_to_all.31), calls=%async_computation.2 | async-start | bytes 2097152 | tf_op jit(solution)/shard_map/all_to_all | solution.py:79
  308.0 209.6 %all-gather.29.cloned.1.call-start = ((), (), s32[]{:S(2)}) async-start(), calls=%async_computation.22 | async-start | bytes 3145728 | tf_op jit(solution)/shard_map/all_gather | solution.py:71
  424.1 23.7 %collective-permute-start.2 = (bf16[224,2048]{1,0:T(8,128)(2,1)}, bf16[224,2048]{1,0:T(8,128)(2,1)}, u32[]{:S(2)}, u32[]{:S(2)}) collective-permute-start(bf16[224,2048]{1,0:T(8,128)(2,1)} %slice.237), channel_id=1, source_target_pairs={{0,1},{2,3},{4,5},{6,7},{8,9},{10,11},{12,13},{14,15},{16,17},{18,... | collective-permute-start | bytes 2752520 | tf_op jit(solution)/shard_map/ppermute | solution.py:196
  429.4 116.4 %all-gather.27.cloned.1.call-start = ((), (), s32[]{:S(2)}) async-start(), calls=%async_computation.21 | async-start | bytes 4128768 | tf_op jit(solution)/shard_map/all_gather | solution.py:63
  463.8 116.9 %all-gather.43.cloned.1.call-start = ((), (), s32[]{:S(2)}) async-start(), calls=%async_computation.41 | async-start | bytes 1572864 | tf_op jit(solution)/shard_map/all_gather | solution.py:71
  464.4 143.9 %all-gather.45.cloned.1.call-start = ((), (), s32[]{:S(2)}) async-start(), calls=%async_computation.42 | async-start | bytes 4128768 | tf_op jit(solution)/shard_map/all_gather | solution.py:63
  465.1 202.8 %reduce-scatter.18.cloned.1.call-start = ((), (), s32[]{:S(2)}) async-start(), calls=%async_computation.24 | async-start | bytes 4128768 | tf_op jit(solution)/shard_map/reduce_scatter | solution.py:66
  625.0 89.5 %reduce-scatter.16.cloned.1.call-start = ((), (), s32[]{:S(2)}) async-start(), calls=%async_computation.23 | async-start | bytes 4128768 | tf_op jit(solution)/shard_map/reduce_scatter | solution.py:66
  630.8 151.1 %all-gather.31.cloned.1.call-start = ((), (), s32[]{:S(2)}) async-start(), calls=%async_computation.25 | async-start | bytes 4128768 | tf_op jit(solution)/shard_map/all_gather | solution.py:63
  726.3 23.5 %collective-permute-start.3 = (bf16[224,2048]{1,0:T(8,128)(2,1)S(1)}, bf16[224,2048]{1,0:T(8,128)(2,1)S(1)}, u32[]{:S(2)}, u32[]{:S(2)}) collective-permute-start(bf16[224,2048]{1,0:T(8,128)(2,1)S(1)} %pad_maximum_fusion.12), channel_id=1, source_target_pairs={{1,0},{3,2},{5,4},{7,6},{9,8},{11,10},{13,12},{15,14},{17,16},{19,... | collective-permute-start | bytes 2752520 | tf_op jit(solution)/shard_map/ppermute | solution.py:268
  754.3 85.4 %reduce-scatter.20.cloned.1.call-start = ((), (), s32[]{:S(2)}) async-start(), calls=%async_computation.26 | async-start | bytes 4128768 | tf_op jit(solution)/shard_map/reduce_scatter | solution.py:66
  796.9 102.7 %reduce-scatter.34.cloned.1.call-start = ((), (), s32[]{:S(2)}) async-start(), calls=%async_computation.33 | async-start | bytes 3145728 | tf_op jit(solution)/shard_map/reduce_scatter | solution.py:74
  805.5 151.4 %reduce-scatter.32.cloned.1.call-start = ((), (), s32[]{:S(2)}) async-start(), calls=%async_computation.32 | async-start | bytes 3145728 | tf_op jit(solution)/shard_map/reduce_scatter | solution.py:74
  814.3 176.2 %reduce-scatter.38.cloned.1.call-start = ((), (), s32[]{:S(2)}) async-start(), calls=%async_computation.35 | async-start | bytes 1572864 | tf_op jit(solution)/shard_map/reduce_scatter | solution.py:74
  820.0 204.3 %reduce-scatter.36.cloned.1.call-start = ((), (), s32[]{:S(2)}) async-start(), calls=%async_computation.34 | async-start | bytes 1572864 | tf_op jit(solution)/shard_map/reduce_scatter | solution.py:74
  825.8 286.7 %reduce-scatter.26.cloned.1.call-start = ((), (), s32[]{:S(2)}) async-start(), calls=%async_computation.29 | async-start | bytes 6684672 | tf_op jit(solution)/shard_map/reduce_scatter | solution.py:282
  831.6 345.9 %reduce-scatter.30.cloned.1.call-start = ((), (), s32[]{:S(2)}) async-start(), calls=%async_computation.31 | async-start | bytes 2228224 | tf_op jit(solution)/shard_map/reduce_scatter | solution.py:272
  835.0 406.7 %reduce-scatter.28.cloned.1.call-start = ((), (), s32[]{:S(2)}) async-start(), calls=%async_computation.30 | async-start | bytes 2228224 | tf_op jit(solution)/shard_map/reduce_scatter | solution.py:272
  853.4 464.1 %reduce-scatter.22.cloned.1.call-start = ((), (), s32[]{:S(2)}) async-start(), calls=%async_computation.27 | async-start | bytes 4456448 | tf_op jit(solution)/shard_map/reduce_scatter | solution.py:285
  891.8 515.5 %reduce-scatter.24.cloned.1.call-start = ((), (), s32[]{:S(2)}) async-start(), calls=%async_computation.28 | async-start | bytes 6963200 | tf_op jit(solution)/shard_map/reduce_scatter | solution.py:282
  956.9 157.6 %all-to-all-start.2 = ((bf16[8,64,1024]{2,1,0:T(8,128)(2,1)}), bf16[8,64,1024]{2,1,0:T(8,128)(2,1)}, u32[]{:S(2)}, u32[]{:S(2)}) async-start(bf16[8,64,1024]{2,1,0:T(8,128)(2,1)} %bitcast.218), calls=%async_computation.12 | async-start | bytes 2097152 | tf_op jit(solution)/shard_map/all_to_all | solution.py:79
  (56 other events, 908.5 us)
Sparse Core Ops, SparseCore 0:
  10.2 55.3 all-gather.32
  68.5 61.8 all-gather.20
  133.1 39.8 all-gather.34
  175.0 55.3 all-gather.24
  232.4 25.9 all-gather.22
  260.3 33.4 all-gather.36
  299.1 52.3 reduce-scatter.13
  354.4 63.8 all-gather.38
  420.5 39.8 all-gather.40
  462.3 55.2 all-gather.28
  519.9 25.9 all-gather.26
  547.2 33.4 all-gather.42
  582.4 25.9 all-gather.44
  625.1 42.7 reduce-scatter.17
  670.1 44.3 reduce-scatter.15
  754.4 27.3 all-gather.30
  797.1 42.5 reduce-scatter.19
  842.4 57.2 reduce-scatter.33
  902.6 54.2 reduce-scatter.31
  959.0 31.4 reduce-scatter.37
  992.8 31.4 reduce-scatter.35
  1028.2 84.2 reduce-scatter.25
  1116.7 60.7 reduce-scatter.29
  1181.1 60.5 reduce-scatter.27
  1246.0 71.4 reduce-scatter.21
  1321.3 85.9 reduce-scatter.23

commit v2 on v1

--- a/solution.py
+++ b/solution.py
@@ -3,6 +3,8 @@
 import jax
 import jax.numpy as jnp
 from jax import lax
+from jax.experimental import pallas as pl
+from jax.experimental.pallas import tpu as pltpu
 from jax.sharding import PartitionSpec as P
 
 HEADS = 16
@@ -51,48 +53,377 @@
     return jnp.dot(values, head_matrix().T, precision=HIGHEST)
 
 
+MESH = pl.DeviceIdType.MESH
+VMEM_LIMIT = 60 * 2**20
+
+
+def in_vmem(count):
+    return [pl.BlockSpec(memory_space=pltpu.VMEM)] * count
+
+
+class Team:
+    SCRATCH_COPIES = 19
+
+    def __init__(self, rows, mine, everyone, sums, scratch):
+        (self.part, self.from_core, self.from_across, self.from_x, self.from_z) = scratch[:5]
+        (self.to_x, self.to_z, self.to_across, self.sent, self.got) = scratch[5:10]
+        self.rows, self.half = rows, rows // 2
+        self.mine, self.everyone, self.sums = mine, everyone, sums
+        index = lax.axis_index("frames")
+        self.place = lax.axis_index("pos")
+        member = lax.rem(index, 8)
+        self.core = lax.rem(member, 2)
+        self.x = lax.rem(member // 2, 2)
+        self.z = member // 4
+        self.core_peer = index + 1 - 2 * self.core
+        self.x_peer = index + 2 - 4 * self.x
+        self.z_peer = index + 4 - 8 * self.z
+
+    @staticmethod
+    def scratch(rows, width):
+        half = rows // 2
+        return [
+            pltpu.VMEM((4, rows, width), BF),
+            pltpu.VMEM((4, rows, width), BF),
+            pltpu.VMEM((2, half, width), BF),
+            pltpu.VMEM((rows, width), BF),
+            pltpu.VMEM((rows, width), BF),
+            pltpu.VMEM((rows, width), BF),
+            pltpu.VMEM((rows, width), BF),
+            pltpu.VMEM((rows, width), BF),
+            pltpu.SemaphoreType.DMA((Team.SCRATCH_COPIES,)),
+            pltpu.SemaphoreType.DMA((Team.SCRATCH_COPIES,)),
+        ]
+
+    def greet(self):
+        barrier = pltpu.get_barrier_semaphore()
+        for peer in (self.core_peer, self.x_peer, self.z_peer):
+            pl.semaphore_signal(barrier, inc=1, device_id=(peer, self.place), device_id_type=MESH)
+        pl.semaphore_wait(barrier, 3)
+
+    def copy(self, number, source, target, peer):
+        return pltpu.make_async_remote_copy(
+            src_ref=source,
+            dst_ref=target,
+            send_sem=self.sent.at[number],
+            recv_sem=self.got.at[number],
+            device_id=(peer, self.place),
+            device_id_type=MESH,
+        )
+
+    def pair_start(self, m):
+        x = self.x + (m % 2) * (1 - 2 * self.x)
+        z = self.z + (m // 2) * (1 - 2 * self.z)
+        return pl.multiple_of((z * 2 + x) * (2 * self.rows), 2 * self.rows)
+
+    def shard(self, m, part=None, core=None):
+        core = self.core if core is None else core
+        start = self.pair_start(m) + core * self.rows
+        size = self.rows
+        if part is not None:
+            start, size = start + part * self.half, self.half
+        return self.everyone.at[pl.ds(pl.multiple_of(start, 16), size)]
+
+    def gather_copies(self):
+        own = self.shard(0)
+        x_rows, z_rows = self.shard(1), self.shard(2)
+        x_low, z_high = self.shard(1, 1), self.shard(2, 0)
+        high, low = self.shard(3, 0), self.shard(3, 1)
+        return [
+            self.copy(0, self.mine, own, self.core_peer),
+            self.copy(1, self.mine, own, self.x_peer),
+            self.copy(2, self.mine, own, self.z_peer),
+            self.copy(3, x_rows, x_rows, self.core_peer),
+            self.copy(4, x_low, x_low, self.z_peer),
+            self.copy(5, z_rows, z_rows, self.core_peer),
+            self.copy(6, z_high, z_high, self.x_peer),
+            self.copy(7, high, high, self.core_peer),
+            self.copy(8, low, low, self.core_peer),
+        ]
+
+    def arrived(self, number):
+        other = 1 - self.core
+        target = [
+            self.shard(0, core=other),
+            self.shard(1),
+            self.shard(2),
+            self.shard(1, core=other),
+            self.shard(3, 1),
+            self.shard(2, core=other),
+            self.shard(3, 0),
+            self.shard(3, 0, core=other),
+            self.shard(3, 1, core=other),
+        ][number]
+        self.copy(number, target, target, self.core_peer).wait_recv()
+
+    def sum_copies(self):
+        half = self.half
+        high, low = pl.ds(0, half), pl.ds(half, half)
+        copies = [
+            self.copy(9 + m, self.part.at[m], self.from_core.at[m], self.core_peer)
+            for m in range(4)
+        ]
+        copies += [
+            self.copy(13, self.to_across.at[high], self.from_across.at[0], self.x_peer),
+            self.copy(14, self.to_across.at[low], self.from_across.at[1], self.z_peer),
+            self.copy(15, self.to_x.at[high], self.from_x.at[high], self.x_peer),
+            self.copy(16, self.to_x.at[low], self.from_x.at[low], self.x_peer),
+            self.copy(17, self.to_z.at[low], self.from_z.at[low], self.z_peer),
+            self.copy(18, self.to_z.at[high], self.from_z.at[high], self.z_peer),
+        ]
+        return copies
+
+    def run(self, compute, between, result):
+        half, rows = self.half, self.rows
+        self.greet()
+        gather = self.gather_copies()
+        adds = self.sum_copies()
+        for copy in gather[:3]:
+            copy.start()
+        start = self.pair_start(0) + self.core * rows
+        self.everyone[pl.ds(pl.multiple_of(start, 16), rows), :] = self.mine[...]
+
+        def total(m, first):
+            return self.sums[m, first : first + half, :] + self.from_core[
+                m, first : first + half, :
+            ].astype(F32)
+
+        def step(m, carry):
+            @pl.when(m == 0)
+            def _():
+                self.arrived(0)
+
+            @pl.when(m == 1)
+            def _():
+                self.arrived(1)
+                gather[4].start()
+                gather[3].start()
+                self.arrived(2)
+                gather[6].start()
+                gather[5].start()
+                self.arrived(3)
+
+            @pl.when(m == 2)
+            def _():
+                self.arrived(5)
+
+            @pl.when(m == 3)
+            def _():
+                self.arrived(6)
+                gather[7].start()
+                self.arrived(4)
+                gather[8].start()
+                self.arrived(7)
+                self.arrived(8)
+
+            compute(m, self.pair_start(m))
+            self.copy(9 + m, self.part.at[m], self.from_core.at[m], self.core_peer).start()
+
+            @pl.when(m == 2)
+            def _():
+                adds[1].wait_recv()
+                self.to_x[:half, :] = total(1, 0).astype(BF)
+                adds[6].start()
+
+            return carry
+
+        lax.fori_loop(0, 4, step, 0)
+        adds[3].wait_recv()
+        self.to_across[:half, :] = total(3, 0).astype(BF)
+        adds[4].start()
+        self.to_across[half:, :] = total(3, half).astype(BF)
+        adds[5].start()
+        adds[2].wait_recv()
+        self.to_z[half:, :] = total(2, half).astype(BF)
+        adds[8].start()
+        between()
+        adds[5].wait_recv()
+        self.to_x[half:, :] = (total(1, half) + self.from_across[1].astype(F32)).astype(BF)
+        adds[7].start()
+        adds[4].wait_recv()
+        self.to_z[:half, :] = (total(2, 0) + self.from_across[0].astype(F32)).astype(BF)
+        adds[9].start()
+        adds[0].wait_recv()
+        for number in (6, 7, 8, 9):
+            adds[number].wait_recv()
+        for first in (0, half):
+            rows_here = slice(first, first + half)
+            result[rows_here, :] = (
+                total(0, first)
+                + self.from_x[rows_here, :].astype(F32)
+                + self.from_z[rows_here, :].astype(F32)
+            )
+        for copy in gather + adds:
+            copy.wait_send()
+
+
+def split_pair(team, m, value, sums, part):
+    rows = team.rows
+
+    @pl.when(team.core == 0)
+    def _():
+        sums[m] = value[:rows]
+        part[m] = value[rows:].astype(BF)
+
+    @pl.when(team.core == 1)
+    def _():
+        sums[m] = value[rows:]
+        part[m] = value[:rows].astype(BF)
+
+
+def ffn_forward_kernel(normed, both, down, everyone, pre, gated, result, sums, *scratch):
+    rows = normed.shape[0]
+    hidden = down.shape[0]
+    tile = min(hidden, 256)
+    team = Team(rows, normed, everyone, sums, scratch)
+
+    def compute(m, start):
+        here = pl.ds(start, 2 * rows)
+        block = everyone[here, :]
+        for first in range(0, hidden, tile):
+            g = plain(block, both[:, first : first + tile])
+            u = plain(block, both[:, hidden + first : hidden + first + tile])
+            pre[here, first : first + tile] = g
+            pre[here, hidden + first : hidden + first + tile] = u
+            gated[here, first : first + tile] = (g * jax.nn.sigmoid(g) * u).astype(BF)
+        split_pair(team, m, plain(gated[here, :], down[...]), sums, team.part)
+
+    team.run(compute, lambda: None, result)
+
+
+def ffn_backward_kernel(
+    grad, both, down, pre, gated, normed, result, both_part, down_part, everyone, d_both, sums, *scratch
+):
+    rows = grad.shape[0]
+    hidden = down.shape[0]
+    tile = min(hidden, 256)
+    team = Team(rows, grad, everyone, sums, scratch)
+
+    def compute(m, start):
+        here = pl.ds(start, 2 * rows)
+        block = everyone[here, :]
+        for first in range(0, hidden, tile):
+            d_gated = right_trans(block, down[first : first + tile, :])
+            g = pre[here, first : first + tile]
+            u = pre[here, hidden + first : hidden + first + tile]
+            sig = jax.nn.sigmoid(g)
+            d_both[here, first : first + tile] = (
+                d_gated * u * sig * (1.0 + g * (1.0 - sig))
+            ).astype(BF)
+            d_both[here, hidden + first : hidden + first + tile] = (d_gated * g * sig).astype(BF)
+        split_pair(team, m, right_trans(d_both[here, :], both[...]), sums, team.part)
+
+    def between():
+        def down_step(i, carry):
+            cols = pl.ds(pl.multiple_of(i * 256, 256), 256)
+            down_part[:, cols] = left_trans(gated[...], everyone[:, cols])
+            return carry
+
+        def both_step(i, carry):
+            cols = pl.ds(pl.multiple_of(i * 256, 256), 256)
+            both_part[:, cols] = left_trans(normed[...], d_both[:, cols]).astype(BF)
+            return carry
+
+        lax.fori_loop(0, down_part.shape[1] // 256, down_step, 0)
+        lax.fori_loop(0, both_part.shape[1] // 256, both_step, 0)
+
+    team.run(compute, between, result)
+
+
+def ffn_forward(normed, both, down):
+    rows, width = normed.shape
+    hidden = down.shape[0]
+    return pl.pallas_call(
+        ffn_forward_kernel,
+        out_shape=(
+            jax.ShapeDtypeStruct((8 * rows, width), BF),
+            jax.ShapeDtypeStruct((8 * rows, 2 * hidden), F32),
+            jax.ShapeDtypeStruct((8 * rows, hidden), BF),
+            jax.ShapeDtypeStruct((rows, width), F32),
+        ),
+        in_specs=in_vmem(3),
+        out_specs=in_vmem(4),
+        scratch_shapes=[pltpu.VMEM((4, rows, width), F32)] + Team.scratch(rows, width),
+        compiler_params=pltpu.CompilerParams(
+            collective_id=1, has_side_effects=True, vmem_limit_bytes=VMEM_LIMIT
+        ),
+        name="ffn_forward",
+    )(normed, both, down)
+
+
+def ffn_backward(grad, both, down, pre, gated, normed):
+    rows, width = grad.shape
+    hidden = down.shape[0]
+    return pl.pallas_call(
+        ffn_backward_kernel,
+        out_shape=(
+            jax.ShapeDtypeStruct((rows, width), F32),
+            jax.ShapeDtypeStruct((width, 2 * hidden), BF),
+            jax.ShapeDtypeStruct((hidden, width), F32),
+        ),
+        in_specs=in_vmem(6),
+        out_specs=in_vmem(3),
+        scratch_shapes=[
+            pltpu.VMEM((8 * rows, width), BF),
+            pltpu.VMEM((8 * rows, 2 * hidden), BF),
+            pltpu.VMEM((4, rows, width), F32),
+        ]
+        + Team.scratch(rows, width),
+        compiler_params=pltpu.CompilerParams(
+            collective_id=2, has_side_effects=True, vmem_limit_bytes=VMEM_LIMIT
+        ),
+        name="ffn_backward",
+    )(grad, both, down, pre, gated, normed)
+
+
 class Plan:
     def __init__(self, count):
         self.count = count
-        self.team = 8 if count % 8 == 0 else count
+        self.team = 8
         self.teams = count // self.team
-        self.inside = [[g * self.team + t for t in range(self.team)] for g in range(self.teams)]
         self.across = [[g * self.team + t for g in range(self.teams)] for t in range(self.team)]
-
-    def gather_inside(self, rows):
-        return lax.all_gather(rows, "frames", axis=0, tiled=True, axis_index_groups=self.inside)
-
-    def scatter_inside(self, rows):
-        return lax.psum_scatter(
-            rows, "frames", scatter_dimension=0, tiled=True, axis_index_groups=self.inside
-        )
-
-    def gather_across(self, rows):
-        return lax.all_gather(rows, "frames", axis=0, tiled=True, axis_index_groups=self.across)
-
-    def scatter_across(self, rows):
-        return lax.psum_scatter(
-            rows, "frames", scatter_dimension=0, tiled=True, axis_index_groups=self.across
-        )
-
-    def swap_inside(self, parts):
-        return lax.all_to_all(
-            parts, "frames", split_axis=0, concat_axis=0, tiled=True, axis_index_groups=self.inside
-        )
 
     def ffn_weights(self, gate, up, down):
         rows = gate.shape[0]
         both = jnp.stack([gate, up], axis=1).reshape(rows, 2, self.teams, self.team, -1)
-        parts = both.transpose(3, 0, 1, 2, 4).reshape(self.team * rows, -1)
-        mine = self.swap_inside(parts)
-        return self.gather_across(mine), self.gather_across(down)
+        parts = both.transpose(3, 0, 1, 2, 4).reshape(self.team, rows, -1)
+        parts = jnp.broadcast_to(parts[None], (self.teams,) + parts.shape)
+        parts = parts.reshape((self.count,) + parts.shape[2:])
+        mine = lax.all_to_all(parts, "frames", split_axis=0, concat_axis=0, tiled=True)
+        return mine.reshape(self.count * rows, -1), self.gather_across(down)
+
+    def gather_across(self, rows):
+        if self.teams != 2:
+            return lax.all_gather(rows, "frames", axis=0, tiled=True, axis_index_groups=self.across)
+        theirs = lax.ppermute(rows, "frames", self.partners())
+        first = lax.axis_index("frames") < self.team
+        return jnp.concatenate([jnp.where(first, rows, theirs), jnp.where(first, theirs, rows)])
+
+    def scatter_across(self, rows):
+        if self.teams != 2:
+            part = lax.psum_scatter(
+                rows.astype(BF),
+                "frames",
+                scatter_dimension=0,
+                tiled=True,
+                axis_index_groups=self.across,
+            )
+            return part.astype(F32)
+        half = rows.shape[0] // 2
+        first = lax.axis_index("frames") < self.team
+        mine = jnp.where(first, rows[:half], rows[half:])
+        sent = jnp.where(first, rows[half:], rows[:half]).astype(BF)
+        return mine + lax.ppermute(sent, "frames", self.partners()).astype(F32)
+
+    def partners(self):
+        return [(i, (i + self.team) % self.count) for i in range(self.count)]
 
     def ffn_grads(self, both_part, down_part):
-        down = self.scatter_across(down_part.astype(BF)).astype(F32)
-        both = self.scatter_across(both_part.astype(BF))
-        parts = self.swap_inside(both)
-        rows = parts.shape[0] // self.team
-        parts = parts.astype(F32).reshape(self.team, rows, 2, self.teams, -1)
+        down = self.scatter_across(down_part)
+        parts = both_part.astype(BF).reshape(self.count, -1, both_part.shape[1])
+        parts = lax.all_to_all(parts, "frames", split_axis=0, concat_axis=0, tiled=True)
+        rows = parts.shape[1]
+        parts = parts.astype(F32).reshape(self.teams, self.team, rows, 2, self.teams, -1).sum(axis=0)
         both = parts.transpose(1, 2, 3, 0, 4).reshape(rows, 2, -1)
         return both[:, 0], both[:, 1], down
 
@@ -198,14 +529,9 @@
         middle = stream + plain(attended, out_all[layer])
         inv_ffn = inverse_rms(middle)
         normed_ffn = (middle * inv_ffn * gain_rows[2 + layer]).astype(BF)
-        team_normed = plan.gather_inside(normed_ffn)
         both_all, down_all = ffn_all[layer]
-        pre = plain(team_normed, both_all)
-        half = pre.shape[1] // 2
-        gate_pre, up_pre = pre[:, :half], pre[:, half:]
-        gated = (jax.nn.silu(gate_pre) * up_pre).astype(BF)
-        result = plain(gated, down_all).astype(BF)
-        new_stream = middle + plan.scatter_inside(result).astype(F32)
+        team_normed, pre, gated, summed = ffn_forward(normed_ffn, both_all, down_all)
+        new_stream = middle + summed
         kept.append(
             (
                 stream,
@@ -219,8 +545,7 @@
                 middle,
                 inv_ffn,
                 team_normed,
-                gate_pre,
-                up_pre,
+                pre,
                 gated,
             )
         )
@@ -243,20 +568,13 @@
             middle,
             inv_ffn,
             team_normed,
-            gate_pre,
-            up_pre,
+            pre,
             gated,
         ) = kept[layer]
         both_all, down_all = ffn_all[layer]
-        grad_out = plan.gather_inside(gradient.astype(BF))
-        grad_gated = right_trans(grad_out, down_all)
-        sig = jax.nn.sigmoid(gate_pre)
-        grad_gate = (grad_gated * up_pre * sig * (1.0 + gate_pre * (1.0 - sig))).astype(BF)
-        grad_up = (grad_gated * gate_pre * sig).astype(BF)
-        grad_both = jnp.concatenate([grad_gate, grad_up], axis=1)
-        grad_normed = plan.scatter_inside(right_trans(grad_both, both_all).astype(BF)).astype(F32)
-        down_part = left_trans(gated, grad_out)
-        both_part = left_trans(team_normed, grad_both)
+        grad_normed, both_part, down_part = ffn_backward(
+            gradient.astype(BF), both_all, down_all, pre, gated, team_normed
+        )
         ffn_shares = plan.ffn_grads(both_part, down_part)
         grad_middle, gain_parts[2 + layer] = norm_back(
             grad_normed, middle, inv_ffn, gain_rows[2 + layer]

time: 1430 us -> 1030 us (0.72)
  waiting for transfers between devices: 1100 us -> 504 us
  Pallas kernels: 0 us -> 268 us
  matrix products: 164 us -> 72.6 us
  blocking collectives: 26.6 us -> 0 us
  other arithmetic: 36.9 us -> 58.7 us
  starting transfers between devices: 30.8 us -> 47.3 us
    pallas_call x0 -> x4, Pallas kernels: none -> 268 us  [the longest x2 167 us: ffn_forward(): pl.pallas_call(ffn_forward_kernel, out_shape=(jax.ShapeDtypeStruct((8 * r...]
    all_gather x8 -> x0, waiting for transfers between devices: 265 us -> none  [the longest x4 154 us: gather_across(): lax.all_gather(rows, 'frames', axis=0, tiled=True, axis_index_groups=self...]
    reduce_scatter x8 -> x0, waiting for transfers between devices: 217 us -> none  [the longest x4 130 us: scatter_inside(): lax.psum_scatter(rows, 'frames', scatter_dimension=0, tiled=True, axis_in...]
    reduce_scatter x2, waiting for transfers between devices: 114 us -> 0.01 us  [body(): lax.psum_scatter(out_part, 'frames', scatter_dimension=0, tiled=True)]
    ppermute x0 -> x4, waiting for transfers between devices: none -> 112 us  [the longest x2 112 us: scatter_across(): return mine + lax.ppermute(sent, 'frames', self.partners()).astype(F32)]
    reduce_scatter x1, waiting for transfers between devices: 74.1 us -> 0.01 us  [body(): lax.psum_scatter(table_part, 'frames', scatter_dimension=0, tiled=True)]
    all_gather x1, waiting for transfers between devices: 65.6 us -> 0.02 us  [body(): qkv_all[1] = lax.all_gather(w_qkv[1, 0], 'frames', axis=0, tiled=True)]
    reduce_scatter x2, waiting for transfers between devices: 174 us -> 132 us  [body(): lax.psum_scatter(qkv_part, 'frames', scatter_dimension=0, tiled=True)]
  transfers between devices with their start and end apart: 34 -> 23, of which waited for: 30 -> 12; matrix products, arithmetic and copies ran while one was open for 13% -> 16% of each run, Pallas kernels for 0% -> 17%
where the time goes in v2:
time: 1030 us; the launch traced here: 1020 us
  waiting for transfers between devices  504 us (49%)
  Pallas kernels  268 us (26%)
  matrix products  72.6 us (7%)
  other arithmetic  58.7 us (6%)
  local copies, waits for them, and re-layouts  56.8 us (6%)
  starting transfers between devices  47.3 us (5%)
  between operations  15.6 us (2%)
    pallas_call x2, Pallas kernels, ffn_forward(): pl.pallas_call(ffn_forward_kernel, out_shape=(jax.ShapeDtypeStruct((8 * r...  167 us
    reduce_scatter x2, waiting for transfers between devices, body(): lax.psum_scatter(qkv_part, 'frames', scatter_dimension=0, tiled=True)  132 us
    ppermute x2, waiting for transfers between devices, scatter_across(): return mine + lax.ppermute(sent, 'frames', self.partners()).astype(F32)  112 us
    pallas_call x2, Pallas kernels, ffn_backward(): pl.pallas_call(ffn_backward_kernel, out_shape=(jax.ShapeDtypeStruct((rows...  101 us
    all_gather x1, waiting for transfers between devices, body(): full_table = lax.all_gather(code_table[0], 'frames', axis=0, tiled=True)  76 us
    all_gather x1, waiting for transfers between devices, body(): lax.all_gather(jnp.concatenate([w_qkv[0, 0], gains], axis=1), 'frames', a...  74.6 us
    ppermute x2, waiting for transfers between devices, body(): arrived = lax.ppermute(d_other.astype(BF), 'pos', backward).astype(F32)  41.9 us
    all_to_all x2, waiting for transfers between devices, ffn_grads(): lax.all_to_all(parts, 'frames', split_axis=0, concat_axis=0, tiled=True)  36.8 us
  transfers between devices with their start and end apart: 23, of which 12 were waited for; matrix products, arithmetic and copies ran while one was open for 16% of the time, Pallas kernels for 17%

profile of v2, /device:TPU:0, one launch (start us, length us, event | category | flops | bytes accessed | tf_op | source)
XLA Modules:
  0.0 1023.8 jit_solution(8793912315797627357)
XLA Ops:
  21.8 7.2 all-to-all-start
  36.7 76.0 %all-gather.12.cloned.1.call-done = bf16[1,2048,1024]{2,1,0:T(8,128)(2,1)} async-done(((bf16[1,128,1024]{2,1,0:T(8,128)(2,1)}), bf16[1,2048,1024]{2,1,0:T(8,128)(2,1)}) %all-gather.12.cloned.1.call-update) | async-done | bytes 4194320 | tf_op jit(solution)/shard_map/all_gather | solution.py:509
  112.7 3.5 multiply_reduce_fusion.11
  116.9 74.6 %all-gather.10.cloned.1.call-done = bf16[1024,3200]{1,0:T(8,128)(2,1)} async-done(((bf16[64,3200]{1,0:T(8,128)(2,1)}), bf16[1024,3200]{1,0:T(8,128)(2,1)}) %all-gather.10.cloned.1.call-update) | async-done | bytes 6553616 | tf_op jit(solution)/shard_map/all_gather | solution.py:510
  193.6 4.4 fusion.12
  199.4 3.6 collective-permute-start.1
  213.4 9.7 collective-permute-done.1
  228.8 4.9 all-gather.14.cloned.1.call-done
  236.2 3.6 broadcast_in_dim.96
  239.8 4.4 all-to-all-start.1
  245.2 115.9 %ffn_forward.2 = (bf16[1792,1024]{1,0:T(8,128)(2,1)}, f32[1792,1024]{1,0:T(8,128)}, bf16[1792,512]{1,0:T(8,128)(2,1)}, f32[224,1024]{1,0:T(8,128)}) custom-call(bf16[224,1024]{1,0:T(8,128)(2,1)} %multiply_convert_fusion.2.normed, bf16[1024,1024]{1,0:T(8,128)(2,1)} %bitcast.179, bf16[512,1024]{1,0:T(8,128)(2,1)} %pad_maximum_fusion.2.down), custom_call_target="tpu_custom_call" | custom-call | tf_op jit(solution)/shard_map/ffn_forward/pallas_call | solution.py:336
  362.8 4.4 fusion.15
  372.9 14.6 %collective-permute-done.3 = bf16[224,2048]{1,0:T(8,128)(2,1)S(1)} collective-permute-done((bf16[224,2048]{1,0:T(8,128)(2,1)S(1)}, bf16[224,2048]{1,0:T(8,128)(2,1)S(1)}, u32[]{:S(2)}, u32[]{:S(2)}) %collective-permute-start.3) | collective-permute-done | bytes 917536 | tf_op jit(solution)/shard_map/ppermute | solution.py:527
  397.2 51.2 %ffn_forward.3 = (bf16[1792,1024]{1,0:T(8,128)(2,1)}, f32[1792,1024]{1,0:T(8,128)}, bf16[1792,512]{1,0:T(8,128)(2,1)}, f32[224,1024]{1,0:T(8,128)}) custom-call(bf16[224,1024]{1,0:T(8,128)(2,1)} %multiply_convert_fusion.normed, bf16[1024,1024]{1,0:T(8,128)(2,1)} %bitcast.21.both, bf16[512,1024]{1,0:T(8,128)(2,1)} %pad_maximum_fusion.3.down), custom_call_target="tpu_custom_call" | custom-call | tf_op jit(solution)/shard_map/ffn_forward/pallas_call | solution.py:336
  448.4 47.6 %ffn_backward.2 = (f32[224,1024]{1,0:T(8,128)}, bf16[1024,1024]{1,0:T(8,128)(2,1)}, f32[512,1024]{1,0:T(8,128)}) custom-call(bf16[224,1024]{1,0:T(8,128)(2,1)} %bitcast.196, bf16[1024,1024]{1,0:T(8,128)(2,1)} %bitcast.21.both, bf16[512,1024]{1,0:T(8,128)(2,1)} %pad_maximum_fusion.3.down, f32[1792,1024]{1,0:T(8,128)} %get-tuple-element.26.pre, ...), custom_call_target="tpu_custom_call" | custom-call | tf_op jit(solution)/shard_map/ffn_backward/pallas_call | solution.py:357
  513.1 20.8 %collective-permute-done.5 = bf16[224,2048]{1,0:T(8,128)(2,1)} collective-permute-done((bf16[224,2048]{1,0:T(8,128)(2,1)}, bf16[224,2048]{1,0:T(8,128)(2,1)}, u32[]{:S(2)}, u32[]{:S(2)}) %collective-permute-start.5) | collective-permute-done | bytes 917536 | tf_op jit(solution)/shard_map/ppermute | solution.py:586
  537.0 5.9 multiply_reduce_fusion.2
  544.4 53.7 %ffn_backward.3 = (f32[224,1024]{1,0:T(8,128)}, bf16[1024,1024]{1,0:T(8,128)(2,1)}, f32[512,1024]{1,0:T(8,128)}) custom-call(bf16[224,1024]{1,0:T(8,128)(2,1)} %get-tuple-element.102.grad, bf16[1024,1024]{1,0:T(8,128)(2,1)} %bitcast.180, bf16[512,1024]{1,0:T(8,128)(2,1)} %pad_maximum_fusion.2.down, f32[1792,1024]{1,0:T(8,128)} %get-tuple-element.30.pre, ...), custom_call_target="tpu_custom_call" | custom-call | tf_op jit(solution)/shard_map/ffn_backward/pallas_call | solution.py:357
  615.3 21.1 %collective-permute-done.6 = bf16[224,2048]{1,0:T(8,128)(2,1)S(1)} collective-permute-done((bf16[224,2048]{1,0:T(8,128)(2,1)S(1)}, bf16[224,2048]{1,0:T(8,128)(2,1)S(1)}, u32[]{:S(2)}, u32[]{:S(2)}) %collective-permute-start.6) | collective-permute-done | bytes 917536 | tf_op jit(solution)/shard_map/ppermute | solution.py:586
  638.4 5.3 multiply_reduce_fusion.3
  649.8 4.7 convolution_convert_fusion
  655.1 5.0 all-to-all-start.3
  667.3 36.8 %all-to-all-done.3 = bf16[16,64,1024]{2,1,0:T(8,128)(2,1)S(1)} async-done(((bf16[16,64,1024]{2,1,0:T(8,128)(2,1)}), bf16[16,64,1024]{2,1,0:T(8,128)(2,1)S(1)}, u32[]{:S(2)}, u32[]{:S(2)}) %all-to-all-start.3) | async-done | bytes 2097184 | tf_op jit(solution)/shard_map/all_to_all | solution.py:424
  704.1 11.7 %all-to-all-start.2 = ((bf16[16,64,1024]{2,1,0:T(8,128)(2,1)}), bf16[16,64,1024]{2,1,0:T(8,128)(2,1)}, u32[]{:S(2)}, u32[]{:S(2)}) async-start(bf16[16,64,1024]{2,1,0:T(8,128)(2,1)} %bitcast.187), calls=%async_computation.7 | async-start | bytes 4194304 | tf_op jit(solution)/shard_map/all_to_all | solution.py:424
  722.5 101.7 %collective-permute-done.8 = bf16[256,1024]{1,0:T(8,128)(2,1)S(1)} collective-permute-done((bf16[256,1024]{1,0:T(8,128)(2,1)S(1)}, bf16[256,1024]{1,0:T(8,128)(2,1)S(1)}, u32[]{:S(2)}, u32[]{:S(2)}) %collective-permute-start.8) | collective-permute-done | bytes 524320 | tf_op jit(solution)/shard_map/ppermute | solution.py:416
  824.5 10.4 %collective-permute-done.7 = bf16[256,1024]{1,0:T(8,128)(2,1)S(1)} collective-permute-done((bf16[256,1024]{1,0:T(8,128)(2,1)S(1)}, bf16[256,1024]{1,0:T(8,128)(2,1)S(1)}, u32[]{:S(2)}, u32[]{:S(2)}) %collective-permute-start.7) | collective-permute-done | bytes 524320 | tf_op jit(solution)/shard_map/ppermute | solution.py:416
  838.7 5.2 reshape.193
  843.9 5.7 reduce_sum.169
  857.1 6.8 reshape.191
  863.8 5.4 reduce_sum.168
  879.5 43.4 %reduce-scatter.10.cloned.1.call-done = bf16[64,3072]{1,0:T(8,128)(2,1)} async-done(((bf16[1024,3072]{1,0:T(8,128)(2,1)}), bf16[64,3072]{1,0:T(8,128)(2,1)}) %reduce-scatter.10.cloned.1.call-update) | async-done | bytes 393232 | tf_op jit(solution)/shard_map/reduce_scatter | solution.py:600
  924.0 89.0 %reduce-scatter.8.cloned.1.call-done = bf16[64,3200]{1,0:T(8,128)(2,1)} async-done(((bf16[1024,3200]{1,0:T(8,128)(2,1)}), bf16[64,3200]{1,0:T(8,128)(2,1)}) %reduce-scatter.8.cloned.1.call-update) | async-done | bytes 409616 | tf_op jit(solution)/shard_map/reduce_scatter | solution.py:600
  (299 shorter events, 149.9 us)
Async XLA Ops:
  7.2 105.5 %all-gather.12.cloned.1.call-start = ((), (), s32[]{:S(2)}) async-start(), calls=%async_computation.15 | async-start | bytes 4456448 | tf_op jit(solution)/shard_map/all_gather | solution.py:509
  7.9 183.6 %all-gather.10.cloned.1.call-start = ((), (), s32[]{:S(2)}) async-start(), calls=%async_computation.9 | async-start | bytes 6963200 | tf_op jit(solution)/shard_map/all_gather | solution.py:510
  11.6 222.1 %all-gather.14.cloned.1.call-start = ((), (), s32[]{:S(2)}) async-start(), calls=%async_computation.16 | async-start | bytes 2228224 | tf_op jit(solution)/shard_map/all_gather | solution.py:515
  12.4 350.4 %all-gather.16.cloned.1.call-start = ((), (), s32[]{:S(2)}) async-start(), calls=%async_computation.17 | async-start | bytes 6684672 | tf_op jit(solution)/shard_map/all_gather | solution.py:517
  13.5 23.1 %collective-permute-start = (s32[2,1]{0,1:T(1,128)}, s32[2,1]{0,1:T(1,128)S(1)}, u32[]{:S(2)}, u32[]{:S(2)}) collective-permute-start(s32[2,1]{0,1:T(1,128)} %slice.173), channel_id=1, source_target_pairs={{0,2},{2,4},{4,6},{6,8},{8,10},{10,12},{12,14},{14,16},{16,18},{18... | collective-permute-start | bytes 32 | tf_op jit(solution)/shard_map/ppermute | solution.py:488
  21.8 214.4 %all-to-all-start = ((bf16[16,64,1024]{2,1,0:T(8,128)(2,1)}), bf16[16,64,1024]{2,1,0:T(8,128)(2,1)S(1)}, u32[]{:S(2)}, u32[]{:S(2)}) async-start(bf16[16,64,1024]{2,1,0:T(8,128)(2,1)} %bitcast.183), calls=%async_computation | async-start | bytes 4194304 | tf_op jit(solution)/shard_map/all_to_all | solution.py:392
  29.0 364.7 %all-gather.18.cloned.1.call-start = ((), (), s32[]{:S(2)}) async-start(), calls=%async_computation.18 | async-start | bytes 2228224 | tf_op jit(solution)/shard_map/all_gather | solution.py:518
  31.4 176.6 %collective-permute-start.4 = (bf16[256,1024]{1,0:T(8,128)(2,1)}, bf16[256,1024]{1,0:T(8,128)(2,1)}, u32[]{:S(2)}, u32[]{:S(2)}) collective-permute-start(bf16[256,1024]{1,0:T(8,128)(2,1)} %get-tuple-element.124), channel_id=1, source_target_pairs={{0,16},{2,18},{4,20},{6,22},{8,24},{10,26},{12,28},{14,30},{16,0},... | collective-permute-start | bytes 1572872 | tf_op jit(solution)/shard_map/ppermute | solution.py:398
  34.2 173.7 %collective-permute-start.2 = (bf16[256,1024]{1,0:T(8,128)(2,1)}, bf16[256,1024]{1,0:T(8,128)(2,1)}, u32[]{:S(2)}, u32[]{:S(2)}) collective-permute-start(bf16[256,1024]{1,0:T(8,128)(2,1)} %get-tuple-element.125), channel_id=1, source_target_pairs={{0,16},{2,18},{4,20},{6,22},{8,24},{10,26},{12,28},{14,30},{16,0},... | collective-permute-start | bytes 1572872 | tf_op jit(solution)/shard_map/ppermute | solution.py:398
  36.6 79.6 %copy-start.65 = (pred[224]{0:T(512)(128)(4,1)}, pred[224]{0:T(512)(128)(4,1)S(1)}, u32[]{:S(2)}) copy-start(pred[224]{0:T(512)(128)(4,1)S(1)} %get-tuple-element.138) | copy-start | bytes 676
  36.7 79.5 %copy-start.62 = (s32[224,1]{0,1:T(1,128)}, s32[224,1]{0,1:T(1,128)S(1)}, u32[]{:S(2)}) copy-start(s32[224,1]{0,1:T(1,128)S(1)} %reshape_select_fusion) | copy-start | bytes 2692
  116.2 81.8 %copy-start.5 = (f32[224,1024]{1,0:T(8,128)}, f32[224,1024]{1,0:T(8,128)S(1)}, u32[]{:S(2)}) copy-start(f32[224,1024]{1,0:T(8,128)S(1)} %get-tuple-element.145) | copy-start | bytes 2752516
  199.4 23.7 %collective-permute-start.1 = (bf16[224,2048]{1,0:T(8,128)(2,1)}, bf16[224,2048]{1,0:T(8,128)(2,1)S(1)}, u32[]{:S(2)}, u32[]{:S(2)}) collective-permute-start(bf16[224,2048]{1,0:T(8,128)(2,1)} %slice.231), channel_id=1, source_target_pairs={{0,1},{2,3},{4,5},{6,7},{8,9},{10,11},{12,13},{14,15},{16,17},{18,... | collective-permute-start | bytes 2752520 | tf_op jit(solution)/shard_map/ppermute | solution.py:527
  239.8 157.3 %all-to-all-start.1 = ((bf16[16,64,1024]{2,1,0:T(8,128)(2,1)}), bf16[16,64,1024]{2,1,0:T(8,128)(2,1)}, u32[]{:S(2)}, u32[]{:S(2)}) async-start(bf16[16,64,1024]{2,1,0:T(8,128)(2,1)} %bitcast.184), calls=%async_computation.1 | async-start | bytes 4194304 | tf_op jit(solution)/shard_map/all_to_all | solution.py:392
  244.3 610.9 %reduce-scatter.14.cloned.1.call-start = ((), (), s32[]{:S(2)}) async-start(), calls=%async_computation.14 | async-start | bytes 2228224 | tf_op jit(solution)/shard_map/reduce_scatter | solution.py:590
  362.7 180.2 %copy-start.58 = (f32[224]{0:T(256)}, f32[224]{0:T(256)S(1)}, u32[]{:S(2)}) copy-start(f32[224]{0:T(256)S(1)} %add_rsqrt_fusion.1) | copy-start | bytes 2692
  367.3 20.2 %collective-permute-start.3 = (bf16[224,2048]{1,0:T(8,128)(2,1)S(1)}, bf16[224,2048]{1,0:T(8,128)(2,1)S(1)}, u32[]{:S(2)}, u32[]{:S(2)}) collective-permute-start(bf16[224,2048]{1,0:T(8,128)(2,1)S(1)} %slice.239), channel_id=1, source_target_pairs={{0,1},{2,3},{4,5},{6,7},{8,9},{10,11},{12,13},{14,15},{16,17},{18,... | collective-permute-start | bytes 2752520 | tf_op jit(solution)/shard_map/ppermute | solution.py:527
  509.6 24.3 %collective-permute-start.5 = (bf16[224,2048]{1,0:T(8,128)(2,1)}, bf16[224,2048]{1,0:T(8,128)(2,1)}, u32[]{:S(2)}, u32[]{:S(2)}) collective-permute-start(bf16[224,2048]{1,0:T(8,128)(2,1)} %pad_maximum_fusion.4), channel_id=1, source_target_pairs={{1,0},{3,2},{5,4},{7,6},{9,8},{11,10},{13,12},{15,14},{17,16},{19,... | collective-permute-start | bytes 2752520 | tf_op jit(solution)/shard_map/ppermute | solution.py:586
  513.0 342.2 %reduce-scatter.12.cloned.1.call-start = ((), (), s32[]{:S(2)}) async-start(), calls=%async_computation.13 | async-start | bytes 2228224 | tf_op jit(solution)/shard_map/reduce_scatter | solution.py:590
  609.7 268.0 %reduce-scatter.6.cloned.1.call-start = ((), (), s32[]{:S(2)}) async-start(), calls=%async_computation.10 | async-start | bytes 4456448 | tf_op jit(solution)/shard_map/reduce_scatter | solution.py:603
  613.5 24.8 %copy-start.44 = (bf16[224,1024]{1,0:T(8,128)(2,1)}, bf16[224,1024]{1,0:T(8,128)(2,1)S(1)}, u32[]{:S(2)}) copy-start(bf16[224,1024]{1,0:T(8,128)(2,1)S(1)} %get-tuple-element.106) | copy-start | bytes 1376260
  613.6 23.1 %copy-start.24 = (f32[224,1024]{1,0:T(8,128)S(1)}, f32[224,1024]{1,0:T(8,128)}, u32[]{:S(2)}) copy-start(f32[224,1024]{1,0:T(8,128)} %get-tuple-element.147) | copy-start | bytes 2752516
  613.6 23.1 %copy-start.35 = (bf16[224,1024]{1,0:T(8,128)(2,1)S(1)}, bf16[224,1024]{1,0:T(8,128)(2,1)}, u32[]{:S(2)}) copy-start(bf16[224,1024]{1,0:T(8,128)(2,1)} %copy-done.34) | copy-start | bytes 1376260
  613.7 22.8 %collective-permute-start.6 = (bf16[224,2048]{1,0:T(8,128)(2,1)S(1)}, bf16[224,2048]{1,0:T(8,128)(2,1)S(1)}, u32[]{:S(2)}, u32[]{:S(2)}) collective-permute-start(bf16[224,2048]{1,0:T(8,128)(2,1)S(1)} %pad_maximum_fusion.5), channel_id=1, source_target_pairs={{1,0},{3,2},{5,4},{7,6},{9,8},{11,10},{13,12},{15,14},{17,16},{19,... | collective-permute-start | bytes 2752520 | tf_op jit(solution)/shard_map/ppermute | solution.py:586
  648.5 274.5 %reduce-scatter.10.cloned.1.call-start = ((), (), s32[]{:S(2)}) async-start(), calls=%async_computation.12 | async-start | bytes 6684672 | tf_op jit(solution)/shard_map/reduce_scatter | solution.py:600
  655.1 48.9 %all-to-all-start.3 = ((bf16[16,64,1024]{2,1,0:T(8,128)(2,1)}), bf16[16,64,1024]{2,1,0:T(8,128)(2,1)S(1)}, u32[]{:S(2)}, u32[]{:S(2)}) async-start(bf16[16,64,1024]{2,1,0:T(8,128)(2,1)} %bitcast.186), calls=%async_computation.8 | async-start | bytes 4194304 | tf_op jit(solution)/shard_map/all_to_all | solution.py:424
  660.1 352.9 %reduce-scatter.8.cloned.1.call-start = ((), (), s32[]{:S(2)}) async-start(), calls=%async_computation.11 | async-start | bytes 6963200 | tf_op jit(solution)/shard_map/reduce_scatter | solution.py:600
  704.1 153.0 %all-to-all-start.2 = ((bf16[16,64,1024]{2,1,0:T(8,128)(2,1)}), bf16[16,64,1024]{2,1,0:T(8,128)(2,1)}, u32[]{:S(2)}, u32[]{:S(2)}) async-start(bf16[16,64,1024]{2,1,0:T(8,128)(2,1)} %bitcast.187), calls=%async_computation.7 | async-start | bytes 4194304 | tf_op jit(solution)/shard_map/all_to_all | solution.py:424
  715.8 108.4 %copy-start.14 = (f32[512,1024]{1,0:T(8,128)S(1)}, f32[512,1024]{1,0:T(8,128)}, u32[]{:S(2)}) copy-start(f32[512,1024]{1,0:T(8,128)} %get-tuple-element.37) | copy-start | bytes 6291460
  717.5 106.6 %collective-permute-start.8 = (bf16[256,1024]{1,0:T(8,128)(2,1)S(1)}, bf16[256,1024]{1,0:T(8,128)(2,1)S(1)}, u32[]{:S(2)}, u32[]{:S(2)}) collective-permute-start(bf16[256,1024]{1,0:T(8,128)(2,1)S(1)} %select_convert_fusion), channel_id=1, source_target_pairs={{0,16},{2,18},{4,20},{6,22},{8,24},{10,26},{12,28},{14,30},{16,0},... | collective-permute-start | bytes 1572872 | tf_op jit(solution)/shard_map/ppermute | solution.py:416
  722.2 112.8 %copy-start.15 = (f32[512,1024]{1,0:T(8,128)S(1)}, f32[512,1024]{1,0:T(8,128)}, u32[]{:S(2)}) copy-start(f32[512,1024]{1,0:T(8,128)} %get-tuple-element.36) | copy-start | bytes 6291460
  722.2 112.7 %collective-permute-start.7 = (bf16[256,1024]{1,0:T(8,128)(2,1)S(1)}, bf16[256,1024]{1,0:T(8,128)(2,1)S(1)}, u32[]{:S(2)}, u32[]{:S(2)}) collective-permute-start(bf16[256,1024]{1,0:T(8,128)(2,1)S(1)} %select_convert_fusion.1), channel_id=1, source_target_pairs={{0,16},{2,18},{4,20},{6,22},{8,24},{10,26},{12,28},{14,30},{16,0},... | collective-permute-start | bytes 1572872 | tf_op jit(solution)/shard_map/ppermute | solution.py:416
  (62 other events, 273.9 us)
Sparse Core Ops, SparseCore 0:
  10.2 102.4 all-gather.11
  115.5 75.9 all-gather.9
  193.7 39.9 all-gather.13
  235.8 94.0 all-gather.15
  332.0 46.6 all-gather.17
  513.2 66.7 reduce-scatter.13
  609.8 71.7 reduce-scatter.11
  685.5 127.1 reduce-scatter.5
  817.1 105.8 reduce-scatter.9
  926.8 86.1 reduce-scatter.7

commit v3 on v2

--- a/solution.py
+++ b/solution.py
@@ -173,7 +173,7 @@
         ]
         return copies
 
-    def run(self, compute, between, result):
+    def run(self, compute, between, result, later=None):
         half, rows = self.half, self.rows
         self.greet()
         gather = self.gather_copies()
@@ -218,6 +218,8 @@
 
             compute(m, self.pair_start(m))
             self.copy(9 + m, self.part.at[m], self.from_core.at[m], self.core_peer).start()
+            if later is not None:
+                later(m)
 
             @pl.when(m == 2)
             def _():
@@ -271,46 +273,54 @@
         part[m] = value[:rows].astype(BF)
 
 
-def ffn_forward_kernel(normed, both, down, everyone, pre, gated, result, sums, *scratch):
+def hidden_units(block, both, hidden, first):
+    gate = plain(block, both[:, first : first + 256])
+    return gate, plain(block, both[:, hidden + first : hidden + first + 256])
+
+
+def ffn_rows(block, both, down):
+    hidden = down.shape[0]
+    parts = []
+    for first in range(0, hidden, 256):
+        gate, up = hidden_units(block, both, hidden, first)
+        parts.append((gate * jax.nn.sigmoid(gate) * up).astype(BF))
+    return plain(jnp.concatenate(parts, axis=1), down[...])
+
+
+def ffn_forward_kernel(normed, both, down, everyone, result, sums, *scratch):
     rows = normed.shape[0]
+    team = Team(rows, normed, everyone, sums, scratch)
+
+    def compute(m, start):
+        block = everyone[pl.ds(start, 2 * rows), :]
+        split_pair(team, m, ffn_rows(block, both, down), sums, team.part)
+
+    team.run(compute, lambda: None, result)
+
+
+def ffn_back_rows(block, normed, both, down, gated, d_both, here):
     hidden = down.shape[0]
-    tile = min(hidden, 256)
-    team = Team(rows, normed, everyone, sums, scratch)
+    before = normed[here, :]
+    for first in range(0, hidden, 256):
+        columns = slice(first, first + 256)
+        gate, up = hidden_units(before, both, hidden, first)
+        d_gated = right_trans(block, down[columns, :])
+        sig = jax.nn.sigmoid(gate)
+        act = gate * sig
+        gated[here, columns] = (act * up).astype(BF)
+        d_both[here, columns] = (d_gated * up * sig * (1.0 + gate * (1.0 - sig))).astype(BF)
+        d_both[here, hidden + first : hidden + first + 256] = (d_gated * act).astype(BF)
+
+
+def ffn_backward_kernel(
+    grad, both, down, normed, result, both_part, down_part, everyone, gated, d_both, sums, *scratch
+):
+    rows = grad.shape[0]
+    team = Team(rows, grad, everyone, sums, scratch)
 
     def compute(m, start):
         here = pl.ds(start, 2 * rows)
-        block = everyone[here, :]
-        for first in range(0, hidden, tile):
-            g = plain(block, both[:, first : first + tile])
-            u = plain(block, both[:, hidden + first : hidden + first + tile])
-            pre[here, first : first + tile] = g
-            pre[here, hidden + first : hidden + first + tile] = u
-            gated[here, first : first + tile] = (g * jax.nn.sigmoid(g) * u).astype(BF)
-        split_pair(team, m, plain(gated[here, :], down[...]), sums, team.part)
-
-    team.run(compute, lambda: None, result)
-
-
-def ffn_backward_kernel(
-    grad, both, down, pre, gated, normed, result, both_part, down_part, everyone, d_both, sums, *scratch
-):
-    rows = grad.shape[0]
-    hidden = down.shape[0]
-    tile = min(hidden, 256)
-    team = Team(rows, grad, everyone, sums, scratch)
-
-    def compute(m, start):
-        here = pl.ds(start, 2 * rows)
-        block = everyone[here, :]
-        for first in range(0, hidden, tile):
-            d_gated = right_trans(block, down[first : first + tile, :])
-            g = pre[here, first : first + tile]
-            u = pre[here, hidden + first : hidden + first + tile]
-            sig = jax.nn.sigmoid(g)
-            d_both[here, first : first + tile] = (
-                d_gated * u * sig * (1.0 + g * (1.0 - sig))
-            ).astype(BF)
-            d_both[here, hidden + first : hidden + first + tile] = (d_gated * g * sig).astype(BF)
+        ffn_back_rows(everyone[here, :], normed, both, down, gated, d_both, here)
         split_pair(team, m, right_trans(d_both[here, :], both[...]), sums, team.part)
 
     def between():
@@ -332,17 +342,14 @@
 
 def ffn_forward(normed, both, down):
     rows, width = normed.shape
-    hidden = down.shape[0]
     return pl.pallas_call(
         ffn_forward_kernel,
         out_shape=(
             jax.ShapeDtypeStruct((8 * rows, width), BF),
-            jax.ShapeDtypeStruct((8 * rows, 2 * hidden), F32),
-            jax.ShapeDtypeStruct((8 * rows, hidden), BF),
             jax.ShapeDtypeStruct((rows, width), F32),
         ),
         in_specs=in_vmem(3),
-        out_specs=in_vmem(4),
+        out_specs=in_vmem(2),
         scratch_shapes=[pltpu.VMEM((4, rows, width), F32)] + Team.scratch(rows, width),
         compiler_params=pltpu.CompilerParams(
             collective_id=1, has_side_effects=True, vmem_limit_bytes=VMEM_LIMIT
@@ -351,7 +358,7 @@
     )(normed, both, down)
 
 
-def ffn_backward(grad, both, down, pre, gated, normed):
+def ffn_backward(grad, both, down, normed):
     rows, width = grad.shape
     hidden = down.shape[0]
     return pl.pallas_call(
@@ -361,10 +368,11 @@
             jax.ShapeDtypeStruct((width, 2 * hidden), BF),
             jax.ShapeDtypeStruct((hidden, width), F32),
         ),
-        in_specs=in_vmem(6),
+        in_specs=in_vmem(4),
         out_specs=in_vmem(3),
         scratch_shapes=[
             pltpu.VMEM((8 * rows, width), BF),
+            pltpu.VMEM((8 * rows, hidden), BF),
             pltpu.VMEM((8 * rows, 2 * hidden), BF),
             pltpu.VMEM((4, rows, width), F32),
         ]
@@ -373,7 +381,456 @@
             collective_id=2, has_side_effects=True, vmem_limit_bytes=VMEM_LIMIT
         ),
         name="ffn_backward",
-    )(grad, both, down, pre, gated, normed)
+    )(grad, both, down, normed)
+
+
+class Place:
+    def __init__(self):
+        self.index = lax.axis_index("frames")
+        self.place = lax.axis_index("pos")
+        self.core = lax.rem(self.index, 2)
+        self.x = lax.rem(self.index // 2, 2)
+        self.z = self.index // 4
+        self.core_peer = self.index + 1 - 2 * self.core
+        self.x_peer = self.index + 2 - 4 * self.x
+
+    def greet_all(self):
+        barrier = pltpu.get_barrier_semaphore()
+
+        def signal(step, carry):
+            peer = lax.rem(self.index + step, 16)
+            pl.semaphore_signal(barrier, inc=1, device_id=(peer, self.place), device_id_type=MESH)
+            return carry
+
+        lax.fori_loop(1, 16, signal, 0)
+        pl.semaphore_signal(
+            barrier, inc=1, device_id=(self.index, 1 - self.place), device_id_type=MESH
+        )
+        pl.semaphore_wait(barrier, 16)
+
+
+class Gather:
+    def __init__(self, where, number, source, full, sent, got):
+        self.where, self.source, self.full = where, source, full
+        self.sent, self.got = sent.at[number], got.at[number]
+        self.rows = source.shape[0]
+
+    def shard(self, z, x, core):
+        start = (z * 4 + x * 2 + core) * self.rows
+        return self.full.at[pl.ds(pl.multiple_of(start, self.rows), self.rows)]
+
+    def copy(self, source, target, sent, got, peer):
+        return pltpu.make_async_remote_copy(
+            src_ref=source,
+            dst_ref=target,
+            send_sem=self.sent.at[sent],
+            recv_sem=self.got.at[got],
+            device_id=(peer, self.where.place),
+            device_id_type=MESH,
+        )
+
+    def z_copy(self, z, up, own=False):
+        w = self.where
+        target = self.shard(z, w.x, w.core)
+        source = self.source if own else target
+        if up:
+            return self.copy(source, target, z, z, jnp.minimum(w.index + 4, 15))
+        return self.copy(source, target, 4 + z, z, jnp.maximum(w.index - 4, 0))
+
+    def x_copy(self, z, own=False):
+        w = self.where
+        target = self.shard(z, w.x, w.core)
+        return self.copy(self.source if own else target, target, 8 + z, 4 + z, w.x_peer)
+
+    def core_copy(self, z, other_x, own=False):
+        w = self.where
+        x = 1 - w.x if other_x else w.x
+        target = self.shard(z, x, w.core)
+        number = z * 2 + other_x
+        return self.copy(
+            self.source if own else target, target, 12 + number, 8 + number, w.core_peer
+        )
+
+    def local(self):
+        w = self.where
+        return pltpu.make_async_copy(
+            self.source, self.shard(w.z, w.x, w.core), self.got.at[w.z]
+        )
+
+    def start(self):
+        w = self.where
+        pl.when(w.z < 3)(lambda: self.z_copy(w.z, True, True).start())
+        pl.when(w.z > 0)(lambda: self.z_copy(w.z, False, True).start())
+        self.x_copy(w.z, True).start()
+        self.core_copy(w.z, 0, True).start()
+        self.local().start()
+
+    def pass_z(self, distance):
+        w = self.where
+
+        @pl.when(w.z >= distance)
+        def _():
+            z = w.z - distance
+            self.z_copy(z, True).wait_recv()
+            pl.when(w.z < 3)(lambda: self.z_copy(z, True).start())
+            self.x_copy(z).start()
+            self.core_copy(z, 0).start()
+
+        @pl.when(w.z + distance <= 3)
+        def _():
+            z = w.z + distance
+            self.z_copy(z, False).wait_recv()
+            pl.when(w.z > 0)(lambda: self.z_copy(z, False).start())
+            self.x_copy(z).start()
+            self.core_copy(z, 0).start()
+
+    def pass_x(self):
+        w = self.where
+
+        def hand(z):
+            target = self.shard(z, 1 - w.x, w.core)
+            self.copy(target, target, 8 + z, 4 + z, w.x_peer).wait_recv()
+            self.core_copy(z, 1).start()
+
+        hand(w.z)
+        for distance in (1, 2, 3):
+            pl.when(w.z >= distance)(lambda: hand(w.z - distance))
+            pl.when(w.z + distance <= 3)(lambda: hand(w.z + distance))
+
+    def finish(self):
+        w = self.where
+        for z in range(4):
+            for other_x in (0, 1):
+                x = 1 - w.x if other_x else w.x
+                target = self.shard(z, x, 1 - w.core)
+                number = z * 2 + other_x
+                self.copy(target, target, 12 + number, 8 + number, w.core_peer).wait_recv()
+        self.local().wait()
+
+    def drain(self):
+        w = self.where
+        for z in range(4):
+            pl.when((z <= w.z) & (w.z < 3))(lambda: self.z_copy(z, True).wait_send())
+            pl.when((z >= w.z) & (w.z > 0))(lambda: self.z_copy(z, False).wait_send())
+            self.x_copy(z).wait_send()
+            self.core_copy(z, 0).wait_send()
+            self.core_copy(z, 1).wait_send()
+
+    def all_steps(self):
+        for distance in (1, 2, 3):
+            self.pass_z(distance)
+        self.pass_x()
+
+
+class Slices:
+    def __init__(self, where, layer, gate, up, down, both, down_all, sent, got):
+        self.where, self.both, self.down_all = where, both.at[layer], down_all.at[layer]
+        self.gate, self.up, self.down = gate.at[layer], up.at[layer], down.at[layer]
+        self.sent, self.got = sent.at[layer], got.at[layer]
+        self.rows = self.gate.shape[0]
+        self.hidden = self.down_all.shape[0]
+
+    def piece(self, source, side, member):
+        here = pl.ds(pl.multiple_of(self.where.index * self.rows, self.rows), self.rows)
+        columns = pl.ds(pl.multiple_of(member * self.hidden, self.hidden), self.hidden)
+        return source.at[:, columns], self.both.at[
+            here, side * self.hidden : (side + 1) * self.hidden
+        ]
+
+    def remote(self, source, target, number, peer):
+        return pltpu.make_async_remote_copy(
+            src_ref=source,
+            dst_ref=target,
+            send_sem=self.sent.at[number],
+            recv_sem=self.got.at[number],
+            device_id=(peer, self.where.place),
+            device_id_type=MESH,
+        )
+
+    def down_target(self):
+        half = self.hidden // 2
+        start = lax.rem(self.where.index, 2) * half
+        return self.down_all.at[pl.ds(pl.multiple_of(start, half), half)]
+
+    def start(self):
+        index = self.where.index
+
+        def send(step, carry):
+            peer = lax.rem(index + step, 16)
+            for side, source in ((0, self.gate), (1, self.up)):
+                part, target = self.piece(source, side, lax.rem(peer, 8))
+                self.remote(part, target, 0, peer).start()
+            return carry
+
+        lax.fori_loop(1, 16, send, 0)
+        for side, source in ((0, self.gate), (1, self.up)):
+            part, target = self.piece(source, side, lax.rem(index, 8))
+            pltpu.make_async_copy(part, target, self.got.at[0]).start()
+        for team in (0, 1):
+            peer = team * 8 + index // 2
+
+            @pl.when(peer != index)
+            def _():
+                self.remote(self.down, self.down_target(), 1, peer).start()
+
+            @pl.when(peer == index)
+            def _():
+                pltpu.make_async_copy(self.down, self.down_target(), self.got.at[1]).start()
+
+    def finish(self):
+        pltpu.make_async_copy(self.both, self.both, self.got.at[0]).wait()
+        pltpu.make_async_copy(self.down_all, self.down_all, self.got.at[1]).wait()
+
+    def drain(self):
+        index = self.where.index
+        most = self.both.at[pl.ds(0, 15 * self.rows)]
+        pltpu.make_async_copy(most, most, self.sent.at[0]).wait()
+        ends = (index == 0) | (index == 15)
+        half = self.down_all.at[pl.ds(0, self.hidden // 2)]
+
+        @pl.when(ends)
+        def _():
+            pltpu.make_async_copy(half, half, self.sent.at[1]).wait()
+
+        @pl.when(jnp.logical_not(ends))
+        def _():
+            pltpu.make_async_copy(self.down_all, self.down_all, self.sent.at[1]).wait()
+
+
+def two_parts(values):
+    high = values.astype(BF)
+    return high, (values - high.astype(F32)).astype(BF)
+
+
+def heads_summed(values, heads):
+    high, low = two_parts(values)
+    return plain(high, heads[...]) + plain(low, heads[...])
+
+
+def heads_spread(values, heads):
+    high, low = two_parts(values)
+    return right_trans(high, heads[...]) + right_trans(low, heads[...])
+
+
+def fill_heads(heads):
+    rows = lax.broadcasted_iota(jnp.int32, heads.shape, 0) // HD
+    columns = lax.broadcasted_iota(jnp.int32, heads.shape, 1)
+    heads[...] = jnp.where(rows == columns, 1.0, 0.0).astype(BF)
+
+
+def probabilities(q, k, k0, heads, place):
+    own = heads_summed(q * k, heads) / math.sqrt(HD)
+    past = jnp.where(place > 0, heads_summed(q * k0, heads) / math.sqrt(HD), -1e30)
+    largest = jnp.maximum(own, past)
+    own, past = jnp.exp(own - largest), jnp.exp(past - largest)
+    total = own + past
+    return own / total, past / total
+
+
+def forward_kernel(
+    frames, onehot, gain_shard, table, qkv0, qkv1, out0, out1, gate, up, down, *refs
+):
+    (act, stream, middle, qkv, other, attended, everyone, gain_rows) = refs[:8]
+    (qkv0_out, qkv1_out, outs_out, both_out, down_out) = refs[8:13]
+    (gains, table_all, qkv0_all, qkv1_all, outs_all, both, down_all) = refs[13:20]
+    (heads, normed, result, sums, gather_sent, gather_got, slice_sent, slice_got) = refs[20:28]
+    (y_sent, y_got, saved) = refs[28:31]
+    team_scratch = refs[31:39]
+    team_sent, team_got = refs[39:41]
+    rows, width = frames.shape
+    where = Place()
+
+    def gather(number, source, full):
+        return Gather(where, number, source, full, gather_sent, gather_got)
+
+    gain_gather = gather(0, gain_shard, gains)
+    table_gather = gather(1, table, table_all)
+    qkv_gathers = [gather(2, qkv0, qkv0_all), gather(3, qkv1, qkv1_all)]
+    out_gathers = [gather(4, out0, outs_all.at[0]), gather(5, out1, outs_all.at[1])]
+    slices = [
+        Slices(where, layer, gate, up, down, both, down_all, slice_sent, slice_got)
+        for layer in range(LAYERS)
+    ]
+    where.greet_all()
+    for item in (gain_gather, table_gather, qkv_gathers[0], out_gathers[0]):
+        item.start()
+    slices[0].start()
+    fill_heads(heads)
+    gain_gather.all_steps()
+    table_gather.all_steps()
+    qkv_gathers[0].all_steps()
+    out_gathers[0].all_steps()
+    gain_gather.finish()
+    for block in range(8):
+        first, second = block * 16, block * 16 + 8
+        gain_rows[:, block * 128 : (block + 1) * 128] = (
+            gains[first : first + 8, :] + gains[second : second + 8, :]
+        )
+    table_gather.finish()
+    for first in range(0, width, 256):
+        columns = slice(first, first + 256)
+        stream[0, :, columns] = frames[:, columns].astype(F32) + plain(
+            onehot[...], table_all[:, columns]
+        )
+    saves = []
+
+    def save(source, target, number):
+        copy = pltpu.make_async_copy(source, target, saved.at[number])
+        copy.start()
+        saves.append(copy)
+
+    for layer in range(LAYERS):
+        value = stream[layer]
+        normed[...] = (value * inverse_rms(value) * gain_rows[layer : layer + 1, :]).astype(BF)
+        qkv_gathers[layer].finish()
+        weights = (qkv0_all, qkv1_all)[layer]
+        save(weights, (qkv0_out, qkv1_out)[layer], layer)
+        exchange = pltpu.make_async_remote_copy(
+            src_ref=qkv.at[layer, :, pl.ds(width, 2 * width)],
+            dst_ref=other.at[layer],
+            send_sem=y_sent.at[layer],
+            recv_sem=y_got.at[layer],
+            device_id=(where.index, 1 - where.place),
+            device_id_type=MESH,
+        )
+        for first in list(range(width, 3 * width, 512)) + list(range(0, width, 512)):
+            if first == 0:
+                exchange.start()
+            columns = slice(first, first + 512)
+            qkv[layer, :, columns] = plain(normed[...], weights[:, columns]).astype(BF)
+        exchange.wait_recv()
+        q = qkv[layer, :, :width].astype(F32)
+        k = qkv[layer, :, width : 2 * width].astype(F32)
+        k0 = other[layer, :, :width].astype(F32)
+        own, past = probabilities(q, k, k0, heads, where.place)
+        attended[layer] = (
+            heads_spread(own, heads) * qkv[layer, :, 2 * width :].astype(F32)
+            + heads_spread(past, heads) * other[layer, :, width:].astype(F32)
+        ).astype(BF)
+        out_gathers[layer].finish()
+        for first in range(0, width, 512):
+            columns = slice(first, first + 512)
+            middle[layer, :, columns] = stream[layer, :, columns] + plain(
+                attended[layer], outs_all[layer, :, columns]
+            )
+        value = middle[layer]
+        normed[...] = (value * inverse_rms(value) * gain_rows[2 + layer : 3 + layer, :]).astype(BF)
+        slices[layer].finish()
+        save(both.at[layer], both_out.at[layer], 2 + layer)
+        save(down_all.at[layer], down_out.at[layer], 4 + layer)
+        team = Team(
+            rows,
+            normed,
+            everyone.at[layer],
+            sums,
+            tuple(team_scratch) + (team_sent.at[layer], team_got.at[layer]),
+        )
+
+        def compute(m, start):
+            block = everyone[layer, pl.ds(start, 2 * rows), :]
+            rows_out = ffn_rows(block, both.at[layer], down_all.at[layer])
+            split_pair(team, m, rows_out, sums, team.part)
+
+        later = None
+        if layer == 0:
+            for item in (qkv_gathers[1], out_gathers[1]):
+                item.start()
+            slices[1].start()
+
+            def later(m):
+                for step in (1, 2, 3):
+
+                    @pl.when(m == step)
+                    def _():
+                        for item in (qkv_gathers[1], out_gathers[1]):
+                            item.pass_z(step)
+
+        def between():
+            if layer == 0:
+                for item in (qkv_gathers[1], out_gathers[1]):
+                    item.pass_x()
+
+        team.run(compute, lambda: None, result, later)
+        between()
+        if layer == 0:
+            stream[1] = middle[0] + result[...]
+        else:
+            act[...] = (middle[1] + result[...]).astype(BF)
+        exchange.wait_send()
+    save(outs_all, outs_out, 6)
+    for item in [gain_gather, table_gather] + qkv_gathers + out_gathers + slices:
+        item.drain()
+    for copy in saves:
+        copy.wait()
+
+
+def forward(frames, onehot, gain_shard, table, w_qkv, w_out, gate, up, down):
+    rows, width = frames.shape
+    hidden = gate.shape[2] // 8
+    vocab = table.shape[0] * 16
+    shape = jax.ShapeDtypeStruct
+    hbm = pl.BlockSpec(memory_space=pl.ANY)
+    return pl.pallas_call(
+        forward_kernel,
+        out_shape=(
+            shape((rows, width), BF),
+            shape((2, rows, width), F32),
+            shape((2, rows, width), F32),
+            shape((2, rows, 3 * width), BF),
+            shape((2, rows, 2 * width), BF),
+            shape((2, rows, width), BF),
+            shape((2, 8 * rows, width), BF),
+            shape((8, width), F32),
+            shape((width, 3 * width), BF),
+            shape((width, 3 * width), BF),
+            shape((2, width, width), BF),
+            shape((2, width, 2 * hidden), BF),
+            shape((2, hidden, width), BF),
+        ),
+        in_specs=in_vmem(2) + [hbm] * 9,
+        out_specs=tuple(in_vmem(8) + [hbm] * 5),
+        scratch_shapes=[
+            pltpu.VMEM((8 * 16, 128), F32),
+            pltpu.VMEM((vocab, width), BF),
+            pltpu.VMEM((width, 3 * width), BF),
+            pltpu.VMEM((width, 3 * width), BF),
+            pltpu.VMEM((2, width, width), BF),
+            pltpu.VMEM((2, width, 2 * hidden), BF),
+            pltpu.VMEM((2, hidden, width), BF),
+            pltpu.VMEM((width, 128), BF),
+            pltpu.VMEM((rows, width), BF),
+            pltpu.VMEM((rows, width), F32),
+            pltpu.VMEM((4, rows, width), F32),
+            pltpu.SemaphoreType.DMA((6, 20)),
+            pltpu.SemaphoreType.DMA((6, 16)),
+            pltpu.SemaphoreType.DMA((2, 2)),
+            pltpu.SemaphoreType.DMA((2, 2)),
+            pltpu.SemaphoreType.DMA((2,)),
+            pltpu.SemaphoreType.DMA((2,)),
+            pltpu.SemaphoreType.DMA((7,)),
+        ]
+        + Team.scratch(rows, width)[:8]
+        + [
+            pltpu.SemaphoreType.DMA((2, Team.SCRATCH_COPIES)),
+            pltpu.SemaphoreType.DMA((2, Team.SCRATCH_COPIES)),
+        ],
+        compiler_params=pltpu.CompilerParams(
+            collective_id=3, has_side_effects=True, vmem_limit_bytes=63 * 2**20
+        ),
+        name="forward_pass",
+    )(
+        frames,
+        onehot,
+        gain_shard,
+        table,
+        w_qkv[0],
+        w_qkv[1],
+        w_out[0],
+        w_out[1],
+        gate,
+        up,
+        down,
+    )
 
 
 class Plan:
@@ -419,11 +876,24 @@
         return [(i, (i + self.team) % self.count) for i in range(self.count)]
 
     def ffn_grads(self, both_part, down_part):
-        down = self.scatter_across(down_part)
         parts = both_part.astype(BF).reshape(self.count, -1, both_part.shape[1])
         parts = lax.all_to_all(parts, "frames", split_axis=0, concat_axis=0, tiled=True)
         rows = parts.shape[1]
-        parts = parts.astype(F32).reshape(self.teams, self.team, rows, 2, self.teams, -1).sum(axis=0)
+        parts = parts.astype(F32).reshape(self.teams, self.team, rows, -1).sum(axis=0)
+        if self.count == 16:
+            half = down_part.shape[0] // 2
+            first = lax.axis_index("frames") < 8
+            one, two = down_part[:half].astype(BF), down_part[half:].astype(BF)
+            straight = [(i, 2 * (i % 8) + i // 8) for i in range(16)]
+            crossed = [(i, 2 * (i % 8) + 1 - i // 8) for i in range(16)]
+            one, two = jnp.where(first, one, two), jnp.where(first, two, one)
+            down = lax.ppermute(one, "frames", straight).astype(F32)
+            down = down + lax.ppermute(two, "frames", crossed).astype(F32)
+            parts = parts.reshape(self.team, rows, 2, -1)
+            both = parts.transpose(1, 2, 0, 3).reshape(rows, 2, -1)
+            return both[:, 0], both[:, 1], down
+        down = self.scatter_across(down_part)
+        parts = parts.reshape(self.team, rows, 2, self.teams, -1)
         both = parts.transpose(1, 2, 3, 0, 4).reshape(rows, 2, -1)
         return both[:, 0], both[:, 1], down
 
@@ -458,6 +928,103 @@
     d_v = own * grad
     d_other = jnp.concatenate([s_past * q, past * grad], axis=1)
     return d_q, d_k, d_v, d_other
+
+
+def plain_forward(
+    plan, onward, frames_in, onehot, code_table, w_qkv, w_out, w_gate, w_up, w_down, gain_attn, gain_ffn
+):
+    width = frames_in.shape[-1]
+    gains = jnp.stack([gain_attn[0, 0], gain_attn[1, 0], gain_ffn[0, 0], gain_ffn[1, 0]], axis=1)
+    gains = jnp.pad(gains, ((0, 0), (0, 124)))
+    full_table = lax.all_gather(code_table[0], "frames", axis=0, tiled=True)
+    first_qkv = lax.all_gather(
+        jnp.concatenate([w_qkv[0, 0], gains], axis=1), "frames", axis=0, tiled=True
+    )
+    gain_rows = first_qkv[:, 3 * width : 3 * width + 4].astype(F32).T
+    qkv_all = [first_qkv[:, : 3 * width], None]
+    out_all = [lax.all_gather(w_out[0, 0], "frames", axis=0, tiled=True), None]
+    ffn_all = [plan.ffn_weights(w_gate[0, 0], w_up[0, 0], w_down[0, 0]), None]
+    qkv_all[1] = lax.all_gather(w_qkv[1, 0], "frames", axis=0, tiled=True)
+    out_all[1] = lax.all_gather(w_out[1, 0], "frames", axis=0, tiled=True)
+    ffn_all[1] = plan.ffn_weights(w_gate[1, 0], w_up[1, 0], w_down[1, 0])
+
+    stream = frames_in[:, 0].astype(F32) + plain(onehot, full_table)
+    kept = []
+    for layer in range(LAYERS):
+        inv_attn = inverse_rms(stream)
+        normed_attn = (stream * inv_attn * gain_rows[layer]).astype(BF)
+        qkv = plain(normed_attn, qkv_all[layer]).astype(BF)
+        other = lax.ppermute(qkv[:, width:], "pos", onward)
+        attended, own, past = attend(qkv, other)
+        middle = stream + plain(attended, out_all[layer])
+        inv_ffn = inverse_rms(middle)
+        normed_ffn = (middle * inv_ffn * gain_rows[2 + layer]).astype(BF)
+        both_all, down_all = ffn_all[layer]
+        team_normed, summed = ffn_forward(normed_ffn, both_all, down_all)
+        new_stream = middle + summed
+        kept.append(
+            (
+                stream,
+                inv_attn,
+                normed_attn,
+                qkv,
+                other,
+                own,
+                past,
+                attended,
+                middle,
+                inv_ffn,
+                team_normed,
+            )
+        )
+        stream = new_stream
+    return kept, stream, gain_rows, qkv_all, out_all, ffn_all
+
+
+def fused_forward(
+    frames_in, onehot, code_table, w_qkv, w_out, w_gate, w_up, w_down, gain_attn, gain_ffn
+):
+    share = gain_attn.shape[-1]
+    gains = jnp.concatenate([gain_attn[:, 0], gain_ffn[:, 0]], axis=0).astype(F32)
+    gains = jnp.pad(gains, ((0, 4), (0, share)))
+    odd = lax.rem(lax.axis_index("frames"), 2) == 1
+    gains = jnp.where(odd, jnp.roll(gains, share, axis=1), gains)
+    (act, stream, middle, qkv, other, attended, normed, gain_rows, qkv0, qkv1, outs, both, down) = (
+        forward(
+            frames_in[:, 0],
+            onehot,
+            gains,
+            code_table[0],
+            w_qkv[:, 0],
+            w_out[:, 0],
+            w_gate[:, 0],
+            w_up[:, 0],
+            w_down[:, 0],
+        )
+    )
+    kept = []
+    for layer in range(LAYERS):
+        inv_attn = inverse_rms(stream[layer])
+        normed_attn = (stream[layer] * inv_attn * gain_rows[layer]).astype(BF)
+        unused, own, past = attend(qkv[layer], other[layer])
+        inv_ffn = inverse_rms(middle[layer])
+        kept.append(
+            (
+                stream[layer],
+                inv_attn,
+                normed_attn,
+                qkv[layer],
+                other[layer],
+                own,
+                past,
+                attended[layer],
+                middle[layer],
+                inv_ffn,
+                normed[layer],
+            )
+        )
+    ffn_all = [(both[layer], down[layer]) for layer in range(LAYERS)]
+    return kept, act, gain_rows, [qkv0, qkv1], outs, ffn_all
 
 
 def body(
@@ -504,52 +1071,15 @@
     matches = code_rows[:, None] == jnp.arange(vocab_size, dtype=jnp.int32)[None, :]
     onehot = (matches & is_valid[:, None]).astype(BF)
 
-    gains = jnp.stack([gain_attn[0, 0], gain_attn[1, 0], gain_ffn[0, 0], gain_ffn[1, 0]], axis=1)
-    gains = jnp.pad(gains, ((0, 0), (0, 124)))
-    full_table = lax.all_gather(code_table[0], "frames", axis=0, tiled=True)
-    first_qkv = lax.all_gather(
-        jnp.concatenate([w_qkv[0, 0], gains], axis=1), "frames", axis=0, tiled=True
-    )
-    gain_rows = first_qkv[:, 3 * width : 3 * width + 4].astype(F32).T
-    qkv_all = [first_qkv[:, : 3 * width], None]
-    out_all = [lax.all_gather(w_out[0, 0], "frames", axis=0, tiled=True), None]
-    ffn_all = [plan.ffn_weights(w_gate[0, 0], w_up[0, 0], w_down[0, 0]), None]
-    qkv_all[1] = lax.all_gather(w_qkv[1, 0], "frames", axis=0, tiled=True)
-    out_all[1] = lax.all_gather(w_out[1, 0], "frames", axis=0, tiled=True)
-    ffn_all[1] = plan.ffn_weights(w_gate[1, 0], w_up[1, 0], w_down[1, 0])
-
-    stream = frames_in[:, 0].astype(F32) + plain(onehot, full_table)
-    kept = []
-    for layer in range(LAYERS):
-        inv_attn = inverse_rms(stream)
-        normed_attn = (stream * inv_attn * gain_rows[layer]).astype(BF)
-        qkv = plain(normed_attn, qkv_all[layer]).astype(BF)
-        other = lax.ppermute(qkv[:, width:], "pos", onward)
-        attended, own, past = attend(qkv, other)
-        middle = stream + plain(attended, out_all[layer])
-        inv_ffn = inverse_rms(middle)
-        normed_ffn = (middle * inv_ffn * gain_rows[2 + layer]).astype(BF)
-        both_all, down_all = ffn_all[layer]
-        team_normed, pre, gated, summed = ffn_forward(normed_ffn, both_all, down_all)
-        new_stream = middle + summed
-        kept.append(
-            (
-                stream,
-                inv_attn,
-                normed_attn,
-                qkv,
-                other,
-                own,
-                past,
-                attended,
-                middle,
-                inv_ffn,
-                team_normed,
-                pre,
-                gated,
-            )
-        )
-        stream = new_stream
+    if count == 16:
+        kept, stream, gain_rows, qkv_all, out_all, ffn_all = fused_forward(
+            frames_in, onehot, code_table, w_qkv, w_out, w_gate, w_up, w_down, gain_attn, gain_ffn
+        )
+    else:
+        kept, stream, gain_rows, qkv_all, out_all, ffn_all = plain_forward(
+            plan, onward, frames_in, onehot, code_table, w_qkv, w_out, w_gate, w_up, w_down,
+            gain_attn, gain_ffn,
+        )
     output = stream.astype(BF)[:, None, :]
 
     gradient = cotangent[:, 0].astype(F32)
@@ -568,12 +1098,10 @@
             middle,
             inv_ffn,
             team_normed,
-            pre,
-            gated,
         ) = kept[layer]
         both_all, down_all = ffn_all[layer]
         grad_normed, both_part, down_part = ffn_backward(
-            gradient.astype(BF), both_all, down_all, pre, gated, team_normed
+            gradient.astype(BF), both_all, down_all, team_normed
         )
         ffn_shares = plan.ffn_grads(both_part, down_part)
         grad_middle, gain_parts[2 + layer] = norm_back(

time: 1030 us -> 961 us (0.933)
  waiting for transfers between devices: 504 us -> 288 us
  Pallas kernels: 268 us -> 475 us
  other arithmetic: 58.7 us -> 36.5 us
  starting transfers between devices: 47.3 us -> 30.9 us
  matrix products: 72.6 us -> 58.4 us
    pallas_call x2 -> x1, Pallas kernels: 167 us -> 377 us  [forward(): pl.pallas_call(forward_kernel, out_shape=(shape((rows, width), BF), shape...]
    all_gather x5 -> x0, waiting for transfers between devices: 156 us -> none  [the longest x1 76 us: body(): full_table = lax.all_gather(code_table[0], 'frames', axis=0, tiled=True)]
    reduce_scatter x2, waiting for transfers between devices: 132 us -> 96.4 us  [body(): lax.psum_scatter(qkv_part, 'frames', scatter_dimension=0, tiled=True)]
    ppermute x6 -> x4, waiting for transfers between devices: 136 us -> 116 us  [the longest x2 116 us: ffn_grads(): down = down + lax.ppermute(two, 'frames', crossed).astype(F32)]
    dot_general x5 -> x0, matrix products: 17.4 us -> none  [plain(): return jnp.dot(left, right, preferred_element_type=F32)]
    squeeze x1 -> x7, local copies, waits for them, and re-layouts: 2.29 us -> 17.2 us  [the longest x1 7.14 us: fused_forward(): normed[layer]]
    all_to_all x2 -> x0, starting transfers between devices: 11.6 us -> none  [ffn_weights(): lax.all_to_all(parts, 'frames', split_axis=0, concat_axis=0, tiled=True)]
  transfers between devices with their start and end apart: 23 -> 14, of which waited for: 12 -> 7; matrix products, arithmetic and copies ran while one was open for 16% -> 11% of each run, Pallas kernels for 17% -> 5%
where the time goes in v3:
time: 961 us; the launch traced here: 951 us
  Pallas kernels  475 us (49%)
  waiting for transfers between devices  288 us (30%)
  matrix products  58.4 us (6%)
  local copies, waits for them, and re-layouts  46.8 us (5%)
  other arithmetic  36.5 us (4%)
  starting transfers between devices  30.9 us (3%)
  between operations  15.2 us (2%)
    pallas_call x1, Pallas kernels, forward(): pl.pallas_call(forward_kernel, out_shape=(shape((rows, width), BF), shape...  377 us
    ppermute x2, waiting for transfers between devices, ffn_grads(): down = down + lax.ppermute(two, 'frames', crossed).astype(F32)  116 us
    pallas_call x2, Pallas kernels, ffn_backward(): pl.pallas_call(ffn_backward_kernel, out_shape=(jax.ShapeDtypeStruct((rows...  98.1 us
    reduce_scatter x2, waiting for transfers between devices, body(): lax.psum_scatter(qkv_part, 'frames', scatter_dimension=0, tiled=True)  96.4 us
    all_to_all x2, waiting for transfers between devices, ffn_grads(): lax.all_to_all(parts, 'frames', split_axis=0, concat_axis=0, tiled=True)  38.4 us
    ppermute x2, waiting for transfers between devices, body(): arrived = lax.ppermute(d_other.astype(BF), 'pos', backward).astype(F32)  36.5 us
  transfers between devices with their start and end apart: 14, of which 7 were waited for; matrix products, arithmetic and copies ran while one was open for 11% of the time, Pallas kernels for 5%

profile of v3, /device:TPU:0, one launch (start us, length us, event | category | flops | bytes accessed | tf_op | source)
XLA Modules:
  0.0 950.7 jit_solution(8911740766267839837)
XLA Ops:
  8.0 2.3 collective-permute-start
  17.9 377.2 %forward_pass.1 = (bf16[224,1024]{1,0:T(8,128)(2,1)}, f32[2,224,1024]{2,1,0:T(8,128)}, f32[2,224,1024]{2,1,0:T(8,128)}, bf16[2,224,3072]{2,1,0:T(8,128)(2,1)}, b...) custom-call(bf16[224,1024]{1,0:T(8,128)(2,1)} %bitcast.228, ...), custom_call_target="tpu_custom_call" | custom-call | tf_op jit(solution)/shard_map/forward_pass/pallas_call | solution.py:773
  395.1 7.1 slice_bitcast_fusion
  402.2 2.5 slice_bitcast_fusion.2
  407.1 47.1 %ffn_backward.2 = (f32[224,1024]{1,0:T(8,128)}, bf16[1024,1024]{1,0:T(8,128)(2,1)}, f32[512,1024]{1,0:T(8,128)}) custom-call(bf16[224,1024]{1,0:T(8,128)(2,1)} %bitcast.224, bf16[1024,1024]{1,0:T(8,128)(2,1)} %get-tuple-element.115.both, bf16[512,1024]{1,0:T(8,128)(2,1)} %get-tuple-element.127.down, bf16[1792,1024]{1,0:T(8,128)(2,1)} %get-tuple-element.113.normed), custom_call_target="tpu_custom_call" | custom-call | tf_op jit(solution)/shard_map/ffn_backward/pallas_call | solution.py:364
  470.2 2.8 fusion.22
  478.8 2.8 convolution_multiply_fusion.1
  483.8 15.4 %collective-permute-done.1 = bf16[224,2048]{1,0:T(8,128)(2,1)} collective-permute-done((bf16[224,2048]{1,0:T(8,128)(2,1)}, bf16[224,2048]{1,0:T(8,128)(2,1)}, u32[]{:S(2)}, u32[]{:S(2)}) %collective-permute-start.1) | collective-permute-done | bytes 917536 | tf_op jit(solution)/shard_map/ppermute | solution.py:1114
  503.9 5.5 fusion.53
  510.9 51.0 %ffn_backward.3 = (f32[224,1024]{1,0:T(8,128)}, bf16[1024,1024]{1,0:T(8,128)(2,1)}, f32[512,1024]{1,0:T(8,128)}) custom-call(bf16[224,1024]{1,0:T(8,128)(2,1)} %get-tuple-element.110.grad, bf16[1024,1024]{1,0:T(8,128)(2,1)} %get-tuple-element.114.both, bf16[512,1024]{1,0:T(8,128)(2,1)} %get-tuple-element.126.down, bf16[1792,1024]{1,0:T(8,128)(2,1)} %get-tuple-element.112.normed), custom_call_target="tpu_custom_call" | custom-call | tf_op jit(solution)/shard_map/ffn_backward/pallas_call | solution.py:364
  563.9 2.8 fusion.16
  569.0 2.5 fusion.12
  574.7 2.8 fusion.24
  580.1 21.1 %collective-permute-done.2 = bf16[224,2048]{1,0:T(8,128)(2,1)S(1)} collective-permute-done((bf16[224,2048]{1,0:T(8,128)(2,1)S(1)}, bf16[224,2048]{1,0:T(8,128)(2,1)S(1)}, u32[]{:S(2)}, u32[]{:S(2)}) %collective-permute-start.2) | collective-permute-done | bytes 917536 | tf_op jit(solution)/shard_map/ppermute | solution.py:1114
  603.6 5.2 fusion.40
  609.2 3.4 convolution_convert_fusion.2
  613.6 5.7 convolution_convert_fusion
  619.3 4.6 all-to-all-start.1
  624.3 3.6 convolution_convert_fusion.1
  627.9 3.1 fusion.1
  631.0 38.4 %all-to-all-done.1 = bf16[16,64,1024]{2,1,0:T(8,128)(2,1)S(1)} async-done(((bf16[16,64,1024]{2,1,0:T(8,128)(2,1)}), bf16[16,64,1024]{2,1,0:T(8,128)(2,1)S(1)}, u32[]{:S(2)}, u32[]{:S(2)}) %all-to-all-start.1) | async-done | bytes 2097184 | tf_op jit(solution)/shard_map/all_to_all | solution.py:880
  669.4 11.3 %all-to-all-start = ((bf16[16,64,1024]{2,1,0:T(8,128)(2,1)}), bf16[16,64,1024]{2,1,0:T(8,128)(2,1)}, u32[]{:S(2)}, u32[]{:S(2)}) async-start(bf16[16,64,1024]{2,1,0:T(8,128)(2,1)} %bitcast.223), calls=%async_computation.5 | async-start | bytes 4194304 | tf_op jit(solution)/shard_map/all_to_all | solution.py:880
  683.5 3.3 collective-permute-start.6
  687.7 4.8 collective-permute-start.4
  692.5 85.5 %collective-permute-done.6 = bf16[256,1024]{1,0:T(8,128)(2,1)S(1)} collective-permute-done((bf16[256,1024]{1,0:T(8,128)(2,1)S(1)}, bf16[256,1024]{1,0:T(8,128)(2,1)S(1)}, u32[]{:S(2)}, u32[]{:S(2)}) %collective-permute-start.6) | collective-permute-done | bytes 524320 | tf_op jit(solution)/shard_map/ppermute | solution.py:891
  778.1 30.8 %collective-permute-done.4 = bf16[256,1024]{1,0:T(8,128)(2,1)S(1)} collective-permute-done((bf16[256,1024]{1,0:T(8,128)(2,1)S(1)}, bf16[256,1024]{1,0:T(8,128)(2,1)S(1)}, u32[]{:S(2)}, u32[]{:S(2)}) %collective-permute-start.4) | collective-permute-done | bytes 524320 | tf_op jit(solution)/shard_map/ppermute | solution.py:891
  814.3 3.1 reshape.170
  817.4 2.6 copy.74
  827.0 2.8 reshape.165
  829.8 4.1 copy.73
  841.7 7.6 reduce-scatter.10.cloned.1.call-done
  850.3 88.8 %reduce-scatter.8.cloned.1.call-done = bf16[64,3200]{1,0:T(8,128)(2,1)} async-done(((bf16[1024,3200]{1,0:T(8,128)(2,1)}), bf16[64,3200]{1,0:T(8,128)(2,1)}) %reduce-scatter.8.cloned.1.call-update) | async-done | bytes 409616 | tf_op jit(solution)/shard_map/reduce_scatter | solution.py:1128
  (192 shorter events, 84.0 us)
Async XLA Ops:
  7.2 9.3 copy-start.38
  7.2 8.5 copy-start.39
  7.2 8.6 copy-start.37
  7.2 8.6 copy-start.36
  7.2 815.7 %reduce-scatter.14.cloned.1.call-start = ((), (), s32[]{:S(2)}) async-start(), calls=%async_computation.11 | async-start | bytes 2228224 | tf_op jit(solution)/shard_map/reduce_scatter | solution.py:1118
  8.0 8.5 collective-permute-start
  395.1 7.1 copy-start.3
  458.9 11.2 %copy-start.8 = (bf16[224,3072]{1,0:T(8,128)(2,1)}, bf16[224,3072]{1,0:T(8,128)(2,1)S(1)}, u32[]{:S(2)}) copy-start(bf16[224,3072]{1,0:T(8,128)(2,1)S(1)} %get-tuple-element.117) | copy-start | bytes 4128772
  474.0 25.2 %collective-permute-start.1 = (bf16[224,2048]{1,0:T(8,128)(2,1)}, bf16[224,2048]{1,0:T(8,128)(2,1)}, u32[]{:S(2)}, u32[]{:S(2)}) collective-permute-start(bf16[224,2048]{1,0:T(8,128)(2,1)} %pad_maximum_fusion.2), channel_id=1, source_target_pairs={{1,0},{3,2},{5,4},{7,6},{9,8},{11,10},{13,12},{15,14},{17,16},{19,... | collective-permute-start | bytes 2752520 | tf_op jit(solution)/shard_map/ppermute | solution.py:1114
  477.4 345.5 %reduce-scatter.12.cloned.1.call-start = ((), (), s32[]{:S(2)}) async-start(), calls=%async_computation.10 | async-start | bytes 2228224 | tf_op jit(solution)/shard_map/reduce_scatter | solution.py:1118
  483.8 18.6 %copy-start.12 = (f32[224,1024]{1,0:T(8,128)S(1)}, f32[224,1024]{1,0:T(8,128)}, u32[]{:S(2)}) copy-start(f32[224,1024]{1,0:T(8,128)} %get-tuple-element.146) | copy-start | bytes 2752516
  502.4 7.0 copy-start.26
  503.9 5.5 copy-start.32
  563.9 8.6 copy-start.1
  566.7 5.8 copy-start.29
  566.7 5.8 copy-start.23
  577.5 262.4 %reduce-scatter.6.cloned.1.call-start = ((), (), s32[]{:S(2)}) async-start(), calls=%async_computation.7 | async-start | bytes 4456448 | tf_op jit(solution)/shard_map/reduce_scatter | solution.py:1131
  578.6 22.8 %copy-start.30 = (bf16[224,1024]{1,0:T(8,128)(2,1)S(1)}, bf16[224,1024]{1,0:T(8,128)(2,1)}, u32[]{:S(2)}) copy-start(bf16[224,1024]{1,0:T(8,128)(2,1)} %copy-done.29) | copy-start | bytes 1376260
  578.7 22.5 %collective-permute-start.2 = (bf16[224,2048]{1,0:T(8,128)(2,1)S(1)}, bf16[224,2048]{1,0:T(8,128)(2,1)S(1)}, u32[]{:S(2)}, u32[]{:S(2)}) collective-permute-start(bf16[224,2048]{1,0:T(8,128)(2,1)S(1)} %pad_maximum_fusion.3), channel_id=1, source_target_pairs={{1,0},{3,2},{5,4},{7,6},{9,8},{11,10},{13,12},{15,14},{17,16},{19,... | collective-permute-start | bytes 2752520 | tf_op jit(solution)/shard_map/ppermute | solution.py:1114
  580.1 23.2 %copy-start.13 = (f32[224,1024]{1,0:T(8,128)S(1)}, f32[224,1024]{1,0:T(8,128)}, u32[]{:S(2)}) copy-start(f32[224,1024]{1,0:T(8,128)} %get-tuple-element.148) | copy-start | bytes 2752516
  603.3 5.5 copy-start.28
  603.5 5.3 copy-start.34
  603.6 5.3 copy-start.2
  612.6 236.7 %reduce-scatter.10.cloned.1.call-start = ((), (), s32[]{:S(2)}) async-start(), calls=%async_computation.9 | async-start | bytes 6684672 | tf_op jit(solution)/shard_map/reduce_scatter | solution.py:1128
  619.3 50.1 %all-to-all-start.1 = ((bf16[16,64,1024]{2,1,0:T(8,128)(2,1)}), bf16[16,64,1024]{2,1,0:T(8,128)(2,1)S(1)}, u32[]{:S(2)}, u32[]{:S(2)}) async-start(bf16[16,64,1024]{2,1,0:T(8,128)(2,1)} %bitcast.222), calls=%async_computation.6 | async-start | bytes 4194304 | tf_op jit(solution)/shard_map/all_to_all | solution.py:880
  624.0 315.2 %reduce-scatter.8.cloned.1.call-start = ((), (), s32[]{:S(2)}) async-start(), calls=%async_computation.8 | async-start | bytes 6963200 | tf_op jit(solution)/shard_map/reduce_scatter | solution.py:1128
  669.4 155.3 %all-to-all-start = ((bf16[16,64,1024]{2,1,0:T(8,128)(2,1)}), bf16[16,64,1024]{2,1,0:T(8,128)(2,1)}, u32[]{:S(2)}, u32[]{:S(2)}) async-start(bf16[16,64,1024]{2,1,0:T(8,128)(2,1)} %bitcast.223), calls=%async_computation.5 | async-start | bytes 4194304 | tf_op jit(solution)/shard_map/all_to_all | solution.py:880
  680.8 6.0 copy-start.15
  682.8 9.7 %collective-permute-start.5 = (bf16[256,1024]{1,0:T(8,128)(2,1)S(1)}, bf16[256,1024]{1,0:T(8,128)(2,1)S(1)}, u32[]{:S(2)}, u32[]{:S(2)}) collective-permute-start(bf16[256,1024]{1,0:T(8,128)(2,1)S(1)} %get-tuple-element.132), channel_id=1, source_target_pairs={{0,0},{2,4},{4,8},{6,12},{8,16},{10,20},{12,24},{14,28},{16,2},{18... | collective-permute-start | bytes 1572872 | tf_op jit(solution)/shard_map/ppermute | solution.py:890
  683.5 94.5 %collective-permute-start.6 = (bf16[256,1024]{1,0:T(8,128)(2,1)S(1)}, bf16[256,1024]{1,0:T(8,128)(2,1)S(1)}, u32[]{:S(2)}, u32[]{:S(2)}) collective-permute-start(bf16[256,1024]{1,0:T(8,128)(2,1)S(1)} %get-tuple-element.133), channel_id=1, source_target_pairs={{0,2},{2,6},{4,10},{6,14},{8,18},{10,22},{12,26},{14,30},{16,0},{1... | collective-permute-start | bytes 1572872 | tf_op jit(solution)/shard_map/ppermute | solution.py:891
  687.0 91.2 %collective-permute-start.3 = (bf16[256,1024]{1,0:T(8,128)(2,1)S(1)}, bf16[256,1024]{1,0:T(8,128)(2,1)S(1)}, u32[]{:S(2)}, u32[]{:S(2)}) collective-permute-start(bf16[256,1024]{1,0:T(8,128)(2,1)S(1)} %get-tuple-element.130), channel_id=1, source_target_pairs={{0,0},{2,4},{4,8},{6,12},{8,16},{10,20},{12,24},{14,28},{16,2},{18... | collective-permute-start | bytes 1572872 | tf_op jit(solution)/shard_map/ppermute | solution.py:890
  687.7 121.3 %collective-permute-start.4 = (bf16[256,1024]{1,0:T(8,128)(2,1)S(1)}, bf16[256,1024]{1,0:T(8,128)(2,1)S(1)}, u32[]{:S(2)}, u32[]{:S(2)}) collective-permute-start(bf16[256,1024]{1,0:T(8,128)(2,1)S(1)} %get-tuple-element.131), channel_id=1, source_target_pairs={{0,2},{2,6},{4,10},{6,14},{8,18},{10,22},{12,26},{14,30},{16,0},{1... | collective-permute-start | bytes 1572872 | tf_op jit(solution)/shard_map/ppermute | solution.py:891
  (23 other events, 55.0 us)
Sparse Core Ops, SparseCore 0:
  477.5 68.1 reduce-scatter.13
  577.6 69.3 reduce-scatter.11
  650.9 108.1 reduce-scatter.5
  763.4 85.8 reduce-scatter.9
  853.1 86.0 reduce-scatter.7

commit v4 on v3

--- a/solution.py
+++ b/solution.py
@@ -173,15 +173,16 @@
         ]
         return copies
 
-    def run(self, compute, between, result, later=None):
+    def run(self, compute, between, result, later=None, early=None):
         half, rows = self.half, self.rows
-        self.greet()
         gather = self.gather_copies()
         adds = self.sum_copies()
         for copy in gather[:3]:
             copy.start()
         start = self.pair_start(0) + self.core * rows
         self.everyone[pl.ds(pl.multiple_of(start, 16), rows), :] = self.mine[...]
+        if early is not None:
+            early()
 
         def total(m, first):
             return self.sums[m, first : first + half, :] + self.from_core[
@@ -239,6 +240,8 @@
         self.to_z[half:, :] = total(2, half).astype(BF)
         adds[8].start()
         between()
+        for copy in gather:
+            copy.wait_send()
         adds[5].wait_recv()
         self.to_x[half:, :] = (total(1, half) + self.from_across[1].astype(F32)).astype(BF)
         adds[7].start()
@@ -255,22 +258,18 @@
                 + self.from_x[rows_here, :].astype(F32)
                 + self.from_z[rows_here, :].astype(F32)
             )
-        for copy in gather + adds:
+        for copy in adds:
             copy.wait_send()
 
 
-def split_pair(team, m, value, sums, part):
+def split_pair(team, m, product, sums, part):
     rows = team.rows
-
-    @pl.when(team.core == 0)
-    def _():
-        sums[m] = value[:rows]
-        part[m] = value[rows:].astype(BF)
-
-    @pl.when(team.core == 1)
-    def _():
-        sums[m] = value[rows:]
-        part[m] = value[:rows].astype(BF)
+    for first in range(0, sums.shape[2], 256):
+        columns = slice(first, first + 256)
+        value = product(columns)
+        low, high = value[:rows], value[rows:]
+        sums[m, :, columns] = jnp.where(team.core == 0, low, high)
+        part[m, :, columns] = jnp.where(team.core == 0, high, low).astype(BF)
 
 
 def hidden_units(block, both, hidden, first):
@@ -284,12 +283,14 @@
     for first in range(0, hidden, 256):
         gate, up = hidden_units(block, both, hidden, first)
         parts.append((gate * jax.nn.sigmoid(gate) * up).astype(BF))
-    return plain(jnp.concatenate(parts, axis=1), down[...])
+    gated = jnp.concatenate(parts, axis=1)
+    return lambda columns: plain(gated, down[:, columns])
 
 
 def ffn_forward_kernel(normed, both, down, everyone, result, sums, *scratch):
     rows = normed.shape[0]
     team = Team(rows, normed, everyone, sums, scratch)
+    team.greet()
 
     def compute(m, start):
         block = everyone[pl.ds(start, 2 * rows), :]
@@ -317,11 +318,12 @@
 ):
     rows = grad.shape[0]
     team = Team(rows, grad, everyone, sums, scratch)
+    team.greet()
 
     def compute(m, start):
         here = pl.ds(start, 2 * rows)
         ffn_back_rows(everyone[here, :], normed, both, down, gated, d_both, here)
-        split_pair(team, m, right_trans(d_both[here, :], both[...]), sums, team.part)
+        split_pair(team, m, lambda c: right_trans(d_both[here, :], both[c, :]), sums, team.part)
 
     def between():
         def down_step(i, carry):
@@ -516,11 +518,6 @@
             self.core_copy(z, 0).wait_send()
             self.core_copy(z, 1).wait_send()
 
-    def all_steps(self):
-        for distance in (1, 2, 3):
-            self.pass_z(distance)
-        self.pass_x()
-
 
 class Slices:
     def __init__(self, where, layer, gate, up, down, both, down_all, sent, got):
@@ -554,15 +551,16 @@
 
     def start(self):
         index = self.where.index
+        base = index - lax.rem(index, 8)
 
         def send(step, carry):
-            peer = lax.rem(index + step, 16)
+            member = lax.rem(index + step, 8)
             for side, source in ((0, self.gate), (1, self.up)):
-                part, target = self.piece(source, side, lax.rem(peer, 8))
-                self.remote(part, target, 0, peer).start()
+                part, target = self.piece(source, side, member)
+                self.remote(part, target, 0, base + member).start()
             return carry
 
-        lax.fori_loop(1, 16, send, 0)
+        lax.fori_loop(1, 8, send, 0)
         for side, source in ((0, self.gate), (1, self.up)):
             part, target = self.piece(source, side, lax.rem(index, 8))
             pltpu.make_async_copy(part, target, self.got.at[0]).start()
@@ -577,14 +575,29 @@
             def _():
                 pltpu.make_async_copy(self.down, self.down_target(), self.got.at[1]).start()
 
+    def team_rows(self, team):
+        size = 8 * self.rows
+        return self.both.at[pl.ds(pl.multiple_of(team * size, size), size)]
+
+    def swap(self):
+        mine = self.team_rows(self.where.index // 8)
+        return self.remote(mine, mine, 2, lax.rem(self.where.index + 8, 16))
+
+    def pass_on(self):
+        mine = self.team_rows(self.where.index // 8)
+        pltpu.make_async_copy(mine, mine, self.got.at[0]).wait()
+        self.swap().start()
+
     def finish(self):
-        pltpu.make_async_copy(self.both, self.both, self.got.at[0]).wait()
+        theirs = self.team_rows(1 - self.where.index // 8)
+        pltpu.make_async_copy(theirs, theirs, self.got.at[2]).wait()
         pltpu.make_async_copy(self.down_all, self.down_all, self.got.at[1]).wait()
 
     def drain(self):
         index = self.where.index
-        most = self.both.at[pl.ds(0, 15 * self.rows)]
+        most = self.both.at[pl.ds(0, 7 * self.rows)]
         pltpu.make_async_copy(most, most, self.sent.at[0]).wait()
+        self.swap().wait_send()
         ends = (index == 0) | (index == 15)
         half = self.down_all.at[pl.ds(0, self.hidden // 2)]
 
@@ -656,10 +669,13 @@
         item.start()
     slices[0].start()
     fill_heads(heads)
-    gain_gather.all_steps()
-    table_gather.all_steps()
-    qkv_gathers[0].all_steps()
-    out_gathers[0].all_steps()
+    first = (gain_gather, table_gather, qkv_gathers[0], out_gathers[0])
+    for item in first:
+        for distance in (1, 2, 3):
+            item.pass_z(distance)
+    slices[0].pass_on()
+    for item in first:
+        item.pass_x()
     gain_gather.finish()
     for block in range(8):
         first, second = block * 16, block * 16 + 8
@@ -673,6 +689,7 @@
             onehot[...], table_all[:, columns]
         )
     saves = []
+    second = (qkv_gathers[1], out_gathers[1])
 
     def save(source, target, number):
         copy = pltpu.make_async_copy(source, target, saved.at[number])
@@ -684,6 +701,9 @@
         normed[...] = (value * inverse_rms(value) * gain_rows[layer : layer + 1, :]).astype(BF)
         qkv_gathers[layer].finish()
         weights = (qkv0_all, qkv1_all)[layer]
+        if layer == 0:
+            for item in second:
+                item.start()
         save(weights, (qkv0_out, qkv1_out)[layer], layer)
         exchange = pltpu.make_async_remote_copy(
             src_ref=qkv.at[layer, :, pl.ds(width, 2 * width)],
@@ -698,6 +718,8 @@
                 exchange.start()
             columns = slice(first, first + 512)
             qkv[layer, :, columns] = plain(normed[...], weights[:, columns]).astype(BF)
+        if layer == 0:
+            slices[1].start()
         exchange.wait_recv()
         q = qkv[layer, :, :width].astype(F32)
         k = qkv[layer, :, width : 2 * width].astype(F32)
@@ -715,6 +737,9 @@
             )
         value = middle[layer]
         normed[...] = (value * inverse_rms(value) * gain_rows[2 + layer : 3 + layer, :]).astype(BF)
+        if layer == 0:
+            for item in second:
+                item.pass_z(1)
         slices[layer].finish()
         save(both.at[layer], both_out.at[layer], 2 + layer)
         save(down_all.at[layer], down_out.at[layer], 4 + layer)
@@ -733,21 +758,19 @@
 
         later = None
         if layer == 0:
-            for item in (qkv_gathers[1], out_gathers[1]):
-                item.start()
-            slices[1].start()
 
             def later(m):
-                for step in (1, 2, 3):
+                pl.when(m == 1)(lambda: slices[1].pass_on())
+                for step in (2, 3):
 
                     @pl.when(m == step)
                     def _():
-                        for item in (qkv_gathers[1], out_gathers[1]):
+                        for item in second:
                             item.pass_z(step)
 
         def between():
             if layer == 0:
-                for item in (qkv_gathers[1], out_gathers[1]):
+                for item in second:
                     item.pass_x()
 
         team.run(compute, lambda: None, result, later)
@@ -803,8 +826,8 @@
             pltpu.VMEM((4, rows, width), F32),
             pltpu.SemaphoreType.DMA((6, 20)),
             pltpu.SemaphoreType.DMA((6, 16)),
-            pltpu.SemaphoreType.DMA((2, 2)),
-            pltpu.SemaphoreType.DMA((2, 2)),
+            pltpu.SemaphoreType.DMA((2, 3)),
+            pltpu.SemaphoreType.DMA((2, 3)),
             pltpu.SemaphoreType.DMA((2,)),
             pltpu.SemaphoreType.DMA((2,)),
             pltpu.SemaphoreType.DMA((7,)),
@@ -833,6 +856,600 @@
     )
 
 
+def own_half(values, core, other):
+    rows, width = values.shape
+    parts = []
+    for first in range(0, width, 256):
+        low, high = values[:, first : first + 128], values[:, first + 128 : first + 256]
+        lane = lax.broadcasted_iota(jnp.int32, low.shape, 1)
+        even = jnp.where(lane < 64, low, pltpu.roll(high, 64, 1))
+        odd = jnp.where(lane < 64, pltpu.roll(low, 64, 1), high)
+        first_core = (core == 0) != other
+        parts.append(jnp.where(first_core, even, odd))
+    return jnp.concatenate(parts, axis=1)
+
+
+def backward_kernel(
+    cotangent, codes, codes_theirs, gain_rows, stream, middle, qkv, other, attended, normed, qkv0,
+    qkv1, outs, both, down, *refs
+):
+    (input_grad, both_got, pair_got, down_got, attn_got, table_got, gain_got) = refs[:7]
+    refs = refs[1:]
+    (v_stream, v_middle, v_qkv, v_other, v_attended, v_normed, w_qkv, w_out, w_both, w_down) = refs[
+        6:16
+    ]
+    (grad, d_middle, rounded, normed2, attended2, d_qkv2, d_middle2, for_core, d_other, y_in) = refs[
+        16:26
+    ]
+    (codes2, grad2, part, from_x, everyone, gated, d_both, sums, both_part, down_part) = refs[26:36]
+    (gain_sums, heads, loaded, core_sent, core_got, y_sent, y_got, x_sent, x_got) = refs[36:45]
+    (z_sent, z_got, f_sent, f_got, f_kept, g_sent, g_got) = refs[45:52]
+    team_scratch = refs[52:60]
+    team_sent, team_got = refs[60:62]
+    rows, width = cotangent.shape
+    share = both_part.shape[0] // 16
+    where = Place()
+    own, theirs = pl.ds(0, rows), pl.ds(rows, rows)
+    chunk, small = rows // 2, 32
+
+    def load(source, target, number):
+        return pltpu.make_async_copy(source, target, loaded.at[number])
+
+    def loads_of(layer):
+        return [
+            load(normed.at[layer], v_normed, 0),
+            load(both.at[layer], w_both, 1),
+            load(down.at[layer], w_down, 2),
+            load(middle.at[layer], v_middle, 3),
+            load(outs.at[layer], w_out, 4),
+            load(qkv.at[layer], v_qkv, 5),
+            load(other.at[layer], v_other, 6),
+            load(stream.at[layer], v_stream, 7),
+            load(attended.at[layer], v_attended, 8),
+            load((qkv0, qkv1)[layer], w_qkv, 9),
+        ]
+
+    def remote(source, target, sent, got, peer, place=None):
+        return pltpu.make_async_remote_copy(
+            src_ref=source,
+            dst_ref=target,
+            send_sem=sent,
+            recv_sem=got,
+            device_id=(peer, where.place if place is None else place),
+            device_id_type=MESH,
+        )
+
+    def wait_bytes(like, semaphore):
+        pltpu.make_async_copy(like, like, semaphore).wait()
+
+    def to_core(source, target, number):
+        return remote(source, target, core_sent.at[number], core_got.at[number], where.core_peer)
+
+    def team_rows(ref, team):
+        return ref.at[pl.ds(pl.multiple_of(team * 8 * share, 8 * share), 8 * share)]
+
+    def swap(layer):
+        team = where.index // 8
+        return remote(
+            team_rows(both_part, 1 - team),
+            pair_got.at[layer],
+            f_sent.at[3 * layer],
+            f_got.at[3 * layer],
+            lax.rem(where.index + 8, 16),
+        )
+
+    def share_ffn(layer, spare):
+        index = where.index
+        team, member = index // 8, lax.rem(index, 8)
+        swap(layer).wait_recv()
+        fetch = load(pair_got.at[layer], spare, 12 + layer)
+        fetch.start()
+        fetch.wait()
+        start = pl.multiple_of(team * 8 * share, 8 * share)
+
+        def add(i, carry):
+            first = pl.multiple_of(i * 32, 32)
+            here = pl.ds(pl.multiple_of(start + first, 32), 32)
+            both_part[here, :] = (
+                both_part[here, :].astype(F32) + spare[pl.ds(first, 32), :].astype(F32)
+            ).astype(BF)
+            return carry
+
+        lax.fori_loop(0, 8 * share // 32, add, 0)
+
+        def piece(owner):
+            first = pl.multiple_of(start + owner * share, share)
+            return both_part.at[pl.ds(first, share)]
+
+        def send(step, carry):
+            owner = lax.rem(member + step, 8)
+            remote(
+                piece(owner),
+                both_got.at[layer, member],
+                f_sent.at[3 * layer + 2],
+                f_got.at[3 * layer + 2],
+                team * 8 + owner,
+            ).start()
+            return carry
+
+        lax.fori_loop(1, 8, send, 0)
+        pltpu.make_async_copy(
+            piece(member), both_got.at[layer, member], f_kept.at[2 * layer]
+        ).start()
+
+    def send_ffn(layer):
+        index = where.index
+        swap(layer).start()
+        half = down_part.shape[0] // 2
+        for side in (0, 1):
+            owner = 2 * lax.rem(index, 8) + side
+            piece = down_part.at[pl.ds(side * half, half)]
+            target = down_got.at[layer, index // 8]
+
+            @pl.when(owner != index)
+            def _():
+                remote(
+                    piece, target, f_sent.at[3 * layer + 1], f_got.at[3 * layer + 1], owner
+                ).start()
+
+            @pl.when(owner == index)
+            def _():
+                pltpu.make_async_copy(piece, target, f_kept.at[2 * layer + 1]).start()
+
+    def drain_ffn(layer):
+        index = where.index
+        swap(layer).wait_send()
+        wait_bytes(both_part.at[pl.ds(0, 7 * share)], f_sent.at[3 * layer + 2])
+        wait_bytes(both_part.at[pl.ds(0, share)], f_kept.at[2 * layer])
+        ends = (index == 0) | (index == 15)
+        half = down_part.shape[0] // 2
+        semaphore = f_sent.at[3 * layer + 1]
+
+        @pl.when(ends)
+        def _():
+            wait_bytes(down_part.at[pl.ds(0, half)], semaphore)
+            wait_bytes(down_part.at[pl.ds(0, half)], f_kept.at[2 * layer + 1])
+
+        @pl.when(jnp.logical_not(ends))
+        def _():
+            wait_bytes(down_part, semaphore)
+
+    def landing(layer):
+        return from_x if layer == 1 else everyone.at[pl.ds(0, 16 * share)]
+
+    def send_x(layer, piece):
+        for z in range(4):
+            start = (z * 2 + 1 - where.x) * share
+            remote(
+                part.at[piece, pl.ds(pl.multiple_of(start, share), share)],
+                landing(layer).at[pl.ds((z * 4 + piece) * share, share)],
+                x_sent.at[4 * layer + piece],
+                x_got.at[4 * layer + piece],
+                where.x_peer,
+            ).start()
+
+    def attention_grads(piece):
+        def step(i, carry):
+            here = pl.ds(pl.multiple_of(i * 256, 256), 256)
+            if piece < 3:
+                right = d_qkv2[:, piece * width : (piece + 1) * width]
+                value = left_trans(normed2[:, here], right)
+            else:
+                value = left_trans(attended2[:, here], d_middle2[...])
+            part[piece, here, :] = value.astype(BF)
+            return carry
+
+        lax.fori_loop(0, normed2.shape[1] // 256, step, 0)
+
+    def send_z(source, target, number, size):
+        for z in range(4):
+            piece = source.at[pl.ds(z * size, size)]
+            peer = z * 4 + where.x * 2 + where.core
+
+            @pl.when(where.z != z)
+            def _():
+                remote(piece, target, z_sent.at[number], z_got.at[number], peer).start()
+
+            @pl.when(where.z == z)
+            def _():
+                pltpu.make_async_copy(piece, target, z_got.at[number]).start()
+
+    def finish_x(layer):
+        arrived = landing(layer)
+        for piece in range(4):
+            wait_bytes(arrived.at[pl.ds(0, 4 * share)], x_got.at[4 * layer + piece])
+            for z in range(4):
+                start = pl.multiple_of((z * 2 + where.x) * share, share)
+                here = pl.ds((z * 4 + piece) * share, share)
+                arrived[here, :] = (
+                    arrived[here, :].astype(F32)
+                    + part[piece, pl.ds(start, share), :].astype(F32)
+                ).astype(BF)
+        send_z(arrived, attn_got.at[layer, where.z], layer, 4 * share)
+
+    first_loads = loads_of(1)
+    starting = [load(cotangent, rounded, 10), load(codes, codes2.at[own], 11)]
+    for copy in starting + first_loads:
+        copy.start()
+    where.greet_all()
+    codes_copy = to_core(codes_theirs, codes2.at[theirs], 8)
+    codes_copy.start()
+    starting[0].wait()
+    grad[...] = rounded[...].astype(F32)
+    gain_sums[...] = jnp.zeros_like(gain_sums)
+    fill_heads(heads)
+    waiting = {1: first_loads, 0: loads_of(0)}
+
+    for layer in (1, 0):
+        copies = waiting[layer]
+        team = Team(
+            rows,
+            rounded,
+            everyone,
+            sums,
+            tuple(team_scratch) + (team_sent.at[layer], team_got.at[layer]),
+        )
+
+        def compute(m, start):
+            here = pl.ds(start, 2 * rows)
+            ffn_back_rows(everyone[here, :], v_normed, w_both, w_down, gated, d_both, here)
+            split_pair(
+                team, m, lambda c: right_trans(d_both[here, :], w_both[c, :]), sums, team.part
+            )
+
+        def between():
+            if layer == 0:
+                drain_ffn(1)
+
+            def down_step(i, carry):
+                here = pl.ds(pl.multiple_of(i * 256, 256), 256)
+                down_part[here, :] = left_trans(gated[:, here], everyone[...]).astype(BF)
+                return carry
+
+            def both_step(i, carry):
+                here = pl.ds(pl.multiple_of(i * 256, 256), 256)
+                both_part[here, :] = left_trans(v_normed[:, here], d_both[...]).astype(BF)
+                return carry
+
+            lax.fori_loop(0, down_part.shape[0] // 256, down_step, 0)
+            lax.fori_loop(0, width // 256, both_step, 0)
+            if layer == 1:
+                for copy in waiting[0][:3]:
+                    copy.start()
+
+        def early():
+            for copy in copies[:3]:
+                copy.wait()
+            if layer == 0:
+                share_ffn(1, d_both.at[pl.ds(0, 8 * share)])
+                for piece in range(4):
+                    attention_grads(piece)
+
+        later = None
+        if layer == 0:
+
+            def later(m):
+                for piece in range(4):
+                    pl.when(m == piece)(lambda: send_x(1, piece))
+
+        team.run(compute, between, d_middle, later, early)
+
+        send_ffn(layer)
+        copies[3].wait()
+
+        def norm_step(i, carry):
+            here = pl.ds(pl.multiple_of(i * chunk, 16), chunk)
+            value = v_middle[here, :]
+            back, gain_grad = norm_back(
+                d_middle[here, :], value, inverse_rms(value), gain_rows[2 + layer : 3 + layer, :]
+            )
+            gain_sums[2 + layer : 3 + layer, :] += gain_grad[None]
+            gradient = grad[here, :] + back
+            d_middle[here, :] = gradient
+            d_middle2[here, :] = gradient.astype(BF)
+            return carry
+
+        lax.fori_loop(0, rows // chunk, norm_step, 0)
+        shared = [to_core(d_middle2.at[own], d_middle2.at[theirs], 4 * layer)]
+        shared[0].start()
+        for copy in copies[4:9]:
+            copy.wait()
+
+        for first in range(0, width, 256):
+            columns = slice(first, first + 256)
+            sums[2, :, columns] = right_trans(d_middle2[:rows, :], w_out[columns, :])
+
+        def attention_step(i, carry):
+            here = pl.ds(pl.multiple_of(i * small, small), small)
+            d_attended = sums[2, here, :].astype(BF).astype(F32)
+            q = v_qkv[here, :width].astype(F32)
+            k = v_qkv[here, width : 2 * width].astype(F32)
+            k0 = v_other[here, :width].astype(F32)
+            mine, past = probabilities(q, k, k0, heads, where.place)
+            d_mine = heads_summed(d_attended * v_qkv[here, 2 * width :].astype(F32), heads)
+            d_past = heads_summed(d_attended * v_other[here, width:].astype(F32), heads)
+            inner = mine * d_mine + past * d_past
+            s_past = heads_spread(past * (d_past - inner) / math.sqrt(HD), heads)
+            d_other[here, :width] = (s_past * q).astype(BF)
+            d_other[here, width:] = (heads_spread(past, heads) * d_attended).astype(BF)
+            s_mine = heads_spread(mine * (d_mine - inner) / math.sqrt(HD), heads)
+            d_qkv2[here, :width] = (s_mine * k + s_past * k0).astype(BF)
+            sums[0, here, :] = s_mine * q
+            sums[1, here, :] = heads_spread(mine, heads) * d_attended
+            return carry
+
+        lax.fori_loop(0, rows // small, attention_step, 0)
+        exchange = remote(
+            d_other, y_in.at[layer], y_sent.at[layer], y_got.at[layer], where.index, 1 - where.place
+        )
+        exchange.start()
+
+        def operand_step(i, carry):
+            here = pl.ds(pl.multiple_of(i * chunk, 16), chunk)
+            value = v_stream[here, :]
+            value = value * inverse_rms(value) * gain_rows[layer : layer + 1, :]
+            for number, item, target in (
+                (0, value.astype(BF).astype(F32), normed2),
+                (1, v_attended[here, :].astype(F32), attended2),
+            ):
+                for_core[number, here, :] = own_half(item, where.core, True).astype(BF)
+                target[here, :] = own_half(item, where.core, False).astype(BF)
+            return carry
+
+        lax.fori_loop(0, rows // chunk, operand_step, 0)
+        shared.append(to_core(for_core.at[0], normed2.at[theirs], 4 * layer + 1))
+        shared.append(to_core(for_core.at[1], attended2.at[theirs], 4 * layer + 2))
+        shared[1].start()
+        shared[2].start()
+        if layer == 0:
+            finish_x(1)
+        exchange.wait_recv()
+        d_qkv2[:rows, width : 2 * width] = (
+            sums[0] + y_in[layer, :, :width].astype(F32)
+        ).astype(BF)
+        d_qkv2[:rows, 2 * width :] = (sums[1] + y_in[layer, :, width:].astype(F32)).astype(BF)
+        shared.append(to_core(d_qkv2.at[own], d_qkv2.at[theirs], 4 * layer + 3))
+        shared[3].start()
+        if layer == 0:
+            for piece in range(4):
+                wait_bytes(part.at[piece, pl.ds(0, 4 * share)], x_sent.at[4 + piece])
+            for copy in shared:
+                copy.wait_recv()
+            for piece in range(4):
+                attention_grads(piece)
+                send_x(0, piece)
+        copies[9].wait()
+        for first in range(0, width, 256):
+            columns = slice(first, first + 256)
+            sums[2, :, columns] = right_trans(d_qkv2[:rows, :], w_qkv[columns, :])
+
+        def stream_step(i, carry):
+            here = pl.ds(pl.multiple_of(i * chunk, 16), chunk)
+            value = v_stream[here, :]
+            back, gain_grad = norm_back(
+                sums[2, here, :], value, inverse_rms(value), gain_rows[layer : layer + 1, :]
+            )
+            gain_sums[layer : layer + 1, :] += gain_grad[None]
+            gradient = d_middle[here, :] + back
+            grad[here, :] = gradient
+            rounded_to = rounded if layer == 1 else grad2
+            rounded_to[here, :] = gradient.astype(BF)
+            return carry
+
+        lax.fori_loop(0, rows // chunk, stream_step, 0)
+        for copy in shared:
+            copy.wait_send()
+        exchange.wait_send()
+        if layer == 1:
+            for copy in shared:
+                copy.wait_recv()
+            for copy in waiting[0][3:]:
+                copy.start()
+
+    grad_out = load(grad, input_grad, 14)
+    grad_out.start()
+    grad_copy = to_core(grad2.at[own], grad2.at[theirs], 9)
+    grad_copy.start()
+    index = where.index
+
+    def gain_columns(device):
+        return gain_sums.at[:, pl.ds(pl.multiple_of(device // 2 * 128, 128), 128)]
+
+    def send_gain(step, carry):
+        peer = lax.rem(index + step, 16)
+        remote(gain_columns(peer), gain_got.at[index], g_sent.at[0], g_got.at[0], peer).start()
+        return carry
+
+    lax.fori_loop(1, 16, send_gain, 0)
+    pltpu.make_async_copy(gain_columns(index), gain_got.at[index], g_got.at[0]).start()
+    grad_copy.wait()
+    codes_copy.wait()
+    starting[1].wait()
+    vocab = codes2.shape[1] // 8
+
+    def table_step(i, carry):
+        here = pl.ds(pl.multiple_of(i * 256, 256), 256)
+        d_both[here, :] = left_trans(codes2[:, here], grad2[...]).astype(BF)
+        return carry
+
+    lax.fori_loop(0, 8 * vocab // 256, table_step, 0)
+    table_in = everyone.at[pl.ds(16 * share, 4 * vocab)]
+    for z in range(4):
+        start = pl.multiple_of((z * 2 + 1 - where.x) * vocab, vocab)
+        remote(
+            d_both.at[pl.ds(start, vocab)],
+            table_in.at[pl.ds(z * vocab, vocab)],
+            x_sent.at[8],
+            x_got.at[8],
+            where.x_peer,
+        ).start()
+    share_ffn(0, d_both.at[pl.ds(8 * vocab, 8 * share)])
+    finish_x(0)
+    wait_bytes(table_in, x_got.at[8])
+    for z in range(4):
+        start = pl.multiple_of((z * 2 + where.x) * vocab, vocab)
+        here = pl.ds(z * vocab, vocab)
+        table_in[here, :] = (
+            table_in[here, :].astype(F32) + d_both[pl.ds(start, vocab), :].astype(F32)
+        ).astype(BF)
+    send_z(table_in, table_got.at[where.z], 2, vocab)
+
+    drain_ffn(0)
+    for layer in (0, 1):
+        wait_bytes(both_got.at[layer, pl.ds(0, 7)], f_got.at[3 * layer + 2])
+        arrived, ends = f_got.at[3 * layer + 1], (index == 0) | (index == 15)
+        pl.when(ends)(lambda: wait_bytes(down_got.at[layer, 0], arrived))
+        pl.when(jnp.logical_not(ends))(lambda: wait_bytes(down_got.at[layer], arrived))
+        wait_bytes(attn_got.at[layer], z_got.at[layer])
+        wait_bytes(everyone.at[pl.ds(0, 12 * share)], z_sent.at[layer])
+    for piece in range(4):
+        wait_bytes(part.at[piece, pl.ds(0, 4 * share)], x_sent.at[piece])
+    wait_bytes(table_got, z_got.at[2])
+    wait_bytes(everyone.at[pl.ds(0, 3 * vocab)], z_sent.at[2])
+    wait_bytes(d_both.at[pl.ds(0, 4 * vocab)], x_sent.at[8])
+    grad_out.wait()
+    wait_bytes(gain_got, g_got.at[0])
+    wait_bytes(gain_got.at[pl.ds(0, 15)], g_sent.at[0])
+
+
+def backward(
+    cotangent, codes, codes_theirs, gain_rows, stream, middle, qkv, other, attended, normed, qkv0,
+    qkv1, outs, both, down
+):
+    rows, width = cotangent.shape
+    hidden = down.shape[1]
+    share = width // 16
+    vocab = codes.shape[1] // 8
+    shape = jax.ShapeDtypeStruct
+    hbm = pl.BlockSpec(memory_space=pl.ANY)
+    vmem = pltpu.VMEM
+    dma = pltpu.SemaphoreType.DMA
+    return pl.pallas_call(
+        backward_kernel,
+        out_shape=(
+            shape((rows, width), F32),
+            shape((2, 8, share, 2 * hidden), BF),
+            shape((2, 8 * share, 2 * hidden), BF),
+            shape((2, 2, hidden // 2, width), BF),
+            shape((2, 4, 4 * share, width), BF),
+            shape((4, vocab, width), BF),
+            shape((16, 8, 128), F32),
+        ),
+        in_specs=[hbm] * 3 + in_vmem(1) + [hbm] * 11,
+        out_specs=tuple([hbm] * 7),
+        scratch_shapes=[
+            vmem((rows, width), F32),
+            vmem((rows, width), F32),
+            vmem((rows, 3 * width), BF),
+            vmem((rows, 2 * width), BF),
+            vmem((rows, width), BF),
+            vmem((8 * rows, width), BF),
+            vmem((width, 3 * width), BF),
+            vmem((width, width), BF),
+            vmem((width, 2 * hidden), BF),
+            vmem((hidden, width), BF),
+            vmem((rows, width), F32),
+            vmem((rows, width), F32),
+            vmem((rows, width), BF),
+            vmem((2 * rows, width // 2), BF),
+            vmem((2 * rows, width // 2), BF),
+            vmem((2 * rows, 3 * width), BF),
+            vmem((2 * rows, width), BF),
+            vmem((2, rows, width // 2), BF),
+            vmem((rows, 2 * width), BF),
+            vmem((2, rows, 2 * width), BF),
+            vmem((2 * rows, 8 * vocab), BF),
+            vmem((2 * rows, width), BF),
+            vmem((4, width // 2, width), BF),
+            vmem((16 * share, width), BF),
+            vmem((8 * rows, width), BF),
+            vmem((8 * rows, hidden), BF),
+            vmem((8 * rows, 2 * hidden), BF),
+            vmem((4, rows, width), F32),
+            vmem((width, 2 * hidden), BF),
+            vmem((hidden, width), BF),
+            vmem((8, width), F32),
+            vmem((width, 128), BF),
+            dma((15,)),
+            dma((10,)),
+            dma((10,)),
+            dma((2,)),
+            dma((2,)),
+            dma((9,)),
+            dma((9,)),
+            dma((3,)),
+            dma((3,)),
+            dma((6,)),
+            dma((6,)),
+            dma((4,)),
+            dma((1,)),
+            dma((1,)),
+        ]
+        + Team.scratch(rows, width)[:8]
+        + [dma((2, Team.SCRATCH_COPIES)), dma((2, Team.SCRATCH_COPIES))],
+        compiler_params=pltpu.CompilerParams(
+            collective_id=4, has_side_effects=True, vmem_limit_bytes=63 * 2**20
+        ),
+        name="backward_pass",
+    )(
+        cotangent,
+        codes,
+        codes_theirs,
+        gain_rows,
+        stream,
+        middle,
+        qkv,
+        other,
+        attended,
+        normed,
+        qkv0,
+        qkv1,
+        outs,
+        both,
+        down,
+    )
+
+
+def finish_kernel(both, down, attn, table, table_grad, qkv_grad, out_grad, gate_grad, up_grad, down_grad):
+    hidden = both.shape[3] // 2
+    share, width = both.shape[2], attn.shape[3]
+    for layer in range(LAYERS):
+        for member in range(8):
+            columns = slice(member * hidden, (member + 1) * hidden)
+            gate_grad[layer, 0, :, columns] = both[layer, member, :, :hidden].astype(F32)
+            up_grad[layer, 0, :, columns] = both[layer, member, :, hidden:].astype(F32)
+        down_grad[layer, 0] = down[layer, 0].astype(F32) + down[layer, 1].astype(F32)
+        for piece in range(4):
+            rows = slice(piece * share, (piece + 1) * share)
+            value = sum(attn[layer, z, rows, :].astype(F32) for z in range(4))
+            if piece < 3:
+                qkv_grad[layer, 0, :, piece * width : (piece + 1) * width] = value
+            else:
+                out_grad[layer, 0] = value
+    table_grad[0] = sum(table[z].astype(F32) for z in range(4))
+
+
+def finish(both, down, attn, table):
+    share, width = both.shape[2], attn.shape[3]
+    hidden = both.shape[3] // 2
+    shape = jax.ShapeDtypeStruct
+    return pl.pallas_call(
+        finish_kernel,
+        out_shape=(
+            shape((1,) + table.shape[1:], F32),
+            shape((LAYERS, 1, share, 3 * width), F32),
+            shape((LAYERS, 1, share, width), F32),
+            shape((LAYERS, 1, share, 8 * hidden), F32),
+            shape((LAYERS, 1, share, 8 * hidden), F32),
+            shape((LAYERS, 1, hidden // 2, width), F32),
+        ),
+        in_specs=in_vmem(4),
+        out_specs=tuple(in_vmem(6)),
+        compiler_params=pltpu.CompilerParams(vmem_limit_bytes=48 * 2**20),
+        name="finish",
+    )(both, down, attn, table)
+
+
 class Plan:
     def __init__(self, count):
         self.count = count
@@ -880,18 +1497,6 @@
         parts = lax.all_to_all(parts, "frames", split_axis=0, concat_axis=0, tiled=True)
         rows = parts.shape[1]
         parts = parts.astype(F32).reshape(self.teams, self.team, rows, -1).sum(axis=0)
-        if self.count == 16:
-            half = down_part.shape[0] // 2
-            first = lax.axis_index("frames") < 8
-            one, two = down_part[:half].astype(BF), down_part[half:].astype(BF)
-            straight = [(i, 2 * (i % 8) + i // 8) for i in range(16)]
-            crossed = [(i, 2 * (i % 8) + 1 - i // 8) for i in range(16)]
-            one, two = jnp.where(first, one, two), jnp.where(first, two, one)
-            down = lax.ppermute(one, "frames", straight).astype(F32)
-            down = down + lax.ppermute(two, "frames", crossed).astype(F32)
-            parts = parts.reshape(self.team, rows, 2, -1)
-            both = parts.transpose(1, 2, 0, 3).reshape(rows, 2, -1)
-            return both[:, 0], both[:, 1], down
         down = self.scatter_across(down_part)
         parts = parts.reshape(self.team, rows, 2, self.teams, -1)
         both = parts.transpose(1, 2, 3, 0, 4).reshape(rows, 2, -1)
@@ -981,50 +1586,64 @@
     return kept, stream, gain_rows, qkv_all, out_all, ffn_all
 
 
-def fused_forward(
-    frames_in, onehot, code_table, w_qkv, w_out, w_gate, w_up, w_down, gain_attn, gain_ffn
+def fused_body(
+    onehot, frames_in, code_table, w_qkv, w_out, w_gate, w_up, w_down, gain_attn, gain_ffn, cotangent
 ):
     share = gain_attn.shape[-1]
+    width = frames_in.shape[-1]
     gains = jnp.concatenate([gain_attn[:, 0], gain_ffn[:, 0]], axis=0).astype(F32)
     gains = jnp.pad(gains, ((0, 4), (0, share)))
     odd = lax.rem(lax.axis_index("frames"), 2) == 1
     gains = jnp.where(odd, jnp.roll(gains, share, axis=1), gains)
-    (act, stream, middle, qkv, other, attended, normed, gain_rows, qkv0, qkv1, outs, both, down) = (
-        forward(
-            frames_in[:, 0],
-            onehot,
-            gains,
-            code_table[0],
-            w_qkv[:, 0],
-            w_out[:, 0],
-            w_gate[:, 0],
-            w_up[:, 0],
-            w_down[:, 0],
-        )
+    act, *saved = forward(
+        frames_in[:, 0],
+        onehot,
+        gains,
+        code_table[0],
+        w_qkv[:, 0],
+        w_out[:, 0],
+        w_gate[:, 0],
+        w_up[:, 0],
+        w_down[:, 0],
     )
-    kept = []
-    for layer in range(LAYERS):
-        inv_attn = inverse_rms(stream[layer])
-        normed_attn = (stream[layer] * inv_attn * gain_rows[layer]).astype(BF)
-        unused, own, past = attend(qkv[layer], other[layer])
-        inv_ffn = inverse_rms(middle[layer])
-        kept.append(
-            (
-                stream[layer],
-                inv_attn,
-                normed_attn,
-                qkv[layer],
-                other[layer],
-                own,
-                past,
-                attended[layer],
-                middle[layer],
-                inv_ffn,
-                normed[layer],
-            )
-        )
-    ffn_all = [(both[layer], down[layer]) for layer in range(LAYERS)]
-    return kept, act, gain_rows, [qkv0, qkv1], outs, ffn_all
+    stream, middle, qkv, other, attended, normed, gain_rows, qkv0, qkv1, outs, both, down = saved
+    blocks = onehot.reshape(onehot.shape[0], 8, 2, -1)
+    first, second = (blocks[:, :, i].reshape(onehot.shape[0], -1) for i in (0, 1))
+    codes, codes_theirs = jnp.where(odd, second, first), jnp.where(odd, first, second)
+    input_grad, both_got, pair_got, down_got, attn_got, table_got, gain_got = backward(
+        cotangent[:, 0],
+        codes,
+        codes_theirs,
+        gain_rows,
+        stream,
+        middle,
+        qkv,
+        other,
+        attended,
+        normed,
+        qkv0,
+        qkv1,
+        outs,
+        both,
+        down,
+    )
+    table, qkv_grad, out_grad, gate_grad, up_grad, down_grad = finish(
+        both_got, down_got, attn_got, table_got
+    )
+    sums = gain_got.sum(axis=0)
+    sums = jnp.where(odd, sums[:4, 64:], sums[:4, :64]).reshape(2, LAYERS, 1, share)
+    return (
+        act[:, None, :],
+        input_grad[:, None, :],
+        table,
+        qkv_grad,
+        out_grad,
+        gate_grad,
+        up_grad,
+        down_grad,
+        sums[0],
+        sums[1],
+    )
 
 
 def body(
@@ -1072,14 +1691,14 @@
     onehot = (matches & is_valid[:, None]).astype(BF)
 
     if count == 16:
-        kept, stream, gain_rows, qkv_all, out_all, ffn_all = fused_forward(
-            frames_in, onehot, code_table, w_qkv, w_out, w_gate, w_up, w_down, gain_attn, gain_ffn
+        return fused_body(
+            onehot, frames_in, code_table, w_qkv, w_out, w_gate, w_up, w_down, gain_attn, gain_ffn,
+            cotangent,
         )
-    else:
-        kept, stream, gain_rows, qkv_all, out_all, ffn_all = plain_forward(
-            plan, onward, frames_in, onehot, code_table, w_qkv, w_out, w_gate, w_up, w_down,
-            gain_attn, gain_ffn,
-        )
+    kept, stream, gain_rows, qkv_all, out_all, ffn_all = plain_forward(
+        plan, onward, frames_in, onehot, code_table, w_qkv, w_out, w_gate, w_up, w_down,
+        gain_attn, gain_ffn,
+    )
     output = stream.astype(BF)[:, None, :]
 
     gradient = cotangent[:, 0].astype(F32)

time: 961 us -> 728 us (0.76)
  waiting for transfers between devices: 288 us -> 0.01 us
  Pallas kernels: 475 us -> 693 us
  matrix products: 58.4 us -> 0 us
  local copies, waits for them, and re-layouts: 46.8 us -> 13.2 us
  other arithmetic: 36.5 us -> 6.17 us
  starting transfers between devices: 30.9 us -> 2.34 us
  between operations: 15.2 us -> 1.22 us
    pallas_call x2, Pallas kernels: 98.1 us -> 372 us  [the longest x1 365 us: backward(): pl.pallas_call(backward_kernel, out_shape=(shape((rows, width), F32), sha...]
    ppermute x6 -> x0, waiting for transfers between devices: 153 us -> none  [the longest x2 116 us: ffn_grads(): down = down + lax.ppermute(two, 'frames', crossed).astype(F32)]
    reduce_scatter x5 -> x0, waiting for transfers between devices: 96.4 us -> none  [the longest x2 96.4 us: body(): lax.psum_scatter(qkv_part, 'frames', scatter_dimension=0, tiled=True)]
    dot_general x25 -> x0, matrix products: 58.4 us -> none  [the longest x5 16.9 us: left_trans(): lax.dot_general(left, right, (((0,), (0,)), ((), ())), preferred_element_...]
    pallas_call x1, Pallas kernels: 377 us -> 322 us  [forward(): pl.pallas_call(forward_kernel, out_shape=(shape((rows, width), BF), shape...]
    all_to_all x2 -> x0, waiting for transfers between devices: 38.4 us -> none  [ffn_grads(): lax.all_to_all(parts, 'frames', split_axis=0, concat_axis=0, tiled=True)]
    all_to_all x2 -> x0, starting transfers between devices: 16 us -> none  [ffn_grads(): lax.all_to_all(parts, 'frames', split_axis=0, concat_axis=0, tiled=True)]
    squeeze x5 -> x0, local copies, waits for them, and re-layouts: 13.4 us -> none  [the longest x1 7.14 us: fused_forward(): normed[layer]]
  transfers between devices with their start and end apart: 14 -> 1, of which waited for: 7 -> 0; matrix products, arithmetic and copies ran while one was open for 11% -> 1% of each run, Pallas kernels for 5% -> 0%
where the time goes in v4:
time: 728 us; the launch traced here: 716 us
  Pallas kernels  693 us (95%)
  local copies, waits for them, and re-layouts  13.2 us (2%)
    pallas_call x1, Pallas kernels, backward(): pl.pallas_call(backward_kernel, out_shape=(shape((rows, width), F32), sha...  365 us
    pallas_call x1, Pallas kernels, forward(): pl.pallas_call(forward_kernel, out_shape=(shape((rows, width), BF), shape...  322 us
  transfers between devices with their start and end apart: 1, of which 0 were waited for; matrix products, arithmetic and copies ran while one was open for 1% of the time, Pallas kernels for 0%

profile of v4, /device:TPU:0, one launch (start us, length us, event | category | flops | bytes accessed | tf_op | source)
XLA Modules:
  0.0 716.4 jit_solution(11567889450291617907)
XLA Ops:
  0.6 0.0 copy-start.6
  0.7 0.0 copy-start.7
  0.7 0.0 copy-start.4
  0.7 0.0 copy-start.5
  0.7 0.8 slice.53
  1.4 2.3 collective-permute-start
  3.8 0.8 reduce-window.9
  4.6 0.7 bitcast_subtract_fusion
  5.3 0.1 convert_reduce_fusion
  5.4 1.7 slice_bitcast_fusion.2
  7.1 2.0 slice_bitcast_fusion
  9.1 0.0 copy-done.7
  9.1 0.1 select_reduce_fusion
  9.2 0.0 copy-done.4
  9.3 0.7 pad_select_fusion.gain_shard
  9.9 0.0 collective-permute-done
  10.0 0.1 reshape_select_fusion
  10.0 1.3 fusion.1.onehot
  11.3 1.4 and_convert_fusion
  12.8 0.1 broadcast_select_fusion
  12.8 321.8 %forward_pass.1 = (bf16[224,1024]{1,0:T(8,128)(2,1)}, f32[2,224,1024]{2,1,0:T(8,128)}, f32[2,224,1024]{2,1,0:T(8,128)}, bf16[2,224,3072]{2,1,0:T(8,128)(2,1)}, b...) custom-call(bf16[224,1024]{1,0:T(8,128)(2,1)} %bitcast.47, ...), custom_call_target="tpu_custom_call" | custom-call | tf_op jit(solution)/shard_map/forward_pass/pallas_call | solution.py:796
  334.7 1.1 copy_bitcast_fusion
  335.7 365.1 %backward_pass.1 = (f32[224,1024]{1,0:T(8,128)}, bf16[2,8,64,1024]{3,2,1,0:T(8,128)(2,1)}, bf16[2,512,1024]{2,1,0:T(8,128)(2,1)}, bf16[2,2,256,1024]{3,2,1,0:T(8...) custom-call(bf16[224,1024]{1,0:T(8,128)(2,1)} %bitcast.46, ...), custom_call_target="tpu_custom_call" | custom-call | tf_op jit(solution)/shard_map/backward_pass/pallas_call | solution.py:1327
  700.8 3.1 copy.26
  703.9 0.9 reduce_sum.39
  704.8 0.1 slice_select_fusion
  704.9 0.6 fusion.9
  705.4 0.0 copy-done.2
  705.4 1.6 copy-done
  707.0 1.6 copy-done.1
  708.6 6.6 finish.1
  715.2 0.8 copy.34
  (12 shorter events, 0.1 us)
Async XLA Ops:
  0.6 9.3 %copy-start.6 = (s32[224,1]{0,1:T(1,128)S(1)}, s32[224,1]{0,1:T(1,128)}, u32[]{:S(2)}) copy-start(s32[224,1]{0,1:T(1,128)} %param.15) | copy-start | bytes 2692
  0.7 8.5 %copy-start.7 = (s32[3,1]{0,1:T(1,128)S(1)}, s32[3,1]{0,1:T(1,128)}, u32[]{:S(2)}) copy-start(s32[3,1]{0,1:T(1,128)} %param.16) | copy-start | bytes 40
  0.7 8.6 %copy-start.4 = (bf16[2,1,64]{2,0,1:T(2,128)(2,1)S(1)}, bf16[2,1,64]{2,0,1:T(2,128)(2,1)}, u32[]{:S(2)}) copy-start(bf16[2,1,64]{2,0,1:T(2,128)(2,1)} %param.24) | copy-start | bytes 772
  0.7 8.6 %copy-start.5 = (bf16[2,1,64]{2,0,1:T(2,128)(2,1)S(1)}, bf16[2,1,64]{2,0,1:T(2,128)(2,1)}, u32[]{:S(2)}) copy-start(bf16[2,1,64]{2,0,1:T(2,128)(2,1)} %param.23) | copy-start | bytes 772
  1.4 8.5 %collective-permute-start = (s32[2,1]{0,1:T(1,128)S(1)}, s32[2,1]{0,1:T(1,128)S(1)}, u32[]{:S(2)}, u32[]{:S(2)}) collective-permute-start(s32[2,1]{0,1:T(1,128)S(1)} %slice.53), channel_id=1, source_target_pairs={{0,2},{2,4},{4,6},{6,8},{8,10},{10,12},{12,14},{14,16},{16,18},{18... | collective-permute-start | bytes 32 | tf_op jit(solution)/shard_map/ppermute | solution.py:1674
  700.8 4.7 copy-start.2
  705.4 1.6 copy-start
  707.0 1.6 copy-start.1
  708.6 6.6 copy-start.3

commit v5 on v4

--- a/solution.py
+++ b/solution.py
@@ -1041,9 +1041,9 @@
 
         lax.fori_loop(0, normed2.shape[1] // 256, step, 0)
 
-    def send_z(source, target, number, size):
+    def send_z(source, target, number, size, stride, first=0):
         for z in range(4):
-            piece = source.at[pl.ds(z * size, size)]
+            piece = source.at[pl.ds(z * stride + first, size)]
             peer = z * 4 + where.x * 2 + where.core
 
             @pl.when(where.z != z)
@@ -1054,9 +1054,9 @@
             def _():
                 pltpu.make_async_copy(piece, target, z_got.at[number]).start()
 
-    def finish_x(layer):
+    def finish_x(layer, pieces):
         arrived = landing(layer)
-        for piece in range(4):
+        for piece in pieces:
             wait_bytes(arrived.at[pl.ds(0, 4 * share)], x_got.at[4 * layer + piece])
             for z in range(4):
                 start = pl.multiple_of((z * 2 + where.x) * share, share)
@@ -1065,14 +1065,15 @@
                     arrived[here, :].astype(F32)
                     + part[piece, pl.ds(start, share), :].astype(F32)
                 ).astype(BF)
-        send_z(arrived, attn_got.at[layer, where.z], layer, 4 * share)
+            target = attn_got.at[layer, where.z, pl.ds(piece * share, share)]
+            send_z(arrived, target, layer, share, 4 * share, piece * share)
 
     first_loads = loads_of(1)
     starting = [load(cotangent, rounded, 10), load(codes, codes2.at[own], 11)]
     for copy in starting + first_loads:
         copy.start()
     where.greet_all()
-    codes_copy = to_core(codes_theirs, codes2.at[theirs], 8)
+    codes_copy = to_core(codes_theirs, codes2.at[theirs], 10)
     codes_copy.start()
     starting[0].wait()
     grad[...] = rounded[...].astype(F32)
@@ -1122,18 +1123,13 @@
                 copy.wait()
             if layer == 0:
                 share_ffn(1, d_both.at[pl.ds(0, 8 * share)])
-                for piece in range(4):
+                for piece in (1, 2):
                     attention_grads(piece)
 
-        later = None
+        team.run(compute, between, d_middle, early=early)
         if layer == 0:
-
-            def later(m):
-                for piece in range(4):
-                    pl.when(m == piece)(lambda: send_x(1, piece))
-
-        team.run(compute, between, d_middle, later, early)
-
+            send_x(1, 1)
+            send_x(1, 2)
         send_ffn(layer)
         copies[3].wait()
 
@@ -1150,7 +1146,7 @@
             return carry
 
         lax.fori_loop(0, rows // chunk, norm_step, 0)
-        shared = [to_core(d_middle2.at[own], d_middle2.at[theirs], 4 * layer)]
+        shared = [to_core(d_middle2.at[own], d_middle2.at[theirs], 5 * layer)]
         shared[0].start()
         for copy in copies[4:9]:
             copy.wait()
@@ -1197,25 +1193,36 @@
             return carry
 
         lax.fori_loop(0, rows // chunk, operand_step, 0)
-        shared.append(to_core(for_core.at[0], normed2.at[theirs], 4 * layer + 1))
-        shared.append(to_core(for_core.at[1], attended2.at[theirs], 4 * layer + 2))
-        shared[1].start()
-        shared[2].start()
-        if layer == 0:
-            finish_x(1)
+        shared.append(to_core(for_core.at[0], normed2.at[theirs], 5 * layer + 1))
+        shared.append(to_core(for_core.at[1], attended2.at[theirs], 5 * layer + 2))
+        queries, others = pl.ds(0, width), pl.ds(width, 2 * width)
+        shared.append(
+            to_core(d_qkv2.at[own, queries], d_qkv2.at[theirs, queries], 5 * layer + 3)
+        )
+        for copy in shared[1:]:
+            copy.start()
+        for copy in shared:
+            copy.wait_recv()
+        for piece in (3, 0):
+            if layer == 0:
+                finish_x(1, (piece,))
+                wait_bytes(part.at[piece, pl.ds(0, 4 * share)], x_sent.at[4 + piece])
+            attention_grads(piece)
+            send_x(layer, piece)
         exchange.wait_recv()
         d_qkv2[:rows, width : 2 * width] = (
             sums[0] + y_in[layer, :, :width].astype(F32)
         ).astype(BF)
         d_qkv2[:rows, 2 * width :] = (sums[1] + y_in[layer, :, width:].astype(F32)).astype(BF)
-        shared.append(to_core(d_qkv2.at[own], d_qkv2.at[theirs], 4 * layer + 3))
-        shared[3].start()
+        last = to_core(d_qkv2.at[own, others], d_qkv2.at[theirs, others], 5 * layer + 4)
+        last.start()
+        shared.append(last)
         if layer == 0:
-            for piece in range(4):
+            finish_x(1, (1, 2))
+            for piece in (1, 2):
                 wait_bytes(part.at[piece, pl.ds(0, 4 * share)], x_sent.at[4 + piece])
-            for copy in shared:
-                copy.wait_recv()
-            for piece in range(4):
+            last.wait_recv()
+            for piece in (1, 2):
                 attention_grads(piece)
                 send_x(0, piece)
         copies[9].wait()
@@ -1241,14 +1248,13 @@
             copy.wait_send()
         exchange.wait_send()
         if layer == 1:
-            for copy in shared:
-                copy.wait_recv()
+            last.wait_recv()
             for copy in waiting[0][3:]:
                 copy.start()
 
     grad_out = load(grad, input_grad, 14)
     grad_out.start()
-    grad_copy = to_core(grad2.at[own], grad2.at[theirs], 9)
+    grad_copy = to_core(grad2.at[own], grad2.at[theirs], 11)
     grad_copy.start()
     index = where.index
 
@@ -1284,7 +1290,7 @@
             where.x_peer,
         ).start()
     share_ffn(0, d_both.at[pl.ds(8 * vocab, 8 * share)])
-    finish_x(0)
+    finish_x(0, (3, 0, 1, 2))
     wait_bytes(table_in, x_got.at[8])
     for z in range(4):
         start = pl.multiple_of((z * 2 + where.x) * vocab, vocab)
@@ -1292,7 +1298,7 @@
         table_in[here, :] = (
             table_in[here, :].astype(F32) + d_both[pl.ds(start, vocab), :].astype(F32)
         ).astype(BF)
-    send_z(table_in, table_got.at[where.z], 2, vocab)
+    send_z(table_in, table_got.at[where.z], 2, vocab, vocab)
 
     drain_ffn(0)
     for layer in (0, 1):
@@ -1371,8 +1377,8 @@
             vmem((8, width), F32),
             vmem((width, 128), BF),
             dma((15,)),
-            dma((10,)),
-            dma((10,)),
+            dma((12,)),
+            dma((12,)),
             dma((2,)),
             dma((2,)),
             dma((9,)),

time: 728 us -> 705 us (0.968)
  Pallas kernels: 693 us -> 669 us
    pallas_call x1, Pallas kernels: 365 us -> 341 us  [backward(): pl.pallas_call(backward_kernel, out_shape=(shape((rows, width), F32), sha...]
where the time goes in v5:
time: 705 us; the launch traced here: 692 us
  Pallas kernels  669 us (95%)
  local copies, waits for them, and re-layouts  13.2 us (2%)
    pallas_call x1, Pallas kernels, backward(): pl.pallas_call(backward_kernel, out_shape=(shape((rows, width), F32), sha...  341 us
    pallas_call x1, Pallas kernels, forward(): pl.pallas_call(forward_kernel, out_shape=(shape((rows, width), BF), shape...  322 us
  transfers between devices with their start and end apart: 1, of which 0 were waited for; matrix products, arithmetic and copies ran while one was open for 1% of the time, Pallas kernels for 0%

profile of v5, /device:TPU:0, one launch (start us, length us, event | category | flops | bytes accessed | tf_op | source)
XLA Modules:
  0.0 692.0 jit_solution(4528218119008032738)
XLA Ops:
  0.6 0.0 copy-start.6
  0.7 0.0 copy-start.7
  0.7 0.0 copy-start.4
  0.7 0.0 copy-start.5
  0.7 0.8 slice.53
  1.4 2.3 collective-permute-start
  3.8 0.8 reduce-window.9
  4.6 0.7 bitcast_subtract_fusion
  5.3 0.1 convert_reduce_fusion
  5.4 1.7 slice_bitcast_fusion.2
  7.1 2.0 slice_bitcast_fusion
  9.1 0.0 copy-done.7
  9.1 0.1 select_reduce_fusion
  9.3 0.7 pad_select_fusion.gain_shard
  9.9 0.0 collective-permute-done
  9.9 0.0 copy-done.6
  10.0 0.1 reshape_select_fusion
  10.0 1.3 fusion.1.onehot
  11.3 1.4 and_convert_fusion
  12.8 0.1 broadcast_select_fusion
  12.8 321.8 %forward_pass.1 = (bf16[224,1024]{1,0:T(8,128)(2,1)}, f32[2,224,1024]{2,1,0:T(8,128)}, f32[2,224,1024]{2,1,0:T(8,128)}, bf16[2,224,3072]{2,1,0:T(8,128)(2,1)}, b...) custom-call(bf16[224,1024]{1,0:T(8,128)(2,1)} %bitcast.47, ...), custom_call_target="tpu_custom_call" | custom-call | tf_op jit(solution)/shard_map/forward_pass/pallas_call | solution.py:796
  334.7 1.1 copy_bitcast_fusion
  335.7 340.7 %backward_pass.1 = (f32[224,1024]{1,0:T(8,128)}, bf16[2,8,64,1024]{3,2,1,0:T(8,128)(2,1)}, bf16[2,512,1024]{2,1,0:T(8,128)(2,1)}, bf16[2,2,256,1024]{3,2,1,0:T(8...) custom-call(bf16[224,1024]{1,0:T(8,128)(2,1)} %bitcast.46, ...), custom_call_target="tpu_custom_call" | custom-call | tf_op jit(solution)/shard_map/backward_pass/pallas_call | solution.py:1333
  676.4 3.1 copy.26
  679.5 0.9 reduce_sum.39
  680.4 0.1 slice_select_fusion
  680.5 0.6 fusion.9
  681.1 0.0 copy-done.2
  681.1 1.6 copy-done
  682.7 1.6 copy-done.1
  684.2 6.6 finish.1
  690.8 0.8 copy.34
  (12 shorter events, 0.1 us)
Async XLA Ops:
  0.6 9.3 %copy-start.6 = (s32[224,1]{0,1:T(1,128)S(1)}, s32[224,1]{0,1:T(1,128)}, u32[]{:S(2)}) copy-start(s32[224,1]{0,1:T(1,128)} %param.15) | copy-start | bytes 2692
  0.7 8.5 %copy-start.7 = (s32[3,1]{0,1:T(1,128)S(1)}, s32[3,1]{0,1:T(1,128)}, u32[]{:S(2)}) copy-start(s32[3,1]{0,1:T(1,128)} %param.16) | copy-start | bytes 40
  0.7 8.6 %copy-start.4 = (bf16[2,1,64]{2,0,1:T(2,128)(2,1)S(1)}, bf16[2,1,64]{2,0,1:T(2,128)(2,1)}, u32[]{:S(2)}) copy-start(bf16[2,1,64]{2,0,1:T(2,128)(2,1)} %param.24) | copy-start | bytes 772
  0.7 8.6 %copy-start.5 = (bf16[2,1,64]{2,0,1:T(2,128)(2,1)S(1)}, bf16[2,1,64]{2,0,1:T(2,128)(2,1)}, u32[]{:S(2)}) copy-start(bf16[2,1,64]{2,0,1:T(2,128)(2,1)} %param.23) | copy-start | bytes 772
  1.4 8.5 %collective-permute-start = (s32[2,1]{0,1:T(1,128)S(1)}, s32[2,1]{0,1:T(1,128)S(1)}, u32[]{:S(2)}, u32[]{:S(2)}) collective-permute-start(s32[2,1]{0,1:T(1,128)S(1)} %slice.53), channel_id=1, source_target_pairs={{0,2},{2,4},{4,6},{6,8},{8,10},{10,12},{12,14},{14,16},{16,18},{18... | collective-permute-start | bytes 32 | tf_op jit(solution)/shard_map/ppermute | solution.py:1680
  676.4 4.7 copy-start.2
  681.1 1.6 copy-start
  682.6 1.6 copy-start.1
  684.2 6.6 copy-start.3

commit v6 on v5

--- a/solution.py
+++ b/solution.py
@@ -634,6 +634,10 @@
 def probabilities(q, k, k0, heads, place):
     own = heads_summed(q * k, heads) / math.sqrt(HD)
     past = jnp.where(place > 0, heads_summed(q * k0, heads) / math.sqrt(HD), -1e30)
+    return softmax_pair(own, past)
+
+
+def softmax_pair(own, past):
     largest = jnp.maximum(own, past)
     own, past = jnp.exp(own - largest), jnp.exp(past - largest)
     total = own + past
@@ -647,9 +651,9 @@
     (qkv0_out, qkv1_out, outs_out, both_out, down_out) = refs[8:13]
     (gains, table_all, qkv0_all, qkv1_all, outs_all, both, down_all) = refs[13:20]
     (heads, normed, result, sums, gather_sent, gather_got, slice_sent, slice_got) = refs[20:28]
-    (y_sent, y_got, saved) = refs[28:31]
-    team_scratch = refs[31:39]
-    team_sent, team_got = refs[39:41]
+    (y_sent, y_got, saved, scores, scores_in) = refs[28:33]
+    team_scratch = refs[33:41]
+    team_sent, team_got = refs[41:43]
     rows, width = frames.shape
     where = Place()
 
@@ -705,26 +709,44 @@
             for item in second:
                 item.start()
         save(weights, (qkv0_out, qkv1_out)[layer], layer)
-        exchange = pltpu.make_async_remote_copy(
-            src_ref=qkv.at[layer, :, pl.ds(width, 2 * width)],
-            dst_ref=other.at[layer],
-            send_sem=y_sent.at[layer],
-            recv_sem=y_got.at[layer],
-            device_id=(where.index, 1 - where.place),
-            device_id_type=MESH,
-        )
-        for first in list(range(width, 3 * width, 512)) + list(range(0, width, 512)):
-            if first == 0:
-                exchange.start()
+        def to_other(source, target, number):
+            return pltpu.make_async_remote_copy(
+                src_ref=source,
+                dst_ref=target,
+                send_sem=y_sent.at[3 * layer + number],
+                recv_sem=y_got.at[3 * layer + number],
+                device_id=(where.index, 1 - where.place),
+                device_id_type=MESH,
+            )
+
+        first = pl.multiple_of(2 * width * (1 - where.place), 128)
+        exchange = [
+            to_other(
+                qkv.at[layer, :, pl.ds(first, width)], other.at[layer, :, pl.ds(width, width)], 0
+            ),
+            to_other(scores, scores_in.at[layer], 1),
+            to_other(
+                qkv.at[layer, :, pl.ds(width, width)], other.at[layer, :, pl.ds(0, width)], 2
+            ),
+        ]
+        for first in list(range(0, width, 512)) + list(range(2 * width, 3 * width, 512)):
+            columns = slice(first, first + 512)
+            qkv[layer, :, columns] = plain(normed[...], weights[:, columns]).astype(BF)
+        exchange[0].start()
+        for first in range(width, 2 * width, 512):
             columns = slice(first, first + 512)
             qkv[layer, :, columns] = plain(normed[...], weights[:, columns]).astype(BF)
         if layer == 0:
             slices[1].start()
-        exchange.wait_recv()
-        q = qkv[layer, :, :width].astype(F32)
         k = qkv[layer, :, width : 2 * width].astype(F32)
-        k0 = other[layer, :, :width].astype(F32)
-        own, past = probabilities(q, k, k0, heads, where.place)
+        own = heads_summed(qkv[layer, :, :width].astype(F32) * k, heads) / math.sqrt(HD)
+        exchange[0].wait_recv()
+        scores[...] = heads_summed(other[layer, :, width:].astype(F32) * k, heads)
+        exchange[1].start()
+        exchange[2].start()
+        exchange[1].wait_recv()
+        past = jnp.where(where.place > 0, scores_in[layer] / math.sqrt(HD), -1e30)
+        own, past = softmax_pair(own, past)
         attended[layer] = (
             heads_spread(own, heads) * qkv[layer, :, 2 * width :].astype(F32)
             + heads_spread(past, heads) * other[layer, :, width:].astype(F32)
@@ -779,7 +801,9 @@
             stream[1] = middle[0] + result[...]
         else:
             act[...] = (middle[1] + result[...]).astype(BF)
-        exchange.wait_send()
+        exchange[2].wait_recv()
+        for copy in exchange:
+            copy.wait_send()
     save(outs_all, outs_out, 6)
     for item in [gain_gather, table_gather] + qkv_gathers + out_gathers + slices:
         item.drain()
@@ -828,9 +852,11 @@
             pltpu.SemaphoreType.DMA((6, 16)),
             pltpu.SemaphoreType.DMA((2, 3)),
             pltpu.SemaphoreType.DMA((2, 3)),
-            pltpu.SemaphoreType.DMA((2,)),
-            pltpu.SemaphoreType.DMA((2,)),
+            pltpu.SemaphoreType.DMA((6,)),
+            pltpu.SemaphoreType.DMA((6,)),
             pltpu.SemaphoreType.DMA((7,)),
+            pltpu.VMEM((rows, 128), F32),
+            pltpu.VMEM((2, rows, 128), F32),
         ]
         + Team.scratch(rows, width)[:8]
         + [
@@ -883,9 +909,9 @@
     ]
     (codes2, grad2, part, from_x, everyone, gated, d_both, sums, both_part, down_part) = refs[26:36]
     (gain_sums, heads, loaded, core_sent, core_got, y_sent, y_got, x_sent, x_got) = refs[36:45]
-    (z_sent, z_got, f_sent, f_got, f_kept, g_sent, g_got) = refs[45:52]
-    team_scratch = refs[52:60]
-    team_sent, team_got = refs[60:62]
+    (z_sent, z_got, f_sent, f_got, f_kept, g_sent, g_got, d_scores, s_in) = refs[45:54]
+    team_scratch = refs[54:62]
+    team_sent, team_got = refs[62:64]
     rows, width = cotangent.shape
     share = both_part.shape[0] // 16
     where = Place()
@@ -1165,9 +1191,10 @@
             d_mine = heads_summed(d_attended * v_qkv[here, 2 * width :].astype(F32), heads)
             d_past = heads_summed(d_attended * v_other[here, width:].astype(F32), heads)
             inner = mine * d_mine + past * d_past
-            s_past = heads_spread(past * (d_past - inner) / math.sqrt(HD), heads)
-            d_other[here, :width] = (s_past * q).astype(BF)
-            d_other[here, width:] = (heads_spread(past, heads) * d_attended).astype(BF)
+            s_past = past * (d_past - inner) / math.sqrt(HD)
+            d_scores[here, :] = s_past
+            s_past = heads_spread(s_past, heads)
+            d_other[here, :] = (heads_spread(past, heads) * d_attended).astype(BF)
             s_mine = heads_spread(mine * (d_mine - inner) / math.sqrt(HD), heads)
             d_qkv2[here, :width] = (s_mine * k + s_past * k0).astype(BF)
             sums[0, here, :] = s_mine * q
@@ -1175,10 +1202,19 @@
             return carry
 
         lax.fori_loop(0, rows // small, attention_step, 0)
-        exchange = remote(
-            d_other, y_in.at[layer], y_sent.at[layer], y_got.at[layer], where.index, 1 - where.place
-        )
-        exchange.start()
+        exchange = [
+            remote(
+                source,
+                target.at[layer],
+                y_sent.at[2 * layer + number],
+                y_got.at[2 * layer + number],
+                where.index,
+                1 - where.place,
+            )
+            for number, (source, target) in enumerate(((d_scores, s_in), (d_other, y_in)))
+        ]
+        for copy in exchange:
+            copy.start()
 
         def operand_step(i, carry):
             here = pl.ds(pl.multiple_of(i * chunk, 16), chunk)
@@ -1209,11 +1245,21 @@
                 wait_bytes(part.at[piece, pl.ds(0, 4 * share)], x_sent.at[4 + piece])
             attention_grads(piece)
             send_x(layer, piece)
-        exchange.wait_recv()
-        d_qkv2[:rows, width : 2 * width] = (
-            sums[0] + y_in[layer, :, :width].astype(F32)
-        ).astype(BF)
-        d_qkv2[:rows, 2 * width :] = (sums[1] + y_in[layer, :, width:].astype(F32)).astype(BF)
+        for copy in exchange:
+            copy.wait_recv()
+
+        def arrival_step(i, carry):
+            here = pl.ds(pl.multiple_of(i * chunk, 16), chunk)
+            spread = heads_spread(s_in[layer, here, :], heads)
+            d_qkv2[here, width : 2 * width] = (
+                sums[0, here, :] + spread * v_other[here, width:].astype(F32)
+            ).astype(BF)
+            d_qkv2[here, 2 * width :] = (
+                sums[1, here, :] + y_in[layer, here, :].astype(F32)
+            ).astype(BF)
+            return carry
+
+        lax.fori_loop(0, rows // chunk, arrival_step, 0)
         last = to_core(d_qkv2.at[own, others], d_qkv2.at[theirs, others], 5 * layer + 4)
         last.start()
         shared.append(last)
@@ -1246,7 +1292,8 @@
         lax.fori_loop(0, rows // chunk, stream_step, 0)
         for copy in shared:
             copy.wait_send()
-        exchange.wait_send()
+        for copy in exchange:
+            copy.wait_send()
         if layer == 1:
             last.wait_recv()
             for copy in waiting[0][3:]:
@@ -1362,8 +1409,8 @@
             vmem((2 * rows, 3 * width), BF),
             vmem((2 * rows, width), BF),
             vmem((2, rows, width // 2), BF),
-            vmem((rows, 2 * width), BF),
-            vmem((2, rows, 2 * width), BF),
+            vmem((rows, width), BF),
+            vmem((2, rows, width), BF),
             vmem((2 * rows, 8 * vocab), BF),
             vmem((2 * rows, width), BF),
             vmem((4, width // 2, width), BF),
@@ -1379,8 +1426,8 @@
             dma((15,)),
             dma((12,)),
             dma((12,)),
-            dma((2,)),
-            dma((2,)),
+            dma((4,)),
+            dma((4,)),
             dma((9,)),
             dma((9,)),
             dma((3,)),
@@ -1390,6 +1437,8 @@
             dma((4,)),
             dma((1,)),
             dma((1,)),
+            vmem((rows, 128), F32),
+            vmem((2, rows, 128), F32),
         ]
         + Team.scratch(rows, width)[:8]
         + [dma((2, Team.SCRATCH_COPIES)), dma((2, Team.SCRATCH_COPIES))],

time: 705 us -> 699 us (level)
  no operation moved by 1% of the time
where the time goes in v6:
time: 699 us; the launch traced here: 686 us
  Pallas kernels  663 us (95%)
  local copies, waits for them, and re-layouts  13.2 us (2%)
    pallas_call x1, Pallas kernels, backward(): pl.pallas_call(backward_kernel, out_shape=(shape((rows, width), F32), sha...  340 us
    pallas_call x1, Pallas kernels, forward(): pl.pallas_call(forward_kernel, out_shape=(shape((rows, width), BF), shape...  316 us
  transfers between devices with their start and end apart: 1, of which 0 were waited for; matrix products, arithmetic and copies ran while one was open for 1% of the time, Pallas kernels for 0%

profile of v6, /device:TPU:0, one launch (start us, length us, event | category | flops | bytes accessed | tf_op | source)
XLA Modules:
  0.0 686.2 jit_solution(11383015859443725213)
XLA Ops:
  0.6 0.0 copy-start.6
  0.7 0.0 copy-start.7
  0.7 0.0 copy-start.4
  0.7 0.0 copy-start.5
  0.7 0.8 slice.53
  1.4 2.3 collective-permute-start
  3.8 0.8 reduce-window.9
  4.6 0.7 bitcast_subtract_fusion
  5.3 0.1 convert_reduce_fusion
  5.4 1.7 slice_bitcast_fusion.2
  7.1 2.0 slice_bitcast_fusion
  9.1 0.0 copy-done.7
  9.1 0.1 select_reduce_fusion
  9.2 0.0 copy-done.4
  9.3 0.7 pad_select_fusion.gain_shard
  9.9 0.0 collective-permute-done
  10.0 0.1 reshape_select_fusion
  10.0 1.3 fusion.1.onehot
  11.3 1.4 and_convert_fusion
  12.8 0.1 broadcast_select_fusion
  12.8 316.3 %forward_pass.1 = (bf16[224,1024]{1,0:T(8,128)(2,1)}, f32[2,224,1024]{2,1,0:T(8,128)}, f32[2,224,1024]{2,1,0:T(8,128)}, bf16[2,224,3072]{2,1,0:T(8,128)(2,1)}, b...) custom-call(bf16[224,1024]{1,0:T(8,128)(2,1)} %bitcast.47, ...), custom_call_target="tpu_custom_call" | custom-call | tf_op jit(solution)/shard_map/forward_pass/pallas_call | solution.py:820
  329.2 1.1 copy_bitcast_fusion
  330.2 340.4 %backward_pass.1 = (f32[224,1024]{1,0:T(8,128)}, bf16[2,8,64,1024]{3,2,1,0:T(8,128)(2,1)}, bf16[2,512,1024]{2,1,0:T(8,128)(2,1)}, bf16[2,2,256,1024]{3,2,1,0:T(8...) custom-call(bf16[224,1024]{1,0:T(8,128)(2,1)} %bitcast.46, ...), custom_call_target="tpu_custom_call" | custom-call | tf_op jit(solution)/shard_map/backward_pass/pallas_call | solution.py:1380
  670.6 3.1 copy.26
  673.8 0.9 reduce_sum.39
  674.6 0.1 slice_select_fusion
  674.7 0.6 fusion.9
  675.3 1.6 copy-done
  676.9 1.6 copy-done.1
  678.5 6.6 finish.1
  685.0 0.0 copy-done.3
  685.0 0.8 copy.34
  (12 shorter events, 0.1 us)
Async XLA Ops:
  0.6 9.3 %copy-start.6 = (s32[224,1]{0,1:T(1,128)S(1)}, s32[224,1]{0,1:T(1,128)}, u32[]{:S(2)}) copy-start(s32[224,1]{0,1:T(1,128)} %param.15) | copy-start | bytes 2692
  0.7 8.5 %copy-start.7 = (s32[3,1]{0,1:T(1,128)S(1)}, s32[3,1]{0,1:T(1,128)}, u32[]{:S(2)}) copy-start(s32[3,1]{0,1:T(1,128)} %param.16) | copy-start | bytes 40
  0.7 8.6 %copy-start.4 = (bf16[2,1,64]{2,0,1:T(2,128)(2,1)S(1)}, bf16[2,1,64]{2,0,1:T(2,128)(2,1)}, u32[]{:S(2)}) copy-start(bf16[2,1,64]{2,0,1:T(2,128)(2,1)} %param.24) | copy-start | bytes 772
  0.7 8.6 %copy-start.5 = (bf16[2,1,64]{2,0,1:T(2,128)(2,1)S(1)}, bf16[2,1,64]{2,0,1:T(2,128)(2,1)}, u32[]{:S(2)}) copy-start(bf16[2,1,64]{2,0,1:T(2,128)(2,1)} %param.23) | copy-start | bytes 772
  1.4 8.5 %collective-permute-start = (s32[2,1]{0,1:T(1,128)S(1)}, s32[2,1]{0,1:T(1,128)S(1)}, u32[]{:S(2)}, u32[]{:S(2)}) collective-permute-start(s32[2,1]{0,1:T(1,128)S(1)} %slice.53), channel_id=1, source_target_pairs={{0,2},{2,4},{4,6},{6,8},{8,10},{10,12},{12,14},{14,16},{16,18},{18... | collective-permute-start | bytes 32 | tf_op jit(solution)/shard_map/ppermute | solution.py:1729
  670.6 4.7 copy-start.2
  675.3 1.6 copy-start
  676.9 1.6 copy-start.1
  678.5 6.6 copy-start.3

commit v7 on v6

--- a/solution.py
+++ b/solution.py
@@ -1156,7 +1156,6 @@
         if layer == 0:
             send_x(1, 1)
             send_x(1, 2)
-        send_ffn(layer)
         copies[3].wait()
 
         def norm_step(i, carry):
@@ -1215,6 +1214,7 @@
         ]
         for copy in exchange:
             copy.start()
+        send_ffn(layer)
 
         def operand_step(i, carry):
             here = pl.ds(pl.multiple_of(i * chunk, 16), chunk)

time: 699 us -> 712 us (1.019)
  Pallas kernels: 663 us -> 676 us
    pallas_call x1, Pallas kernels: 340 us -> 353 us  [backward(): pl.pallas_call(backward_kernel, out_shape=(shape((rows, width), F32), sha...]
where the time goes in v7:
time: 712 us; the launch traced here: 699 us
  Pallas kernels  676 us (95%)
  local copies, waits for them, and re-layouts  13.2 us (2%)
    pallas_call x1, Pallas kernels, backward(): pl.pallas_call(backward_kernel, out_shape=(shape((rows, width), F32), sha...  353 us
    pallas_call x1, Pallas kernels, forward(): pl.pallas_call(forward_kernel, out_shape=(shape((rows, width), BF), shape...  316 us
  transfers between devices with their start and end apart: 1, of which 0 were waited for; matrix products, arithmetic and copies ran while one was open for 1% of the time, Pallas kernels for 0%

profile of v7, /device:TPU:0, one launch (start us, length us, event | category | flops | bytes accessed | tf_op | source)
XLA Modules:
  0.0 698.9 jit_solution(8671231741016110726)
XLA Ops:
  0.6 0.0 copy-start.6
  0.7 0.0 copy-start.7
  0.7 0.0 copy-start.4
  0.7 0.0 copy-start.5
  0.7 0.8 slice.53
  1.4 2.3 collective-permute-start
  3.8 0.8 reduce-window.9
  4.6 0.7 bitcast_subtract_fusion
  5.3 0.1 convert_reduce_fusion
  5.4 1.7 slice_bitcast_fusion.2
  7.1 2.0 slice_bitcast_fusion
  9.1 0.0 copy-done.7
  9.1 0.1 select_reduce_fusion
  9.3 0.7 pad_select_fusion.gain_shard
  9.9 0.0 collective-permute-done
  10.0 0.1 reshape_select_fusion
  10.0 1.3 fusion.1.onehot
  11.3 1.4 and_convert_fusion
  12.8 0.1 broadcast_select_fusion
  12.8 316.3 %forward_pass.1 = (bf16[224,1024]{1,0:T(8,128)(2,1)}, f32[2,224,1024]{2,1,0:T(8,128)}, f32[2,224,1024]{2,1,0:T(8,128)}, bf16[2,224,3072]{2,1,0:T(8,128)(2,1)}, b...) custom-call(bf16[224,1024]{1,0:T(8,128)(2,1)} %bitcast.47, ...), custom_call_target="tpu_custom_call" | custom-call | tf_op jit(solution)/shard_map/forward_pass/pallas_call | solution.py:820
  329.2 1.1 copy_bitcast_fusion
  330.2 353.1 %backward_pass.1 = (f32[224,1024]{1,0:T(8,128)}, bf16[2,8,64,1024]{3,2,1,0:T(8,128)(2,1)}, bf16[2,512,1024]{2,1,0:T(8,128)(2,1)}, bf16[2,2,256,1024]{3,2,1,0:T(8...) custom-call(bf16[224,1024]{1,0:T(8,128)(2,1)} %bitcast.46, ...), custom_call_target="tpu_custom_call" | custom-call | tf_op jit(solution)/shard_map/backward_pass/pallas_call | solution.py:1380
  683.3 0.0 copy-start.2
  683.3 3.1 copy.26
  686.5 0.9 reduce_sum.39
  687.3 0.1 slice_select_fusion
  687.4 0.6 fusion.9
  688.0 1.6 copy-done
  689.6 1.6 copy-done.1
  691.2 6.6 finish.1
  697.7 0.0 copy-done.3
  697.7 0.8 copy.34
  (12 shorter events, 0.1 us)
Async XLA Ops:
  0.6 9.3 %copy-start.6 = (s32[224,1]{0,1:T(1,128)S(1)}, s32[224,1]{0,1:T(1,128)}, u32[]{:S(2)}) copy-start(s32[224,1]{0,1:T(1,128)} %param.15) | copy-start | bytes 2692
  0.7 8.5 %copy-start.7 = (s32[3,1]{0,1:T(1,128)S(1)}, s32[3,1]{0,1:T(1,128)}, u32[]{:S(2)}) copy-start(s32[3,1]{0,1:T(1,128)} %param.16) | copy-start | bytes 40
  0.7 8.6 %copy-start.4 = (bf16[2,1,64]{2,0,1:T(2,128)(2,1)S(1)}, bf16[2,1,64]{2,0,1:T(2,128)(2,1)}, u32[]{:S(2)}) copy-start(bf16[2,1,64]{2,0,1:T(2,128)(2,1)} %param.24) | copy-start | bytes 772
  0.7 8.6 %copy-start.5 = (bf16[2,1,64]{2,0,1:T(2,128)(2,1)S(1)}, bf16[2,1,64]{2,0,1:T(2,128)(2,1)}, u32[]{:S(2)}) copy-start(bf16[2,1,64]{2,0,1:T(2,128)(2,1)} %param.23) | copy-start | bytes 772
  1.4 8.5 %collective-permute-start = (s32[2,1]{0,1:T(1,128)S(1)}, s32[2,1]{0,1:T(1,128)S(1)}, u32[]{:S(2)}, u32[]{:S(2)}) collective-permute-start(s32[2,1]{0,1:T(1,128)S(1)} %slice.53), channel_id=1, source_target_pairs={{0,2},{2,4},{4,6},{6,8},{8,10},{10,12},{12,14},{14,16},{16,18},{18... | collective-permute-start | bytes 32 | tf_op jit(solution)/shard_map/ppermute | solution.py:1729
  683.3 4.7 copy-start.2
  688.0 1.6 copy-start
  689.6 1.6 copy-start.1
  691.2 6.6 copy-start.3
